TPU v7x, 32 devices: a whole 2x2x4 slice. The times are simulated.
32 devices in a mesh: pipe: 2 (over x), expert: 16 (over z, y, core).
Axes of the slice: x: 2, y: 2, z: 4, core: 2. Of those that a mesh axis runs over, the one named last changes fastest.
Arguments:
- x_first: bfloat16 [2, 2048, 4096], P('pipe', 'expert'), may hold values from -6 to 6
- grad_first: bfloat16 [2, 2048, 4096], P('pipe', 'expert'), may hold values from -12 to 12
- x_second: bfloat16 [2, 2048, 4096], P('pipe', 'expert'), may hold values from -6 to 6
- grad_last: bfloat16 [2048, 4096], P('expert'), may hold values from -12 to 12
- ids_first: int32 [2, 2048, 8], P('pipe', 'expert'), may hold values from 0 to 127, all different within a row; in each aligned block of 128 rows (0 to 127, 128 to 255, ..., all dimensions but the last counted through in order) at most 12 rows name the same one
- probs_first: float32 [2, 2048, 8], P('pipe', 'expert'), may hold values from 0.05 to 1
- ids_second: int32 [2, 2048, 8], P('pipe', 'expert'), may hold values from 0 to 127, all different within a row; in each aligned block of 128 rows (0 to 127, 128 to 255, ..., all dimensions but the last counted through in order) at most 12 rows name the same one
- probs_second: float32 [2, 2048, 8], P('pipe', 'expert'), may hold values from 0.05 to 1
- w_gate: bfloat16 [2, 16, 4096, 256], P('pipe', 'expert'), may hold values from -0.09375 to 0.09375
- w_up: bfloat16 [2, 16, 4096, 256], P('pipe', 'expert'), may hold values from -0.09375 to 0.09375
- w_down: bfloat16 [2, 16, 256, 4096], P('pipe', 'expert'), may hold values from -0.1875 to 0.1875
Outputs:
- dx_first: bfloat16 [2, 2048, 4096], P('pipe', 'expert')
- dx_second: bfloat16 [2, 2048, 4096], P('pipe', 'expert')
Inputs may be any that keep to these rules, and one draw needn't show every extreme that they name: `ids_first`: each token names 8 different experts; among the rows of one device each expert is named by at most 12 tokens. `ids_second`: each token names 8 different experts; among the rows of one device each expert is named by at most 12 tokens.
All inputs are finite; a program needn't handle non-finite values.
Results may differ from a plain program's by a relative error of at most 0.006.
Values may be sent and summed in bfloat16 or wider, within the bound.
No kernel may reach another device: no remote copies, remote signals or barrier semaphores. Data moves between devices by JAX's collectives and lax.ppermute only.
A program may use at most 128 MiB of HBM per device.

v0:
```python
import jax
import jax.numpy as jnp
from jax import lax
from jax.sharding import PartitionSpec as P

EXPERTS = 128
SPLIT = 4


def shifted(x, axis, by):
    peers = lax.axis_size(axis)
    pairs = [(i, i + by) for i in range(peers) if 0 <= i + by < peers]
    return lax.ppermute(x, axis, pairs)


def unit_back(inputs, row_grads, gate_w, up_w, down_w):
    gate_pre = jnp.einsum("...d,dh->...h", inputs, gate_w, preferred_element_type=jnp.float32)
    up_pre = jnp.einsum("...d,dh->...h", inputs, up_w, preferred_element_type=jnp.float32)
    grad_act = jnp.einsum("...d,hd->...h", row_grads, down_w, preferred_element_type=jnp.float32)
    sigmoid_gate = jax.nn.sigmoid(gate_pre)
    grad_up = (grad_act * gate_pre * sigmoid_gate).astype(jnp.bfloat16)
    grad_gate = (grad_act * up_pre * sigmoid_gate * (1.0 + gate_pre * (1.0 - sigmoid_gate))).astype(
        jnp.bfloat16
    )
    return jnp.einsum(
        "...h,dh->...d", grad_gate, gate_w, preferred_element_type=jnp.float32
    ) + jnp.einsum("...h,dh->...d", grad_up, up_w, preferred_element_type=jnp.float32)


def route_rows(expert_ids, probs, window):
    weights = probs / jnp.sum(probs, axis=-1, keepdims=True)
    flat_ids = expert_ids.reshape(-1)
    picks = (flat_ids[:, None] == jnp.arange(window, dtype=jnp.int32)[None, :]).astype(jnp.int32)
    slot_index = jnp.sum((jnp.cumsum(picks, axis=0) - 1) * picks, axis=1)
    return (weights.reshape(-1), flat_ids, slot_index)


def pack_rows(inputs, grads, flat_weights, target, slot_count, topk):
    slot_table = (jnp.arange(slot_count, dtype=jnp.int32)[:, None] == target[None, :]).astype(
        jnp.float32
    )
    slot_coef = jnp.sum(slot_table * flat_weights[None, :], axis=1)
    tok_table = slot_table.reshape(slot_count, inputs.shape[0], topk).sum(axis=2)
    tok_bf = tok_table.astype(jnp.bfloat16)
    x_slots = jnp.dot(tok_bf, inputs, preferred_element_type=jnp.float32).astype(jnp.bfloat16)
    grad_picked = jnp.dot(tok_bf, grads, preferred_element_type=jnp.float32)
    grad_slots = (slot_coef[:, None] * grad_picked).astype(jnp.bfloat16)
    return (x_slots, grad_slots, tok_bf)


def unpack_rows(tok_bf, contrib):
    high_part = contrib.astype(jnp.bfloat16)
    low_part = (contrib - high_part.astype(jnp.float32)).astype(jnp.bfloat16)
    back_table = tok_bf.T
    return jnp.dot(back_table, high_part, preferred_element_type=jnp.float32) + jnp.dot(
        back_table, low_part, preferred_element_type=jnp.float32
    )


def body(
    x_first,
    grad_first,
    x_second,
    grad_last,
    ids_first,
    probs_first,
    ids_second,
    probs_second,
    w_gate,
    w_up,
    w_down,
):
    gate_w = w_gate[0, 0]
    up_w = w_up[0, 0]
    down_w = w_down[0, 0]
    width = gate_w.shape[0]
    topk = ids_first.shape[2]
    tok_count = x_first.shape[1]
    devices = lax.axis_size("expert")
    window = devices // SPLIT
    capacity = 3 * tok_count * topk // (2 * EXPERTS)

    def layer_grad(inputs, grads, expert_ids, probs):
        flat_weights, flat_ids, slot_index = route_rows(expert_ids, probs, window)
        target = flat_ids * capacity + slot_index
        x_slots, grad_slots, tok_bf = pack_rows(
            inputs, grads, flat_weights, target, window * capacity, topk
        )
        x_slots = jnp.repeat(x_slots.reshape(window, capacity, width), SPLIT, axis=0)
        grad_slots = jnp.repeat(grad_slots.reshape(window, capacity, width), SPLIT, axis=0)
        contrib = unit_back(
            lax.all_to_all(x_slots, "expert", split_axis=0, concat_axis=0, tiled=True),
            lax.all_to_all(grad_slots, "expert", split_axis=0, concat_axis=0, tiled=True),
            gate_w,
            up_w,
            down_w,
        )
        returned = lax.all_to_all(contrib, "expert", split_axis=0, concat_axis=0, tiled=True)
        summed = (
            returned.reshape(window, SPLIT, capacity, width)
            .sum(axis=1)
            .reshape(window * capacity, width)
        )
        return unpack_rows(tok_bf, summed)

    section_index = lax.axis_index("pipe")
    last_section = lax.axis_size("pipe") - 1
    dx_one = layer_grad(x_first[0], grad_first[0], ids_first[0], probs_first[0]).astype(
        jnp.bfloat16
    )
    received = shifted(dx_one, "pipe", -1)
    incoming = jnp.where(section_index == last_section, grad_last, received)
    dx_two = layer_grad(x_second[0], incoming, ids_second[0], probs_second[0]).astype(jnp.bfloat16)
    return (dx_one[None], dx_two[None])


def solution(mesh):
    placed = (
        P("pipe", "expert", None),
        P("pipe", "expert", None),
        P("pipe", "expert", None),
        P("expert", None),
        P("pipe", "expert", None),
        P("pipe", "expert", None),
        P("pipe", "expert", None),
        P("pipe", "expert", None),
        P("pipe", "expert", None, None),
        P("pipe", "expert", None, None),
        P("pipe", "expert", None, None),
    )
    return jax.shard_map(
        body,
        mesh=mesh,
        in_specs=placed,
        out_specs=(P("pipe", "expert", None), P("pipe", "expert", None)),
        check_vma=False,
    )
```

profile of v0, /device:TPU:0, one launch (start us, length us, event | category | flops | bytes accessed | tf_op | source)
XLA Modules:
  0.0 442.8 jit_solution(4517370425447268421)
XLA Ops:
  0.6 0.9 copy.51
  1.8 1.1 reduce-window.14
  2.9 0.2 slice_reduce_fusion.1
  3.1 0.2 reduce-window.15
  3.7 1.5 convolution_convert_fusion.1
  5.3 1.5 broadcast_in_dim.13
  6.8 7.6 %all-to-all-start.1 = ((bf16[16,12,4096]{2,1,0:T(8,128)(2,1)}), bf16[16,12,4096]{2,1,0:T(8,128)(2,1)}, u32[]{:S(2)}, u32[]{:S(2)}) async-start(bf16[16,12,4096]{2,1,0:T(8,128)(2,1)} %bitcast.118), calls=%async_computation.1 | async-start | bytes 4194304 | tf_op jit(solution)/shard_map/all_to_all | solution.py:92
  15.0 1.5 fusion.3
  16.6 39.0 %all-to-all-done.1 = bf16[16,12,4096]{2,1,0:T(8,128)(2,1)} async-done(((bf16[16,12,4096]{2,1,0:T(8,128)(2,1)}), bf16[16,12,4096]{2,1,0:T(8,128)(2,1)}, u32[]{:S(2)}, u32[]{:S(2)}) %all-to-all-start.1) | async-done | bytes 1572896 | tf_op jit(solution)/shard_map/all_to_all | solution.py:92
  55.6 1.6 broadcast_in_dim.12
  57.1 11.3 %all-to-all-start = ((bf16[16,12,4096]{2,1,0:T(8,128)(2,1)}), bf16[16,12,4096]{2,1,0:T(8,128)(2,1)}, u32[]{:S(2)}, u32[]{:S(2)}) async-start(bf16[16,12,4096]{2,1,0:T(8,128)(2,1)} %bitcast.119), calls=%async_computation | async-start | bytes 4194304 | tf_op jit(solution)/shard_map/all_to_all | solution.py:93
  68.4 2.3 fusion.11
  70.7 38.8 %all-to-all-done = bf16[16,12,4096]{2,1,0:T(8,128)(2,1)} async-done(((bf16[16,12,4096]{2,1,0:T(8,128)(2,1)}), bf16[16,12,4096]{2,1,0:T(8,128)(2,1)}, u32[]{:S(2)}, u32[]{:S(2)}) %all-to-all-start) | async-done | bytes 1572896 | tf_op jit(solution)/shard_map/all_to_all | solution.py:93
  109.6 3.1 multiply_convert_fusion.1
  112.7 2.3 fusion.44
  115.0 0.8 fusion.9
  115.9 0.9 convolution_add_fusion.1
  116.7 3.8 copy.58
  120.6 11.4 %all-to-all-start.2 = ((f32[16,12,4096]{2,1,0:T(8,128)}), f32[16,12,4096]{2,1,0:T(8,128)}, u32[]{:S(2)}, u32[]{:S(2)}) async-start(f32[16,12,4096]{2,1,0:T(8,128)} %copy.58), calls=%async_computation.2 | async-start | bytes 8388608 | tf_op jit(solution)/shard_map/all_to_all | solution.py:98
  132.3 1.1 reduce-window.16
  133.4 0.2 slice_reduce_fusion
  133.6 0.2 reduce-window.19
  134.2 1.5 convolution_convert_fusion
  135.8 73.8 %all-to-all-done.2 = f32[16,12,4096]{2,1,0:T(8,128)} async-done(((f32[16,12,4096]{2,1,0:T(8,128)}), f32[16,12,4096]{2,1,0:T(8,128)}, u32[]{:S(2)}, u32[]{:S(2)}) %all-to-all-start.2) | async-done | bytes 3145760 | tf_op jit(solution)/shard_map/all_to_all | solution.py:98
  209.6 1.6 broadcast_in_dim.32
  211.2 19.7 %all-to-all-start.4 = ((bf16[16,12,4096]{2,1,0:T(8,128)(2,1)}), bf16[16,12,4096]{2,1,0:T(8,128)(2,1)}, u32[]{:S(2)}, u32[]{:S(2)}) async-start(bf16[16,12,4096]{2,1,0:T(8,128)(2,1)} %bitcast.117), calls=%async_computation.4 | async-start | bytes 4194304 | tf_op jit(solution)/shard_map/all_to_all | solution.py:92
  230.9 3.5 bitcast_reduce_fusion.1
  234.4 1.3 reshape.152
  235.7 0.5 fusion.56
  236.2 1.4 fusion
  237.6 1.3 collective-permute-start
  239.5 25.8 %collective-permute-done = bf16[128,4096]{1,0:T(8,128)(2,1)} collective-permute-done((bf16[128,4096]{1,0:T(8,128)(2,1)}, bf16[128,4096]{1,0:T(8,128)(2,1)}, u32[]{:S(2)}, u32[]{:S(2)}) %collective-permute-start) | collective-permute-done | bytes 1048608 | tf_op jit(solution)/shard_map/ppermute | solution.py:13
  265.3 1.6 fusion.4
  267.0 5.1 %all-to-all-done.4 = bf16[16,12,4096]{2,1,0:T(8,128)(2,1)} async-done(((bf16[16,12,4096]{2,1,0:T(8,128)(2,1)}), bf16[16,12,4096]{2,1,0:T(8,128)(2,1)}, u32[]{:S(2)}, u32[]{:S(2)}) %all-to-all-start.4) | async-done | bytes 1572896 | tf_op jit(solution)/shard_map/all_to_all | solution.py:92
  272.1 1.5 broadcast_in_dim.15
  273.6 11.3 %all-to-all-start.3 = ((bf16[16,12,4096]{2,1,0:T(8,128)(2,1)}), bf16[16,12,4096]{2,1,0:T(8,128)(2,1)}, u32[]{:S(2)}, u32[]{:S(2)}) async-start(bf16[16,12,4096]{2,1,0:T(8,128)(2,1)} %bitcast.120), calls=%async_computation.3 | async-start | bytes 4194304 | tf_op jit(solution)/shard_map/all_to_all | solution.py:93
  284.9 2.3 fusion.7
  287.2 38.8 %all-to-all-done.3 = bf16[16,12,4096]{2,1,0:T(8,128)(2,1)} async-done(((bf16[16,12,4096]{2,1,0:T(8,128)(2,1)}), bf16[16,12,4096]{2,1,0:T(8,128)(2,1)}, u32[]{:S(2)}, u32[]{:S(2)}) %all-to-all-start.3) | async-done | bytes 1572896 | tf_op jit(solution)/shard_map/all_to_all | solution.py:93
  326.1 3.1 multiply_convert_fusion
  329.2 2.3 fusion.41
  331.5 0.8 fusion.5
  332.4 0.9 convolution_add_fusion
  333.2 1.9 copy.68
  335.1 103.3 %all_to_all.30 = f32[16,12,4096]{2,1,0:T(8,128)S(1)} all-to-all(f32[16,12,4096]{2,1,0:T(8,128)S(1)} %copy.68), channel_id=1, replica_groups=mesh['pipe'=2,'expert'=16] {'expert'}, dimensions={0} | all-to-all | bytes 6291456 | tf_op jit(solution)/shard_map/all_to_all | solution.py:98
  438.4 1.2 bitcast_reduce_fusion
  439.6 1.3 reshape.159
  440.9 0.5 fusion.53
  441.4 1.4 fusion.2
  (51 shorter events, 2.6 us)
Async XLA Ops:
  0.6 67.8 %copy-start = (bf16[1,1,4096,256]{3,2,1,0:T(8,128)(2,1)S(1)}, bf16[1,1,4096,256]{3,2,1,0:T(8,128)(2,1)}, u32[]{:S(2)}) copy-start(bf16[1,1,4096,256]{3,2,1,0:T(8,128)(2,1)} %param.19) | copy-start | bytes 6291460
  6.8 7.6 %copy-start.3 = (f32[1,128,8]{1,2,0:T(8,128)S(1)}, f32[1,128,8]{1,2,0:T(8,128)}, u32[]{:S(2)}) copy-start(f32[1,128,8]{1,2,0:T(8,128)} %param.16) | copy-start | bytes 12292
  6.8 48.7 %all-to-all-start.1 = ((bf16[16,12,4096]{2,1,0:T(8,128)(2,1)}), bf16[16,12,4096]{2,1,0:T(8,128)(2,1)}, u32[]{:S(2)}, u32[]{:S(2)}) async-start(bf16[16,12,4096]{2,1,0:T(8,128)(2,1)} %bitcast.118), calls=%async_computation.1 | async-start | bytes 4194304 | tf_op jit(solution)/shard_map/all_to_all | solution.py:92
  57.1 52.4 %all-to-all-start = ((bf16[16,12,4096]{2,1,0:T(8,128)(2,1)}), bf16[16,12,4096]{2,1,0:T(8,128)(2,1)}, u32[]{:S(2)}, u32[]{:S(2)}) async-start(bf16[16,12,4096]{2,1,0:T(8,128)(2,1)} %bitcast.119), calls=%async_computation | async-start | bytes 4194304 | tf_op jit(solution)/shard_map/all_to_all | solution.py:93
  109.6 3.1 copy-start.1
  120.6 11.4 %copy-start.5 = (s32[1,128,8]{1,2,0:T(8,128)S(1)}, s32[1,128,8]{1,2,0:T(8,128)}, u32[]{:S(2)}) copy-start(s32[1,128,8]{1,2,0:T(8,128)} %param.17) | copy-start | bytes 12292
  120.6 89.1 %all-to-all-start.2 = ((f32[16,12,4096]{2,1,0:T(8,128)}), f32[16,12,4096]{2,1,0:T(8,128)}, u32[]{:S(2)}, u32[]{:S(2)}) async-start(f32[16,12,4096]{2,1,0:T(8,128)} %copy.58), calls=%async_computation.2 | async-start | bytes 8388608 | tf_op jit(solution)/shard_map/all_to_all | solution.py:98
  211.2 60.9 %all-to-all-start.4 = ((bf16[16,12,4096]{2,1,0:T(8,128)(2,1)}), bf16[16,12,4096]{2,1,0:T(8,128)(2,1)}, u32[]{:S(2)}, u32[]{:S(2)}) async-start(bf16[16,12,4096]{2,1,0:T(8,128)(2,1)} %bitcast.117), calls=%async_computation.4 | async-start | bytes 4194304 | tf_op jit(solution)/shard_map/all_to_all | solution.py:92
  236.2 2.7 copy-start.4
  237.6 27.6 %collective-permute-start = (bf16[128,4096]{1,0:T(8,128)(2,1)}, bf16[128,4096]{1,0:T(8,128)(2,1)}, u32[]{:S(2)}, u32[]{:S(2)}) collective-permute-start(bf16[128,4096]{1,0:T(8,128)(2,1)} %fusion), channel_id=1, source_target_pairs={{16,0},{17,1},{18,2},{19,3},{20,4},{21,5},{22,6},{23,7},{24,8},{25... | collective-permute-start | bytes 3145736 | tf_op jit(solution)/shard_map/ppermute | solution.py:13
  273.6 52.4 %all-to-all-start.3 = ((bf16[16,12,4096]{2,1,0:T(8,128)(2,1)}), bf16[16,12,4096]{2,1,0:T(8,128)(2,1)}, u32[]{:S(2)}, u32[]{:S(2)}) async-start(bf16[16,12,4096]{2,1,0:T(8,128)(2,1)} %bitcast.120), calls=%async_computation.3 | async-start | bytes 4194304 | tf_op jit(solution)/shard_map/all_to_all | solution.py:93
  326.1 3.1 copy-start.2
where the time goes:
time: 444 us; the launch traced here: 443 us
  waiting for transfers between devices  221 us (50%)
  blocking collectives  103 us (23%)
  starting transfers between devices  62.5 us (14%)
  matrix products  28.7 us (6%)
  local copies, waits for them, and re-layouts  17.8 us (4%)
  other arithmetic  8.11 us (2%)
    all_to_all x1, blocking collectives, layer_grad(): lax.all_to_all(contrib, 'expert', split_axis=0, concat_axis=0, tiled=True)  103 us
    all_to_all x2, waiting for transfers between devices, layer_grad(): lax.all_to_all(grad_slots, 'expert', split_axis=0, concat_axis=0, tiled=T...  77.7 us
    all_to_all x1, waiting for transfers between devices, layer_grad(): lax.all_to_all(contrib, 'expert', split_axis=0, concat_axis=0, tiled=True)  73.8 us
    all_to_all x2, waiting for transfers between devices, layer_grad(): lax.all_to_all(x_slots, 'expert', split_axis=0, concat_axis=0, tiled=True)  44.1 us
    all_to_all x2, starting transfers between devices, layer_grad(): lax.all_to_all(x_slots, 'expert', split_axis=0, concat_axis=0, tiled=True)  27.3 us
    ppermute x1, waiting for transfers between devices, shifted(): return lax.ppermute(x, axis, pairs)  25.8 us
    all_to_all x2, starting transfers between devices, layer_grad(): lax.all_to_all(grad_slots, 'expert', split_axis=0, concat_axis=0, tiled=T...  22.5 us
    all_to_all x1, starting transfers between devices, layer_grad(): lax.all_to_all(contrib, 'expert', split_axis=0, concat_axis=0, tiled=True)  11.4 us
  transfers between devices with their start and end apart: 6, of which 6 were waited for; matrix products, arithmetic and copies ran while one was open for 4% of the time, Pallas kernels for 0%

commit v1 on v0

v1 whole, which is shorter than its diff:
```python
import functools

import jax
import jax.numpy as jnp
from jax import lax
from jax.experimental import pallas as pl
from jax.experimental.pallas import tpu as pltpu
from jax.sharding import PartitionSpec as P

EXPERTS = 128
SPLIT = 4
F32, BF16 = jnp.float32, jnp.bfloat16
VMEM_BYTES = 48 * 1024 * 1024


def call(body, outs, args, flops=0, bytes_moved=0):
    return pl.pallas_call(
        body,
        out_shape=outs,
        in_specs=[pl.BlockSpec(memory_space=pltpu.VMEM)] * len(args),
        out_specs=jax.tree.map(lambda _: pl.BlockSpec(memory_space=pltpu.VMEM), outs),
        compiler_params=pltpu.CompilerParams(vmem_limit_bytes=VMEM_BYTES),
        cost_estimate=pl.CostEstimate(
            flops=flops, bytes_accessed=bytes_moved, transcendentals=0
        ),
    )(*args)


def tables(ids, window, cap, probs=None):
    me = lax.axis_index("expert") // SPLIT
    tok = ids.shape[0]
    ids_t = jnp.transpose(ids)
    weights = None
    if probs is not None:
        probs_t = jnp.transpose(probs)
        weights = probs_t / jnp.sum(probs_t, axis=0, keepdims=True)
    named, coefs = [], []
    for k in range(window):
        match = ids_t == (me ^ k)
        named.append(jnp.sum(jnp.where(match, 1.0, 0.0), axis=0, keepdims=True))
        if probs is not None:
            coefs.append(jnp.sum(jnp.where(match, weights, 0.0), axis=0, keepdims=True))
    pad = [jnp.zeros((-window % 8, tok), F32)] if window % 8 else []
    stacked = jnp.concatenate(named + pad, axis=0).astype(BF16)
    before = (
        lax.broadcasted_iota(jnp.int32, (tok, tok), 0)
        < lax.broadcasted_iota(jnp.int32, (tok, tok), 1)
    ).astype(F32).astype(BF16)
    place = jnp.dot(stacked, before, preferred_element_type=F32)
    rows = lax.broadcasted_iota(jnp.int32, (2 * cap, tok), 0).astype(F32)
    top, bot, coef = [], [], []
    for k in range(window):
        slot = jnp.where(named[k] > 0.0, place[k : k + 1], -1000.0)
        upper = jnp.where(rows == slot, 1.0, 0.0)
        lower = jnp.where(rows == slot + cap, 1.0, 0.0)
        top.append(upper)
        bot.append(lower)
        if probs is not None:
            coef.append(jnp.sum((upper + lower) * coefs[k], axis=1, keepdims=True))
    top, bot = jnp.concatenate(top, axis=0), jnp.concatenate(bot, axis=0)
    return top, bot, jnp.concatenate(coef, axis=0) if coef else None


def gathered(top, bot, rows):
    half = rows.shape[1] // 2
    return jnp.dot(top.astype(BF16), rows[:, :half], preferred_element_type=F32) + jnp.dot(
        bot.astype(BF16), rows[:, half:], preferred_element_type=F32
    )


def pack_pair(window, cap, ids_ref, probs_ref, x_ref, grad_ref, *out_refs):
    top, bot, coef = tables(ids_ref[0], window, cap, probs_ref[0])
    picked_x = gathered(top, bot, x_ref[0])
    picked_grad = gathered(top, bot, grad_ref[0]) * coef
    for k in range(window):
        part = slice(2 * cap * k, 2 * cap * (k + 1))
        out_refs[k][0] = picked_x[part].astype(BF16)
        out_refs[k][1] = picked_grad[part].astype(BF16)


def pack_x(window, cap, ids_ref, x_ref, *out_refs):
    top, bot, _ = tables(ids_ref[0], window, cap)
    picked_x = gathered(top, bot, x_ref[0])
    for k in range(window):
        out_refs[k][...] = picked_x[2 * cap * k : 2 * cap * (k + 1)].astype(BF16)


def scattered(ids_ref, window, cap, blocks):
    top, bot, _ = tables(ids_ref[0], window, cap)
    rows = jnp.concatenate([b[...].astype(F32) for b in blocks], axis=0).astype(BF16)
    turned = (((0,), (0,)), ((), ()))
    left = lax.dot_general(top.astype(BF16), rows, turned, preferred_element_type=F32)
    right = lax.dot_general(bot.astype(BF16), rows, turned, preferred_element_type=F32)
    return left.astype(BF16), right.astype(BF16)


def relay(window, cap, ids_ref, ids_next_ref, probs_next_ref, grad_last_ref, *refs):
    blocks, dx_ref, out_refs = refs[:window], refs[window], refs[window + 1 :]
    left, right = scattered(ids_ref, window, cap, blocks)
    half = left.shape[1]
    dx_ref[0, :, :half] = left
    dx_ref[0, :, half:] = right
    opening = lax.axis_index("pipe") == 0
    left = jnp.where(opening, grad_last_ref[:, :half], left)
    right = jnp.where(opening, grad_last_ref[:, half:], right)
    top, bot, coef = tables(ids_next_ref[0], window, cap, probs_next_ref[0])
    picked = coef * (
        jnp.dot(top.astype(BF16), left, preferred_element_type=F32)
        + jnp.dot(bot.astype(BF16), right, preferred_element_type=F32)
    )
    for k in range(window):
        out_refs[k][...] = picked[2 * cap * k : 2 * cap * (k + 1)].astype(BF16)


def finish(window, cap, ids_ref, *refs):
    blocks, dx_ref = refs[:window], refs[window]
    left, right = scattered(ids_ref, window, cap, blocks)
    half = left.shape[1]
    dx_ref[0, :, :half] = left
    dx_ref[0, :, half:] = right


NT = (((1,), (1,)), ((), ()))


def joined(blocks):
    return jnp.concatenate([b.astype(F32) for b in blocks], axis=0).astype(BF16)


def factors(rows, cap, gate_ref, up_ref):
    half = rows.shape[1]

    def product(ref):
        lower = jnp.dot(rows, ref[half:, :], preferred_element_type=F32)
        return jnp.dot(rows, ref[:half, :], preferred_element_type=F32) + pltpu.roll(
            lower, rows.shape[0] - cap, 0
        )

    gate, up = product(gate_ref), product(up_ref)
    sig = jax.nn.sigmoid(gate)
    return gate * sig, up * sig * (1.0 + gate * (1.0 - sig))


def input_grads(rows, cap, halves, scales, own_ref, far_ref):
    count, half = rows.shape
    valid = lax.broadcasted_iota(jnp.int32, (count, 1), 0) % (2 * cap) < cap
    lhs = []
    for (gate_ref, up_ref, down_ref), (for_up, for_gate) in zip(halves, scales):
        lower = lax.dot_general(rows, down_ref[:, half:], NT, preferred_element_type=F32)
        back = lax.dot_general(
            rows, down_ref[:, :half], NT, preferred_element_type=F32
        ) + pltpu.roll(lower, count - cap, 0)
        d_up = jnp.where(valid, back * for_up, 0.0)
        d_gate = jnp.where(valid, back * for_gate, 0.0)
        lhs.append(
            (
                (d_gate.astype(BF16), pltpu.roll(d_gate, cap, 0).astype(BF16), gate_ref),
                (d_up.astype(BF16), pltpu.roll(d_up, cap, 0).astype(BF16), up_ref),
            )
        )
    step = 256
    own_rows = own_ref.shape[0]
    for n in range(0, half, step):
        total = None
        for pair in lhs:
            for upper, lower, ref in pair:
                term = lax.dot_general(
                    upper, ref[n : n + step, :], NT, preferred_element_type=F32
                ) + lax.dot_general(
                    lower, ref[half + n : half + n + step, :], NT, preferred_element_type=F32
                )
                total = term if total is None else total + term
        own_ref[:, n : n + step] = total[:own_rows]
        far_ref[:, n : n + step] = total[own_rows:].astype(BF16)


def whole_unit(blocks, cap, *refs):
    ins, weights, (own_ref, far_ref) = refs[:blocks], refs[blocks:-2], refs[-2:]
    x_rows = joined([b[0] for b in ins])
    grad_rows = joined([b[1] for b in ins])
    halves = (weights[:3], weights[3:])
    scales = [factors(x_rows, cap, g, u) for g, u, _ in halves]
    input_grads(grad_rows, cap, halves, scales, own_ref, far_ref)


def unit_x(blocks, cap, *refs):
    ins, weights, out_ref = refs[:blocks], refs[blocks:-1], refs[-1]
    x_rows = joined([b[...] for b in ins])
    for i in range(2):
        out_ref[2 * i], out_ref[2 * i + 1] = factors(x_rows, cap, *weights[2 * i : 2 * i + 2])


def unit_grad(blocks, cap, *refs):
    ins, scale_ref, weights, (own_ref, far_ref) = (
        refs[:blocks],
        refs[blocks],
        refs[blocks + 1 : -2],
        refs[-2:],
    )
    grad_rows = joined([b[...] for b in ins])
    scales = [(scale_ref[2 * i], scale_ref[2 * i + 1]) for i in range(2)]
    input_grads(grad_rows, cap, (weights[:3], weights[3:]), scales, own_ref, far_ref)


def add_far(window, cap, own_ref, far_ref, *out_refs):
    for k in range(window):
        part = slice(2 * cap * k, 2 * cap * (k + 1))
        out_refs[k][...] = (own_ref[part] + far_ref[part].astype(F32)).astype(BF16)


def body(
    x_first,
    grad_first,
    x_second,
    grad_last,
    ids_first,
    probs_first,
    ids_second,
    probs_second,
    w_gate,
    w_up,
    w_down,
):
    tok, width = x_first.shape[1:]
    topk = ids_first.shape[2]
    devices = lax.axis_size("expert")
    sections = lax.axis_size("pipe")
    window = devices // SPLIT
    cap = 3 * tok * topk // (2 * EXPERTS)
    half = width // 2
    shape = jax.ShapeDtypeStruct

    def send(x, bits):
        return lax.ppermute(x, "expert", [(i, i ^ bits) for i in range(devices)])

    def plane(x, k):
        return send(x, SPLIT * k) if k else x

    def across(x):
        return send(x, 2)

    order = list(range(window))[::-1]
    own_w = (w_gate[0, 0], w_up[0, 0], w_down[0, 0])
    msg = shape((2 * cap, half), BF16)
    pair = shape((2, 2 * cap, half), BF16)
    weights = own_w + tuple(send(w, 1) for w in own_w)
    ring = [(s, (s + 1) % sections) for s in range(sections)]
    ids_next, probs_next = (
        lax.ppermute(a, "pipe", ring) for a in (ids_second, probs_second)
    )

    def spread(msgs):
        near = [None] * window
        far = [None] * window
        for k in order:
            near[k] = plane(msgs[k], k)
        for k in order[::-1]:
            far[k] = across(near[k])
        return near + far

    def bring_back(own, far):
        far = across(far)
        sums = call(
            functools.partial(add_far, window, cap),
            [msg] * window,
            (own, far),
        )
        back = [None] * window
        for k in order:
            back[k] = plane(sums[k], k)
        return back

    rows = window * 2 * cap
    partial_shapes = [shape((rows, half), F32), shape((rows, half), BF16)]

    first = call(
        functools.partial(pack_pair, window, cap),
        [pair] * window,
        (ids_first, probs_first, x_first, grad_first),
    )
    first = spread(first)
    second_x = call(
        functools.partial(pack_x, window, cap), [msg] * window, (ids_second, x_second)
    )
    own, far = call(
        functools.partial(whole_unit, 2 * window, cap), partial_shapes, (*first, *weights)
    )
    back = bring_back(own, far)
    second_x = spread(second_x)
    scales = call(
        functools.partial(unit_x, 2 * window, cap),
        shape((4, 2 * rows, w_gate.shape[3]), F32),
        (*second_x, weights[0], weights[1], weights[3], weights[4]),
    )
    dx_first, *grads = call(
        functools.partial(relay, window, cap),
        [shape((1, tok, width), BF16)] + [msg] * window,
        (ids_first, ids_next, probs_next, grad_last, *back),
    )
    near = [None] * window
    for k in order:
        pairs = [
            (s * devices + i, (s - 1) % sections * devices + (i ^ (SPLIT * k)))
            for s in range(sections)
            for i in range(devices)
        ]
        near[k] = lax.ppermute(grads[k], ("pipe", "expert"), pairs)
    grads = near + [across(near[k]) for k in range(window)]
    own, far = call(
        functools.partial(unit_grad, 2 * window, cap), partial_shapes, (*grads, scales, *weights)
    )
    back = bring_back(own, far)
    dx_second = call(
        functools.partial(finish, window, cap),
        shape((1, tok, width), BF16),
        (ids_second, *back),
    )
    return dx_first, dx_second


def solution(mesh):
    split = P("pipe", "expert", None)
    stacked = P("pipe", "expert", None, None)
    return jax.shard_map(
        body,
        mesh=mesh,
        in_specs=(
            split,
            split,
            split,
            P("expert", None),
            split,
            split,
            split,
            split,
            stacked,
            stacked,
            stacked,
        ),
        out_specs=(split, split),
        check_vma=False,
    )
```

time: 444 us -> 134 us (0.30)
  waiting for transfers between devices: 221 us -> 43.5 us
  blocking collectives: 103 us -> 0 us
  Pallas kernels: 0 us -> 29.5 us
  matrix products: 28.7 us -> 0 us
  starting transfers between devices: 62.5 us -> 50.9 us
  local copies, waits for them, and re-layouts: 17.8 us -> 9.06 us
  other arithmetic: 8.11 us -> 0 us
    all_to_all x5 -> x0, waiting for transfers between devices: 196 us -> none  [the longest x2 77.7 us: layer_grad(): lax.all_to_all(grad_slots, 'expert', split_axis=0, concat_axis=0, tiled=T...]
    all_to_all x1 -> x0, blocking collectives: 103 us -> none  [layer_grad(): lax.all_to_all(contrib, 'expert', split_axis=0, concat_axis=0, tiled=True)]
    all_to_all x5 -> x0, starting transfers between devices: 61.2 us -> none  [the longest x2 27.3 us: layer_grad(): lax.all_to_all(x_slots, 'expert', split_axis=0, concat_axis=0, tiled=True)]
    ppermute x1 -> x35, starting transfers between devices: 1.28 us -> 50.9 us  [the longest x29 42.1 us: send(): return lax.ppermute(x, 'expert', [(i, i ^ bits) for i in range(devices)])]
    pallas_call x0 -> x9, Pallas kernels: none -> 29.5 us  [call(): pl.pallas_call(body, out_shape=outs, in_specs=[pl.BlockSpec(memory_space=...]
    dot_general x18 -> x0, matrix products: 28.7 us -> none  [the longest x2 6.23 us: unit_back(): jnp.einsum('...d,hd->...h', row_grads, down_w, preferred_element_type=jnp...]
    ppermute x1 -> x35, waiting for transfers between devices: 25.8 us -> 43.5 us  [the longest x29 38 us: send(): return lax.ppermute(x, 'expert', [(i, i ^ bits) for i in range(devices)])]
    unnamed x16 -> x24, local copies, waits for them, and re-layouts: 1.27 us -> 9.06 us
  transfers between devices with their start and end apart: 6 -> 35, of which waited for: 6 -> 15; matrix products, arithmetic and copies ran while one was open for 4% -> 1% of each run, Pallas kernels for 0% -> 6%
where the time goes in v1:
time: 134 us
  starting transfers between devices  50.9 us (38%)
  waiting for transfers between devices  43.5 us (32%)
  Pallas kernels  29.5 us (22%)
  local copies, waits for them, and re-layouts  9.06 us (7%)
    ppermute x29, starting transfers between devices, send(): return lax.ppermute(x, 'expert', [(i, i ^ bits) for i in range(devices)])  42.1 us
    ppermute x29, waiting for transfers between devices, send(): return lax.ppermute(x, 'expert', [(i, i ^ bits) for i in range(devices)])  38 us
    pallas_call x9, Pallas kernels, call(): pl.pallas_call(body, out_shape=outs, in_specs=[pl.BlockSpec(memory_space=...  29.5 us
    unnamed x24, local copies, waits for them, and re-layouts  9.06 us
    ppermute x4, starting transfers between devices, body(): near[k] = lax.ppermute(grads[k], ('pipe', 'expert'), pairs)  6.75 us
    ppermute x2, waiting for transfers between devices, body(): lax.ppermute(a, 'pipe', ring)  3.44 us
  transfers between devices with their start and end apart: 35, of which 15 were waited for; matrix products, arithmetic and copies ran while one was open for 1% of the time, Pallas kernels for 6%

profile of v1, /device:TPU:0, one launch (start us, length us, event | category | flops | bytes accessed | tf_op | source)
XLA Modules:
  0.0 133.6 jit_solution(16168686558545588903)
XLA Ops:
  3.2 1.2 copy-done.2
  4.5 1.2 copy-done.3
  6.5 2.7 %collective-permute-start.2 = (bf16[2,24,2048]{2,1,0:T(8,128)(2,1)S(1)}, bf16[2,24,2048]{2,1,0:T(8,128)(2,1)S(1)}, u32[]{:S(2)}, u32[]{:S(2)}) collective-permute-start(bf16[2,24,2048]{2,1,0:T(8,128)(2,1)S(1)} %get-tuple-element.28), channel_id=1, source_target_pairs={{0,4},{1,5},{2,6},{3,7},{4,0},{5,1},{6,2},{7,3},{8,12},{9,13},{10,... | collective-permute-start | bytes 589832 | tf_op jit(solution)/shard_map/ppermute | solution.py:234
  9.2 2.6 %collective-permute-start.3 = (bf16[2,24,2048]{2,1,0:T(8,128)(2,1)S(1)}, bf16[2,24,2048]{2,1,0:T(8,128)(2,1)S(1)}, u32[]{:S(2)}, u32[]{:S(2)}) collective-permute-start(bf16[2,24,2048]{2,1,0:T(8,128)(2,1)S(1)} %get-tuple-element.29), channel_id=1, source_target_pairs={{0,8},{1,9},{2,10},{3,11},{4,12},{5,13},{6,14},{7,15},{8,0},{9,1},... | collective-permute-start | bytes 589832 | tf_op jit(solution)/shard_map/ppermute | solution.py:234
  11.8 7.0 %collective-permute-done.2.refs_1_ = bf16[2,24,2048]{2,1,0:T(8,128)(2,1)S(1)} collective-permute-done((bf16[2,24,2048]{2,1,0:T(8,128)(2,1)S(1)}, bf16[2,24,2048]{2,1,0:T(8,128)(2,1)S(1)}, u32[]{:S(2)}, u32[]{:S(2)}) %collective-permute-start.2) | collective-permute-done | bytes 196640 | tf_op jit(solution)/shard_map/ppermute | solution.py:234
  18.8 2.7 %collective-permute-start.4 = (bf16[2,24,2048]{2,1,0:T(8,128)(2,1)S(1)}, bf16[2,24,2048]{2,1,0:T(8,128)(2,1)S(1)}, u32[]{:S(2)}, u32[]{:S(2)}) collective-permute-start(bf16[2,24,2048]{2,1,0:T(8,128)(2,1)S(1)} %get-tuple-element.30), channel_id=1, source_target_pairs={{0,12},{1,13},{2,14},{3,15},{4,8},{5,9},{6,10},{7,11},{8,4},{9,5},... | collective-permute-start | bytes 589832 | tf_op jit(solution)/shard_map/ppermute | solution.py:234
  21.4 1.5 %collective-permute-start.5 = (bf16[2,24,2048]{2,1,0:T(8,128)(2,1)S(1)}, bf16[2,24,2048]{2,1,0:T(8,128)(2,1)S(1)}, u32[]{:S(2)}, u32[]{:S(2)}) collective-permute-start(bf16[2,24,2048]{2,1,0:T(8,128)(2,1)S(1)} %get-tuple-element.27.refs_0_), channel_id=1, source_target_pairs={{0,2},{1,3},{2,0},{3,1},{4,6},{5,7},{6,4},{7,5},{8,10},{9,11},{10,... | collective-permute-start | bytes 589832 | tf_op jit(solution)/shard_map/ppermute | solution.py:234
  22.9 4.4 %collective-permute-done.4.refs_3_ = bf16[2,24,2048]{2,1,0:T(8,128)(2,1)S(1)} collective-permute-done((bf16[2,24,2048]{2,1,0:T(8,128)(2,1)S(1)}, bf16[2,24,2048]{2,1,0:T(8,128)(2,1)S(1)}, u32[]{:S(2)}, u32[]{:S(2)}) %collective-permute-start.4) | collective-permute-done | bytes 196640 | tf_op jit(solution)/shard_map/ppermute | solution.py:234
  27.3 1.5 %collective-permute-start.6 = (bf16[2,24,2048]{2,1,0:T(8,128)(2,1)S(1)}, bf16[2,24,2048]{2,1,0:T(8,128)(2,1)S(1)}, u32[]{:S(2)}, u32[]{:S(2)}) collective-permute-start(bf16[2,24,2048]{2,1,0:T(8,128)(2,1)S(1)} %collective-permute-done.2.refs_1_), channel_id=1, source_target_pairs={{0,2},{1,3},{2,0},{3,1},{4,6},{5,7},{6,4},{7,5},{8,10},{9,11},{10,... | collective-permute-start | bytes 589832 | tf_op jit(solution)/shard_map/ppermute | solution.py:234
  29.4 5.8 %collective-permute-done.6.refs_5_ = bf16[2,24,2048]{2,1,0:T(8,128)(2,1)S(1)} collective-permute-done((bf16[2,24,2048]{2,1,0:T(8,128)(2,1)S(1)}, bf16[2,24,2048]{2,1,0:T(8,128)(2,1)S(1)}, u32[]{:S(2)}, u32[]{:S(2)}) %collective-permute-start.6) | collective-permute-done | bytes 196640 | tf_op jit(solution)/shard_map/ppermute | solution.py:234
  35.2 1.5 %collective-permute-start.8 = (bf16[2,24,2048]{2,1,0:T(8,128)(2,1)S(1)}, bf16[2,24,2048]{2,1,0:T(8,128)(2,1)S(1)}, u32[]{:S(2)}, u32[]{:S(2)}) collective-permute-start(bf16[2,24,2048]{2,1,0:T(8,128)(2,1)S(1)} %collective-permute-done.4.refs_3_), channel_id=1, source_target_pairs={{0,2},{1,3},{2,0},{3,1},{4,6},{5,7},{6,4},{7,5},{8,10},{9,11},{10,... | collective-permute-start | bytes 589832 | tf_op jit(solution)/shard_map/ppermute | solution.py:234
  36.7 2.7 %collective-permute-done.7.refs_6_ = bf16[2,24,2048]{2,1,0:T(8,128)(2,1)S(1)} collective-permute-done((bf16[2,24,2048]{2,1,0:T(8,128)(2,1)S(1)}, bf16[2,24,2048]{2,1,0:T(8,128)(2,1)S(1)}, u32[]{:S(2)}, u32[]{:S(2)}) %collective-permute-start.7) | collective-permute-done | bytes 196640 | tf_op jit(solution)/shard_map/ppermute | solution.py:234
  39.4 2.1 %collective-permute-done.8.refs_7_ = bf16[2,24,2048]{2,1,0:T(8,128)(2,1)S(1)} collective-permute-done((bf16[2,24,2048]{2,1,0:T(8,128)(2,1)S(1)}, bf16[2,24,2048]{2,1,0:T(8,128)(2,1)S(1)}, u32[]{:S(2)}, u32[]{:S(2)}) %collective-permute-start.8) | collective-permute-done | bytes 196640 | tf_op jit(solution)/shard_map/ppermute | solution.py:234
  41.5 10.7 %shard_map.123 = (f32[96,2048]{1,0:T(8,128)S(1)}, bf16[96,2048]{1,0:T(8,128)(2,1)}) custom-call(bf16[2,24,2048]{2,1,0:T(8,128)(2,1)S(1)} %get-tuple-element.27.refs_0_, bf16[2,24,2048]{2,1,0:T(8,128)(2,1)S(1)} %collective-permute-done.2.refs_1_, bf16[2,24,2048]{2,1,0:T(8,128)(2,1)S(1)} %collective-permute-done.3.refs_2_, ...), custom_call_target="tpu_custom_call" | custom-call | tf_op jit(solution)/shard_map/pallas_call | solution.py:17
  53.2 1.3 collective-permute-start.12
  54.6 1.2 shard_map.126
  55.8 4.2 %collective-permute-start.24 = (bf16[24,2048]{1,0:T(8,128)(2,1)}, bf16[24,2048]{1,0:T(8,128)(2,1)S(1)}, u32[]{:S(2)}, u32[]{:S(2)}) collective-permute-start(bf16[24,2048]{1,0:T(8,128)(2,1)} %get-tuple-element.43), channel_id=1, source_target_pairs={{0,4},{1,5},{2,6},{3,7},{4,0},{5,1},{6,2},{7,3},{8,12},{9,13},{10,... | collective-permute-start | bytes 294920 | tf_op jit(solution)/shard_map/ppermute | solution.py:234
  60.4 2.2 %collective-permute-done.12.far_ref = bf16[96,2048]{1,0:T(8,128)(2,1)} collective-permute-done((bf16[96,2048]{1,0:T(8,128)(2,1)}, bf16[96,2048]{1,0:T(8,128)(2,1)}, u32[]{:S(2)}, u32[]{:S(2)}) %collective-permute-start.12) | collective-permute-done | bytes 393248 | tf_op jit(solution)/shard_map/ppermute | solution.py:234
  62.6 1.1 copy-done.7
  63.7 1.1 shard_map.124
  64.7 5.3 %collective-permute-start.13 = (bf16[24,2048]{1,0:T(8,128)(2,1)S(1)}, bf16[24,2048]{1,0:T(8,128)(2,1)S(1)}, u32[]{:S(2)}, u32[]{:S(2)}) collective-permute-start(bf16[24,2048]{1,0:T(8,128)(2,1)S(1)} %get-tuple-element.34), channel_id=1, source_target_pairs={{0,4},{1,5},{2,6},{3,7},{4,0},{5,1},{6,2},{7,3},{8,12},{9,13},{10,... | collective-permute-start | bytes 294920 | tf_op jit(solution)/shard_map/ppermute | solution.py:234
  70.2 1.3 collective-permute-start.1
  72.2 2.2 %collective-permute-done.1.probs_next_ref = f32[1,128,8]{2,1,0:T(8,128)S(1)} collective-permute-done((f32[1,128,8]{2,1,0:T(8,128)S(1)}, f32[1,128,8]{2,1,0:T(8,128)S(1)}, u32[]{:S(2)}, u32[]{:S(2)}) %collective-permute-start.1) | collective-permute-done | bytes 4128 | tf_op jit(solution)/shard_map/ppermute | solution.py:249
  74.5 1.2 collective-permute-done.ids_next_ref
  75.7 1.2 collective-permute-start.15
  76.9 2.6 %collective-permute-start.26 = (bf16[24,2048]{1,0:T(8,128)(2,1)S(1)}, bf16[24,2048]{1,0:T(8,128)(2,1)S(1)}, u32[]{:S(2)}, u32[]{:S(2)}) collective-permute-start(bf16[24,2048]{1,0:T(8,128)(2,1)S(1)} %get-tuple-element.45), channel_id=1, source_target_pairs={{0,12},{1,13},{2,14},{3,15},{4,8},{5,9},{6,10},{7,11},{8,4},{9,5},... | collective-permute-start | bytes 294920 | tf_op jit(solution)/shard_map/ppermute | solution.py:234
  79.5 1.5 %collective-permute-start.27 = (bf16[24,2048]{1,0:T(8,128)(2,1)S(1)}, bf16[24,2048]{1,0:T(8,128)(2,1)S(1)}, u32[]{:S(2)}, u32[]{:S(2)}) collective-permute-start(bf16[24,2048]{1,0:T(8,128)(2,1)S(1)} %get-tuple-element.42.refs_0_), channel_id=1, source_target_pairs={{0,2},{1,3},{2,0},{3,1},{4,6},{5,7},{6,4},{7,5},{8,10},{9,11},{10,... | collective-permute-start | bytes 294920 | tf_op jit(solution)/shard_map/ppermute | solution.py:234
  81.5 2.8 %collective-permute-done.14.refs_2_ = bf16[24,2048]{1,0:T(8,128)(2,1)S(1)} collective-permute-done((bf16[24,2048]{1,0:T(8,128)(2,1)S(1)}, bf16[24,2048]{1,0:T(8,128)(2,1)S(1)}, u32[]{:S(2)}, u32[]{:S(2)}) %collective-permute-start.14) | collective-permute-done | bytes 98336 | tf_op jit(solution)/shard_map/ppermute | solution.py:234
  84.3 1.5 %collective-permute-start.29 = (bf16[24,2048]{1,0:T(8,128)(2,1)S(1)}, bf16[24,2048]{1,0:T(8,128)(2,1)S(1)}, u32[]{:S(2)}, u32[]{:S(2)}) collective-permute-start(bf16[24,2048]{1,0:T(8,128)(2,1)S(1)} %collective-permute-done.25.refs_2_), channel_id=1, source_target_pairs={{0,2},{1,3},{2,0},{3,1},{4,6},{5,7},{6,4},{7,5},{8,10},{9,11},{10,... | collective-permute-start | bytes 294920 | tf_op jit(solution)/shard_map/ppermute | solution.py:234
  85.8 1.2 copy-done.5
  87.1 1.6 %shard_map.125 = (bf16[1,128,4096]{2,1,0:T(8,128)(2,1)}, bf16[24,2048]{1,0:T(8,128)(2,1)S(1)}, bf16[24,2048]{1,0:T(8,128)(2,1)S(1)}, bf16[24,2048]{1,0:T(8,128)(2,1)S(1)}, bf16[24,2048]{1,0:T(8,128)(2,1)S(1)}) custom-call(s32[1,128,8]{2,1,0:T(8,128)S(1)} %copy.17.ids_ref, s32[1,128,8]{2,1,0:T(8,128)S(1)} %collective-permute-done.ids_next_ref, ...), custom_call_target="tpu_custom_call" | custom-call | tf_op jit(solution)/shard_map/pallas_call | solution.py:17
  88.7 1.0 collective-permute-start.16
  89.7 1.3 %collective-permute-start.17 = (bf16[24,2048]{1,0:T(8,128)(2,1)S(1)}, bf16[24,2048]{1,0:T(8,128)(2,1)S(1)}, u32[]{:S(2)}, u32[]{:S(2)}) collective-permute-start(bf16[24,2048]{1,0:T(8,128)(2,1)S(1)} %get-tuple-element.39), channel_id=1, source_target_pairs={{0,20},{1,21},{2,22},{3,23},{4,16},{5,17},{6,18},{7,19},{8,28},{9,... | collective-permute-start | bytes 294920 | tf_op jit(solution)/shard_map/ppermute | solution.py:307
  91.0 1.9 %collective-permute-start.18 = (bf16[24,2048]{1,0:T(8,128)(2,1)S(1)}, bf16[24,2048]{1,0:T(8,128)(2,1)S(1)}, u32[]{:S(2)}, u32[]{:S(2)}) collective-permute-start(bf16[24,2048]{1,0:T(8,128)(2,1)S(1)} %get-tuple-element.40), channel_id=1, source_target_pairs={{0,24},{1,25},{2,26},{3,27},{4,28},{5,29},{6,30},{7,31},{8,16},{9,... | collective-permute-start | bytes 294920 | tf_op jit(solution)/shard_map/ppermute | solution.py:307
  93.0 2.5 %collective-permute-start.19 = (bf16[24,2048]{1,0:T(8,128)(2,1)S(1)}, bf16[24,2048]{1,0:T(8,128)(2,1)S(1)}, u32[]{:S(2)}, u32[]{:S(2)}) collective-permute-start(bf16[24,2048]{1,0:T(8,128)(2,1)S(1)} %get-tuple-element.41), channel_id=1, source_target_pairs={{0,28},{1,29},{2,30},{3,31},{4,24},{5,25},{6,26},{7,27},{8,20},{9,... | collective-permute-start | bytes 294920 | tf_op jit(solution)/shard_map/ppermute | solution.py:307
  96.0 1.2 collective-permute-done.16.refs_0_
  97.5 1.7 %collective-permute-start.21 = (bf16[24,2048]{1,0:T(8,128)(2,1)S(1)}, bf16[24,2048]{1,0:T(8,128)(2,1)S(1)}, u32[]{:S(2)}, u32[]{:S(2)}) collective-permute-start(bf16[24,2048]{1,0:T(8,128)(2,1)S(1)} %collective-permute-done.17.refs_1_), channel_id=1, source_target_pairs={{0,2},{1,3},{2,0},{3,1},{4,6},{5,7},{6,4},{7,5},{8,10},{9,11},{10,... | collective-permute-start | bytes 294920 | tf_op jit(solution)/shard_map/ppermute | solution.py:234
  101.2 1.6 %copy-done.1 = bf16[1,1,4096,256]{3,2,1,0:T(8,128)(2,1)S(1)} copy-done((bf16[1,1,4096,256]{3,2,1,0:T(8,128)(2,1)S(1)}, bf16[1,1,4096,256]{3,2,1,0:T(8,128)(2,1)}, u32[]{:S(2)}) %copy-start.1) | copy-done | bytes 2097176
  102.8 4.0 %shard_map.127.refs_8_ = f32[4,192,256]{2,1,0:T(8,128)S(1)} custom-call(bf16[24,2048]{1,0:T(8,128)(2,1)S(1)} %get-tuple-element.42.refs_0_, bf16[24,2048]{1,0:T(8,128)(2,1)S(1)} %collective-permute-done.24.refs_1_, bf16[24,2048]{1,0:T(8,128)(2,1)S(1)} %collective-permute-done.25.refs_2_, bf16[24,2048]{1,0:T(8,128)(2,1)S(1)} %collective-permute-done.26.refs_3_, ...), custom_call_target="tpu_custom_call" | custom-call | tf_op jit(solution)/shard_map/pallas_call | solution.py:17
  106.9 8.3 %shard_map.128 = (f32[96,2048]{1,0:T(8,128)S(1)}, bf16[96,2048]{1,0:T(8,128)(2,1)S(1)}) custom-call(bf16[24,2048]{1,0:T(8,128)(2,1)S(1)} %collective-permute-done.16.refs_0_, bf16[24,2048]{1,0:T(8,128)(2,1)S(1)} %collective-permute-done.17.refs_1_, bf16[24,2048]{1,0:T(8,128)(2,1)S(1)} %collective-permute-done.18.refs_2_, ...), custom_call_target="tpu_custom_call" | custom-call | tf_op jit(solution)/shard_map/pallas_call | solution.py:17
  115.3 1.3 collective-permute-start.31
  116.5 6.6 %collective-permute-done.31.far_ref = bf16[96,2048]{1,0:T(8,128)(2,1)S(1)} collective-permute-done((bf16[96,2048]{1,0:T(8,128)(2,1)S(1)}, bf16[96,2048]{1,0:T(8,128)(2,1)S(1)}, u32[]{:S(2)}, u32[]{:S(2)}) %collective-permute-start.31) | collective-permute-done | bytes 393248 | tf_op jit(solution)/shard_map/ppermute | solution.py:234
  123.2 1.1 collective-permute-start.32
  124.3 1.2 collective-permute-start.33
  125.5 2.1 %collective-permute-start.34 = (bf16[24,2048]{1,0:T(8,128)(2,1)S(1)}, bf16[24,2048]{1,0:T(8,128)(2,1)S(1)}, u32[]{:S(2)}, u32[]{:S(2)}) collective-permute-start(bf16[24,2048]{1,0:T(8,128)(2,1)S(1)} %get-tuple-element.51), channel_id=1, source_target_pairs={{0,12},{1,13},{2,14},{3,15},{4,8},{5,9},{6,10},{7,11},{8,4},{9,5},... | collective-permute-start | bytes 294920 | tf_op jit(solution)/shard_map/ppermute | solution.py:234
  127.9 3.0 %collective-permute-done.33.refs_2_ = bf16[24,2048]{1,0:T(8,128)(2,1)S(1)} collective-permute-done((bf16[24,2048]{1,0:T(8,128)(2,1)S(1)}, bf16[24,2048]{1,0:T(8,128)(2,1)S(1)}, u32[]{:S(2)}, u32[]{:S(2)}) %collective-permute-start.33) | collective-permute-done | bytes 98336 | tf_op jit(solution)/shard_map/ppermute | solution.py:234
  130.9 1.1 collective-permute-done.34.refs_3_
  132.0 1.6 %shard_map.130 = bf16[1,128,4096]{2,1,0:T(8,128)(2,1)} custom-call(s32[1,128,8]{2,1,0:T(8,128)S(1)} %copy.13.ids_ref, bf16[24,2048]{1,0:T(8,128)(2,1)S(1)} %get-tuple-element.48.refs_0_, bf16[24,2048]{1,0:T(8,128)(2,1)S(1)} %collective-permute-done.32.refs_1_, bf16[24,2048]{1,0:T(8,128)(2,1)S(1)} %collective-permute-done.33.refs_2_, ...), custom_call_target="tpu_custom_call" | custom-call | tf_op jit(solution)/shard_map/pallas_call | solution.py:17
  (55 shorter events, 10.0 us)
Async XLA Ops:
  0.6 40.9 %copy-start = (bf16[1,1,4096,256]{3,2,1,0:T(8,128)(2,1)S(1)}, bf16[1,1,4096,256]{3,2,1,0:T(8,128)(2,1)}, u32[]{:S(2)}) copy-start(bf16[1,1,4096,256]{3,2,1,0:T(8,128)(2,1)} %param.19) | copy-start | bytes 6291460
  0.6 40.9 %collective-permute-start.9 = (bf16[4096,256]{1,0:T(8,128)(2,1)}, bf16[4096,256]{1,0:T(8,128)(2,1)}, u32[]{:S(2)}, u32[]{:S(2)}) collective-permute-start(bf16[4096,256]{1,0:T(8,128)(2,1)} %bitcast.3), channel_id=1, source_target_pairs={{0,1},{1,0},{2,3},{3,2},{4,5},{5,4},{6,7},{7,6},{8,9},{9,8},{10,11... | collective-permute-start | bytes 6291464 | tf_op jit(solution)/shard_map/ppermute | solution.py:234
  1.2 40.4 %collective-permute-start.10 = (bf16[4096,256]{1,0:T(8,128)(2,1)}, bf16[4096,256]{1,0:T(8,128)(2,1)}, u32[]{:S(2)}, u32[]{:S(2)}) collective-permute-start(bf16[4096,256]{1,0:T(8,128)(2,1)} %bitcast.7), channel_id=1, source_target_pairs={{0,1},{1,0},{2,3},{3,2},{4,5},{5,4},{6,7},{7,6},{8,9},{9,8},{10,11... | collective-permute-start | bytes 6291464 | tf_op jit(solution)/shard_map/ppermute | solution.py:234
  1.2 40.3 %collective-permute-start.11 = (bf16[256,4096]{1,0:T(8,128)(2,1)}, bf16[256,4096]{1,0:T(8,128)(2,1)}, u32[]{:S(2)}, u32[]{:S(2)}) collective-permute-start(bf16[256,4096]{1,0:T(8,128)(2,1)} %bitcast.11), channel_id=1, source_target_pairs={{0,1},{1,0},{2,3},{3,2},{4,5},{5,4},{6,7},{7,6},{8,9},{9,8},{10,11... | collective-permute-start | bytes 6291464 | tf_op jit(solution)/shard_map/ppermute | solution.py:234
  3.2 1.2 copy-start.2
  4.5 1.2 copy-start.3
  6.5 12.3 %collective-permute-start.2 = (bf16[2,24,2048]{2,1,0:T(8,128)(2,1)S(1)}, bf16[2,24,2048]{2,1,0:T(8,128)(2,1)S(1)}, u32[]{:S(2)}, u32[]{:S(2)}) collective-permute-start(bf16[2,24,2048]{2,1,0:T(8,128)(2,1)S(1)} %get-tuple-element.28), channel_id=1, source_target_pairs={{0,4},{1,5},{2,6},{3,7},{4,0},{5,1},{6,2},{7,3},{8,12},{9,13},{10,... | collective-permute-start | bytes 589832 | tf_op jit(solution)/shard_map/ppermute | solution.py:234
  9.2 12.2 %collective-permute-start.3 = (bf16[2,24,2048]{2,1,0:T(8,128)(2,1)S(1)}, bf16[2,24,2048]{2,1,0:T(8,128)(2,1)S(1)}, u32[]{:S(2)}, u32[]{:S(2)}) collective-permute-start(bf16[2,24,2048]{2,1,0:T(8,128)(2,1)S(1)} %get-tuple-element.29), channel_id=1, source_target_pairs={{0,8},{1,9},{2,10},{3,11},{4,12},{5,13},{6,14},{7,15},{8,0},{9,1},... | collective-permute-start | bytes 589832 | tf_op jit(solution)/shard_map/ppermute | solution.py:234
  18.8 8.6 %collective-permute-start.4 = (bf16[2,24,2048]{2,1,0:T(8,128)(2,1)S(1)}, bf16[2,24,2048]{2,1,0:T(8,128)(2,1)S(1)}, u32[]{:S(2)}, u32[]{:S(2)}) collective-permute-start(bf16[2,24,2048]{2,1,0:T(8,128)(2,1)S(1)} %get-tuple-element.30), channel_id=1, source_target_pairs={{0,12},{1,13},{2,14},{3,15},{4,8},{5,9},{6,10},{7,11},{8,4},{9,5},... | collective-permute-start | bytes 589832 | tf_op jit(solution)/shard_map/ppermute | solution.py:234
  21.4 33.0 %copy-start.8 = (s32[1,128,8]{1,2,0:T(8,128)S(1)}, s32[1,128,8]{1,2,0:T(8,128)}, u32[]{:S(2)}) copy-start(s32[1,128,8]{1,2,0:T(8,128)} %param.17) | copy-start | bytes 12292
  21.4 33.1 %copy-start.4 = (bf16[1,128,4096]{2,1,0:T(8,128)(2,1)S(1)}, bf16[1,128,4096]{2,1,0:T(8,128)(2,1)}, u32[]{:S(2)}) copy-start(bf16[1,128,4096]{2,1,0:T(8,128)(2,1)} %x_ref.3) | copy-start | bytes 3145732
  21.4 7.4 %collective-permute-start.5 = (bf16[2,24,2048]{2,1,0:T(8,128)(2,1)S(1)}, bf16[2,24,2048]{2,1,0:T(8,128)(2,1)S(1)}, u32[]{:S(2)}, u32[]{:S(2)}) collective-permute-start(bf16[2,24,2048]{2,1,0:T(8,128)(2,1)S(1)} %get-tuple-element.27.refs_0_), channel_id=1, source_target_pairs={{0,2},{1,3},{2,0},{3,1},{4,6},{5,7},{6,4},{7,5},{8,10},{9,11},{10,... | collective-permute-start | bytes 589832 | tf_op jit(solution)/shard_map/ppermute | solution.py:234
  27.3 7.8 %collective-permute-start.6 = (bf16[2,24,2048]{2,1,0:T(8,128)(2,1)S(1)}, bf16[2,24,2048]{2,1,0:T(8,128)(2,1)S(1)}, u32[]{:S(2)}, u32[]{:S(2)}) collective-permute-start(bf16[2,24,2048]{2,1,0:T(8,128)(2,1)S(1)} %collective-permute-done.2.refs_1_), channel_id=1, source_target_pairs={{0,2},{1,3},{2,0},{3,1},{4,6},{5,7},{6,4},{7,5},{8,10},{9,11},{10,... | collective-permute-start | bytes 589832 | tf_op jit(solution)/shard_map/ppermute | solution.py:234
  28.8 10.5 %collective-permute-start.7 = (bf16[2,24,2048]{2,1,0:T(8,128)(2,1)S(1)}, bf16[2,24,2048]{2,1,0:T(8,128)(2,1)S(1)}, u32[]{:S(2)}, u32[]{:S(2)}) collective-permute-start(bf16[2,24,2048]{2,1,0:T(8,128)(2,1)S(1)} %collective-permute-done.3.refs_2_), channel_id=1, source_target_pairs={{0,2},{1,3},{2,0},{3,1},{4,6},{5,7},{6,4},{7,5},{8,10},{9,11},{10,... | collective-permute-start | bytes 589832 | tf_op jit(solution)/shard_map/ppermute | solution.py:234
  35.2 6.4 %collective-permute-start.8 = (bf16[2,24,2048]{2,1,0:T(8,128)(2,1)S(1)}, bf16[2,24,2048]{2,1,0:T(8,128)(2,1)S(1)}, u32[]{:S(2)}, u32[]{:S(2)}) collective-permute-start(bf16[2,24,2048]{2,1,0:T(8,128)(2,1)S(1)} %collective-permute-done.4.refs_3_), channel_id=1, source_target_pairs={{0,2},{1,3},{2,0},{3,1},{4,6},{5,7},{6,4},{7,5},{8,10},{9,11},{10,... | collective-permute-start | bytes 589832 | tf_op jit(solution)/shard_map/ppermute | solution.py:234
  52.3 0.9 copy-start.6
  53.2 16.9 %copy-start.9 = (f32[1,128,8]{1,2,0:T(8,128)S(1)}, f32[1,128,8]{1,2,0:T(8,128)}, u32[]{:S(2)}) copy-start(f32[1,128,8]{1,2,0:T(8,128)} %param.18) | copy-start | bytes 12292
  53.2 9.4 %collective-permute-start.12 = (bf16[96,2048]{1,0:T(8,128)(2,1)}, bf16[96,2048]{1,0:T(8,128)(2,1)}, u32[]{:S(2)}, u32[]{:S(2)}) collective-permute-start(bf16[96,2048]{1,0:T(8,128)(2,1)} %get-tuple-element.32), channel_id=1, source_target_pairs={{0,2},{1,3},{2,0},{3,1},{4,6},{5,7},{6,4},{7,5},{8,10},{9,11},{10,... | collective-permute-start | bytes 1179656 | tf_op jit(solution)/shard_map/ppermute | solution.py:234
  55.8 21.1 %collective-permute-start.24 = (bf16[24,2048]{1,0:T(8,128)(2,1)}, bf16[24,2048]{1,0:T(8,128)(2,1)S(1)}, u32[]{:S(2)}, u32[]{:S(2)}) collective-permute-start(bf16[24,2048]{1,0:T(8,128)(2,1)} %get-tuple-element.43), channel_id=1, source_target_pairs={{0,4},{1,5},{2,6},{3,7},{4,0},{5,1},{6,2},{7,3},{8,12},{9,13},{10,... | collective-permute-start | bytes 294920 | tf_op jit(solution)/shard_map/ppermute | solution.py:234
  59.9 19.6 %collective-permute-start.25 = (bf16[24,2048]{1,0:T(8,128)(2,1)}, bf16[24,2048]{1,0:T(8,128)(2,1)S(1)}, u32[]{:S(2)}, u32[]{:S(2)}) collective-permute-start(bf16[24,2048]{1,0:T(8,128)(2,1)} %get-tuple-element.44), channel_id=1, source_target_pairs={{0,8},{1,9},{2,10},{3,11},{4,12},{5,13},{6,14},{7,15},{8,0},{9,1},... | collective-permute-start | bytes 294920 | tf_op jit(solution)/shard_map/ppermute | solution.py:234
  62.5 1.1 copy-start.7
  64.7 16.3 %collective-permute-start.13 = (bf16[24,2048]{1,0:T(8,128)(2,1)S(1)}, bf16[24,2048]{1,0:T(8,128)(2,1)S(1)}, u32[]{:S(2)}, u32[]{:S(2)}) collective-permute-start(bf16[24,2048]{1,0:T(8,128)(2,1)S(1)} %get-tuple-element.34), channel_id=1, source_target_pairs={{0,4},{1,5},{2,6},{3,7},{4,0},{5,1},{6,2},{7,3},{8,12},{9,13},{10,... | collective-permute-start | bytes 294920 | tf_op jit(solution)/shard_map/ppermute | solution.py:234
  70.2 4.3 %collective-permute-start.1 = (f32[1,128,8]{2,1,0:T(8,128)S(1)}, f32[1,128,8]{2,1,0:T(8,128)S(1)}, u32[]{:S(2)}, u32[]{:S(2)}) collective-permute-start(f32[1,128,8]{2,1,0:T(8,128)S(1)} %copy.14), channel_id=1, source_target_pairs={{0,16},{16,0},{1,17},{17,1},{2,18},{18,2},{3,19},{19,3},{4,20},{20... | collective-permute-start | bytes 12296 | tf_op jit(solution)/shard_map/ppermute | solution.py:249
  71.4 4.3 %collective-permute-start = (s32[1,128,8]{2,1,0:T(8,128)S(1)}, s32[1,128,8]{2,1,0:T(8,128)S(1)}, u32[]{:S(2)}, u32[]{:S(2)}) collective-permute-start(s32[1,128,8]{2,1,0:T(8,128)S(1)} %copy.13.ids_ref), channel_id=1, source_target_pairs={{0,16},{16,0},{1,17},{17,1},{2,18},{18,2},{3,19},{19,3},{4,20},{20... | collective-permute-start | bytes 12296 | tf_op jit(solution)/shard_map/ppermute | solution.py:249
  74.5 9.9 %collective-permute-start.14 = (bf16[24,2048]{1,0:T(8,128)(2,1)S(1)}, bf16[24,2048]{1,0:T(8,128)(2,1)S(1)}, u32[]{:S(2)}, u32[]{:S(2)}) collective-permute-start(bf16[24,2048]{1,0:T(8,128)(2,1)S(1)} %get-tuple-element.35), channel_id=1, source_target_pairs={{0,8},{1,9},{2,10},{3,11},{4,12},{5,13},{6,14},{7,15},{8,0},{9,1},... | collective-permute-start | bytes 294920 | tf_op jit(solution)/shard_map/ppermute | solution.py:234
  75.7 10.2 %collective-permute-start.15 = (bf16[24,2048]{1,0:T(8,128)(2,1)S(1)}, bf16[24,2048]{1,0:T(8,128)(2,1)S(1)}, u32[]{:S(2)}, u32[]{:S(2)}) collective-permute-start(bf16[24,2048]{1,0:T(8,128)(2,1)S(1)} %get-tuple-element.36), channel_id=1, source_target_pairs={{0,12},{1,13},{2,14},{3,15},{4,8},{5,9},{6,10},{7,11},{8,4},{9,5},... | collective-permute-start | bytes 294920 | tf_op jit(solution)/shard_map/ppermute | solution.py:234
  76.9 12.8 %collective-permute-start.26 = (bf16[24,2048]{1,0:T(8,128)(2,1)S(1)}, bf16[24,2048]{1,0:T(8,128)(2,1)S(1)}, u32[]{:S(2)}, u32[]{:S(2)}) collective-permute-start(bf16[24,2048]{1,0:T(8,128)(2,1)S(1)} %get-tuple-element.45), channel_id=1, source_target_pairs={{0,12},{1,13},{2,14},{3,15},{4,8},{5,9},{6,10},{7,11},{8,4},{9,5},... | collective-permute-start | bytes 294920 | tf_op jit(solution)/shard_map/ppermute | solution.py:234
  79.5 11.5 %collective-permute-start.27 = (bf16[24,2048]{1,0:T(8,128)(2,1)S(1)}, bf16[24,2048]{1,0:T(8,128)(2,1)S(1)}, u32[]{:S(2)}, u32[]{:S(2)}) collective-permute-start(bf16[24,2048]{1,0:T(8,128)(2,1)S(1)} %get-tuple-element.42.refs_0_), channel_id=1, source_target_pairs={{0,2},{1,3},{2,0},{3,1},{4,6},{5,7},{6,4},{7,5},{8,10},{9,11},{10,... | collective-permute-start | bytes 294920 | tf_op jit(solution)/shard_map/ppermute | solution.py:234
  81.0 12.0 %collective-permute-start.28 = (bf16[24,2048]{1,0:T(8,128)(2,1)S(1)}, bf16[24,2048]{1,0:T(8,128)(2,1)S(1)}, u32[]{:S(2)}, u32[]{:S(2)}) collective-permute-start(bf16[24,2048]{1,0:T(8,128)(2,1)S(1)} %collective-permute-done.24.refs_1_), channel_id=1, source_target_pairs={{0,2},{1,3},{2,0},{3,1},{4,6},{5,7},{6,4},{7,5},{8,10},{9,11},{10,... | collective-permute-start | bytes 294920 | tf_op jit(solution)/shard_map/ppermute | solution.py:234
  84.3 11.1 %collective-permute-start.29 = (bf16[24,2048]{1,0:T(8,128)(2,1)S(1)}, bf16[24,2048]{1,0:T(8,128)(2,1)S(1)}, u32[]{:S(2)}, u32[]{:S(2)}) collective-permute-start(bf16[24,2048]{1,0:T(8,128)(2,1)S(1)} %collective-permute-done.25.refs_2_), channel_id=1, source_target_pairs={{0,2},{1,3},{2,0},{3,1},{4,6},{5,7},{6,4},{7,5},{8,10},{9,11},{10,... | collective-permute-start | bytes 294920 | tf_op jit(solution)/shard_map/ppermute | solution.py:234
  85.8 1.2 copy-start.5
  88.7 8.5 %collective-permute-start.16 = (bf16[24,2048]{1,0:T(8,128)(2,1)S(1)}, bf16[24,2048]{1,0:T(8,128)(2,1)S(1)}, u32[]{:S(2)}, u32[]{:S(2)}) collective-permute-start(bf16[24,2048]{1,0:T(8,128)(2,1)S(1)} %get-tuple-element.38), channel_id=1, source_target_pairs={{0,16},{1,17},{2,18},{3,19},{4,20},{5,21},{6,22},{7,23},{8,24},{9,... | collective-permute-start | bytes 294920 | tf_op jit(solution)/shard_map/ppermute | solution.py:307
  89.7 7.8 %collective-permute-start.17 = (bf16[24,2048]{1,0:T(8,128)(2,1)S(1)}, bf16[24,2048]{1,0:T(8,128)(2,1)S(1)}, u32[]{:S(2)}, u32[]{:S(2)}) collective-permute-start(bf16[24,2048]{1,0:T(8,128)(2,1)S(1)} %get-tuple-element.39), channel_id=1, source_target_pairs={{0,20},{1,21},{2,22},{3,23},{4,16},{5,17},{6,18},{7,19},{8,28},{9,... | collective-permute-start | bytes 294920 | tf_op jit(solution)/shard_map/ppermute | solution.py:307
  91.0 8.2 %collective-permute-start.18 = (bf16[24,2048]{1,0:T(8,128)(2,1)S(1)}, bf16[24,2048]{1,0:T(8,128)(2,1)S(1)}, u32[]{:S(2)}, u32[]{:S(2)}) collective-permute-start(bf16[24,2048]{1,0:T(8,128)(2,1)S(1)} %get-tuple-element.40), channel_id=1, source_target_pairs={{0,24},{1,25},{2,26},{3,27},{4,28},{5,29},{6,30},{7,31},{8,16},{9,... | collective-permute-start | bytes 294920 | tf_op jit(solution)/shard_map/ppermute | solution.py:307
  93.0 7.4 %collective-permute-start.19 = (bf16[24,2048]{1,0:T(8,128)(2,1)S(1)}, bf16[24,2048]{1,0:T(8,128)(2,1)S(1)}, u32[]{:S(2)}, u32[]{:S(2)}) collective-permute-start(bf16[24,2048]{1,0:T(8,128)(2,1)S(1)} %get-tuple-element.41), channel_id=1, source_target_pairs={{0,28},{1,29},{2,30},{3,31},{4,24},{5,25},{6,26},{7,27},{8,20},{9,... | collective-permute-start | bytes 294920 | tf_op jit(solution)/shard_map/ppermute | solution.py:307
  95.5 5.8 %collective-permute-start.30 = (bf16[24,2048]{1,0:T(8,128)(2,1)S(1)}, bf16[24,2048]{1,0:T(8,128)(2,1)S(1)}, u32[]{:S(2)}, u32[]{:S(2)}) collective-permute-start(bf16[24,2048]{1,0:T(8,128)(2,1)S(1)} %collective-permute-done.26.refs_3_), channel_id=1, source_target_pairs={{0,2},{1,3},{2,0},{3,1},{4,6},{5,7},{6,4},{7,5},{8,10},{9,11},{10,... | collective-permute-start | bytes 294920 | tf_op jit(solution)/shard_map/ppermute | solution.py:234
  97.2 9.7 %collective-permute-start.20 = (bf16[24,2048]{1,0:T(8,128)(2,1)S(1)}, bf16[24,2048]{1,0:T(8,128)(2,1)S(1)}, u32[]{:S(2)}, u32[]{:S(2)}) collective-permute-start(bf16[24,2048]{1,0:T(8,128)(2,1)S(1)} %collective-permute-done.16.refs_0_), channel_id=1, source_target_pairs={{0,2},{1,3},{2,0},{3,1},{4,6},{5,7},{6,4},{7,5},{8,10},{9,11},{10,... | collective-permute-start | bytes 294920 | tf_op jit(solution)/shard_map/ppermute | solution.py:234
  97.5 9.4 %collective-permute-start.21 = (bf16[24,2048]{1,0:T(8,128)(2,1)S(1)}, bf16[24,2048]{1,0:T(8,128)(2,1)S(1)}, u32[]{:S(2)}, u32[]{:S(2)}) collective-permute-start(bf16[24,2048]{1,0:T(8,128)(2,1)S(1)} %collective-permute-done.17.refs_1_), channel_id=1, source_target_pairs={{0,2},{1,3},{2,0},{3,1},{4,6},{5,7},{6,4},{7,5},{8,10},{9,11},{10,... | collective-permute-start | bytes 294920 | tf_op jit(solution)/shard_map/ppermute | solution.py:234
  99.2 7.7 %collective-permute-start.22 = (bf16[24,2048]{1,0:T(8,128)(2,1)S(1)}, bf16[24,2048]{1,0:T(8,128)(2,1)S(1)}, u32[]{:S(2)}, u32[]{:S(2)}) collective-permute-start(bf16[24,2048]{1,0:T(8,128)(2,1)S(1)} %collective-permute-done.18.refs_2_), channel_id=1, source_target_pairs={{0,2},{1,3},{2,0},{3,1},{4,6},{5,7},{6,4},{7,5},{8,10},{9,11},{10,... | collective-permute-start | bytes 294920 | tf_op jit(solution)/shard_map/ppermute | solution.py:234
  100.4 6.5 %collective-permute-start.23 = (bf16[24,2048]{1,0:T(8,128)(2,1)S(1)}, bf16[24,2048]{1,0:T(8,128)(2,1)S(1)}, u32[]{:S(2)}, u32[]{:S(2)}) collective-permute-start(bf16[24,2048]{1,0:T(8,128)(2,1)S(1)} %collective-permute-done.19.refs_3_), channel_id=1, source_target_pairs={{0,2},{1,3},{2,0},{3,1},{4,6},{5,7},{6,4},{7,5},{8,10},{9,11},{10,... | collective-permute-start | bytes 294920 | tf_op jit(solution)/shard_map/ppermute | solution.py:234
  101.2 1.6 %copy-start.1 = (bf16[1,1,4096,256]{3,2,1,0:T(8,128)(2,1)S(1)}, bf16[1,1,4096,256]{3,2,1,0:T(8,128)(2,1)}, u32[]{:S(2)}) copy-start(bf16[1,1,4096,256]{3,2,1,0:T(8,128)(2,1)} %param.20) | copy-start | bytes 6291460
  115.3 7.8 %collective-permute-start.31 = (bf16[96,2048]{1,0:T(8,128)(2,1)S(1)}, bf16[96,2048]{1,0:T(8,128)(2,1)S(1)}, u32[]{:S(2)}, u32[]{:S(2)}) collective-permute-start(bf16[96,2048]{1,0:T(8,128)(2,1)S(1)} %get-tuple-element.47), channel_id=1, source_target_pairs={{0,2},{1,3},{2,0},{3,1},{4,6},{5,7},{6,4},{7,5},{8,10},{9,11},{10,... | collective-permute-start | bytes 1179656 | tf_op jit(solution)/shard_map/ppermute | solution.py:234
  123.2 4.7 %collective-permute-start.32 = (bf16[24,2048]{1,0:T(8,128)(2,1)S(1)}, bf16[24,2048]{1,0:T(8,128)(2,1)S(1)}, u32[]{:S(2)}, u32[]{:S(2)}) collective-permute-start(bf16[24,2048]{1,0:T(8,128)(2,1)S(1)} %get-tuple-element.49), channel_id=1, source_target_pairs={{0,4},{1,5},{2,6},{3,7},{4,0},{5,1},{6,2},{7,3},{8,12},{9,13},{10,... | collective-permute-start | bytes 294920 | tf_op jit(solution)/shard_map/ppermute | solution.py:234
  124.3 6.6 %collective-permute-start.33 = (bf16[24,2048]{1,0:T(8,128)(2,1)S(1)}, bf16[24,2048]{1,0:T(8,128)(2,1)S(1)}, u32[]{:S(2)}, u32[]{:S(2)}) collective-permute-start(bf16[24,2048]{1,0:T(8,128)(2,1)S(1)} %get-tuple-element.50), channel_id=1, source_target_pairs={{0,8},{1,9},{2,10},{3,11},{4,12},{5,13},{6,14},{7,15},{8,0},{9,1},... | collective-permute-start | bytes 294920 | tf_op jit(solution)/shard_map/ppermute | solution.py:234
  125.5 6.5 %collective-permute-start.34 = (bf16[24,2048]{1,0:T(8,128)(2,1)S(1)}, bf16[24,2048]{1,0:T(8,128)(2,1)S(1)}, u32[]{:S(2)}, u32[]{:S(2)}) collective-permute-start(bf16[24,2048]{1,0:T(8,128)(2,1)S(1)} %get-tuple-element.51), channel_id=1, source_target_pairs={{0,12},{1,13},{2,14},{3,15},{4,8},{5,9},{6,10},{7,11},{8,4},{9,5},... | collective-permute-start | bytes 294920 | tf_op jit(solution)/shard_map/ppermute | solution.py:234

commit v2 on v1

v2 whole, which is shorter than its diff:
```python
import functools

import jax
import jax.numpy as jnp
from jax import lax
from jax.experimental import pallas as pl
from jax.experimental.pallas import tpu as pltpu
from jax.sharding import PartitionSpec as P

EXPERTS = 128
SPLIT = 4
F32, BF16 = jnp.float32, jnp.bfloat16
MIB = 1024 * 1024
COMPUTE_MIB = 26
PACK_MIB = 44


def call(body, outs, args, mib, away=(), scratch=(), us=1.0):
    return pl.pallas_call(
        body,
        out_shape=outs,
        in_specs=[
            pl.BlockSpec(memory_space=pl.ANY if i in away else pltpu.VMEM)
            for i in range(len(args))
        ],
        out_specs=jax.tree.map(lambda _: pl.BlockSpec(memory_space=pltpu.VMEM), outs),
        scratch_shapes=scratch,
        compiler_params=pltpu.CompilerParams(vmem_limit_bytes=mib * MIB),
        cost_estimate=pl.CostEstimate(
            flops=0, bytes_accessed=int(us * 3.6e6), transcendentals=0
        ),
    )(*args)


def fetch(pairs, sems):
    copies = [pltpu.make_async_copy(a, b, sems.at[i]) for i, (a, b) in enumerate(pairs)]
    for c in copies:
        c.start()
    return copies


def row_parts(ref, buf, parts=4):
    step = buf.shape[0] // parts
    return [(ref.at[pl.ds(step * i, step)], buf.at[pl.ds(step * i, step)]) for i in range(parts)]


def sequence(window):
    return [k for k in range(2, window)] + [1, 0][-window:]


def tables(ids_t, window, cap, probs_t=None):
    me = lax.axis_index("expert") // SPLIT
    tok = ids_t.shape[1]
    weights = None
    if probs_t is not None:
        weights = probs_t / jnp.sum(probs_t, axis=0, keepdims=True)
    named, coefs = [], []
    for k in range(window):
        match = ids_t == (me ^ sequence(window)[k])
        named.append(jnp.sum(jnp.where(match, 1.0, 0.0), axis=0, keepdims=True))
        if probs_t is not None:
            coefs.append(jnp.sum(jnp.where(match, weights, 0.0), axis=0, keepdims=True))
    pad = [jnp.zeros((-window % 8, tok), F32)] if window % 8 else []
    stacked = jnp.concatenate(named + pad, axis=0).astype(BF16)
    before = (
        lax.broadcasted_iota(jnp.int32, (tok, tok), 0)
        < lax.broadcasted_iota(jnp.int32, (tok, tok), 1)
    ).astype(F32).astype(BF16)
    place = jnp.dot(stacked, before, preferred_element_type=F32)
    rows = lax.broadcasted_iota(jnp.int32, (2 * cap, tok), 0).astype(F32)
    top, bot, coef = [], [], []
    for k in range(window):
        slot = jnp.where(named[k] > 0.0, place[k : k + 1], -1000.0)
        upper = jnp.where(rows == slot, 1.0, 0.0)
        lower = jnp.where(rows == slot + cap, 1.0, 0.0)
        top.append(upper)
        bot.append(lower)
        if probs_t is not None:
            coef.append(jnp.sum((upper + lower) * coefs[k], axis=1, keepdims=True))
    top, bot = jnp.concatenate(top, axis=0), jnp.concatenate(bot, axis=0)
    return top, bot, jnp.concatenate(coef, axis=0) if coef else None


def gathered(top, bot, rows):
    half = rows.shape[1] // 2
    return jnp.dot(top.astype(BF16), rows[:, :half], preferred_element_type=F32) + jnp.dot(
        bot.astype(BF16), rows[:, half:], preferred_element_type=F32
    )


def pack_x(window, cap, ids_ref, x_ref, *refs):
    out_refs, (x_buf, sems) = refs[-2 - window : -2], refs[-2:]
    copies = fetch(row_parts(x_ref, x_buf), sems)
    top, bot, _ = tables(ids_ref[...], window, cap)
    for c in copies:
        c.wait()
    picked = gathered(top, bot, x_buf[...])
    for k in range(window):
        out_refs[k][...] = picked[2 * cap * k : 2 * cap * (k + 1)].astype(BF16)


def pack_grad(window, cap, ids_ref, probs_ref, ids_on_ref, probs_on_ref, grad_ref, *refs):
    keys_ref, *out_refs = refs[-3 - window : -2]
    grad_buf, sems = refs[-2:]
    topk = ids_on_ref.shape[0]
    keys_ref[:topk] = ids_on_ref[...].astype(F32)
    keys_ref[topk:] = probs_on_ref[...]
    copies = fetch(row_parts(grad_ref, grad_buf), sems)
    top, bot, coef = tables(ids_ref[...], window, cap, probs_ref[...])
    for c in copies:
        c.wait()
    picked = gathered(top, bot, grad_buf[...]) * coef
    for k in range(window):
        out_refs[k][...] = picked[2 * cap * k : 2 * cap * (k + 1)].astype(BF16)


def scattered(ids_ref, window, cap, blocks):
    top, bot, _ = tables(ids_ref[...], window, cap)
    rows = jnp.concatenate([b[...].astype(F32) for b in blocks], axis=0).astype(BF16)
    turned = (((0,), (0,)), ((), ()))
    left = lax.dot_general(top.astype(BF16), rows, turned, preferred_element_type=F32)
    right = lax.dot_general(bot.astype(BF16), rows, turned, preferred_element_type=F32)
    return left.astype(BF16), right.astype(BF16)


def relay(window, cap, ids_ref, keys_ref, grad_last_ref, *refs):
    topk = ids_ref.shape[0]
    blocks, dx_ref, out_refs = refs[:window], refs[window], refs[window + 1 : -2]
    grad_buf, sems = refs[-2:]
    copies = fetch(row_parts(grad_last_ref, grad_buf), sems)
    left, right = scattered(ids_ref, window, cap, blocks)
    half = left.shape[1]
    dx_ref[0, :, :half] = left
    dx_ref[0, :, half:] = right
    top, bot, coef = tables(
        keys_ref[:topk].astype(jnp.int32), window, cap, keys_ref[topk:]
    )
    for c in copies:
        c.wait()
    opening = lax.axis_index("pipe") == 0
    left = jnp.where(opening, grad_buf[:, :half], left)
    right = jnp.where(opening, grad_buf[:, half:], right)
    picked = coef * (
        jnp.dot(top.astype(BF16), left, preferred_element_type=F32)
        + jnp.dot(bot.astype(BF16), right, preferred_element_type=F32)
    )
    for k in range(window):
        out_refs[k][...] = picked[2 * cap * k : 2 * cap * (k + 1)].astype(BF16)


def finish(window, cap, ids_ref, *refs):
    blocks, dx_ref = refs[:window], refs[window]
    left, right = scattered(ids_ref, window, cap, blocks)
    half = left.shape[1]
    dx_ref[0, :, :half] = left
    dx_ref[0, :, half:] = right


NT = (((1,), (1,)), ((), ()))


def joined(blocks):
    return jnp.concatenate([b.astype(F32) for b in blocks], axis=0).astype(BF16)


def factors(rows, cap, gate_ref, up_ref):
    half = rows.shape[1]

    def product(ref):
        lower = jnp.dot(rows, ref[half:, :], preferred_element_type=F32)
        return jnp.dot(rows, ref[:half, :], preferred_element_type=F32) + pltpu.roll(
            lower, rows.shape[0] - cap, 0
        )

    gate, up = product(gate_ref), product(up_ref)
    sig = jax.nn.sigmoid(gate)
    return gate * sig, up * sig * (1.0 + gate * (1.0 - sig))


def hidden_grads(rows, cap, down_ref, for_up, for_gate):
    count, half = rows.shape
    valid = lax.broadcasted_iota(jnp.int32, (count, 1), 0) % (2 * cap) < cap
    lower = lax.dot_general(rows, down_ref[:, half:], NT, preferred_element_type=F32)
    back = lax.dot_general(
        rows, down_ref[:, :half], NT, preferred_element_type=F32
    ) + pltpu.roll(lower, count - cap, 0)
    d_up = jnp.where(valid, back * for_up, 0.0)
    d_gate = jnp.where(valid, back * for_gate, 0.0)
    return [
        (d.astype(BF16), pltpu.roll(d, cap, 0).astype(BF16)) for d in (d_gate, d_up)
    ]


def input_grads(lhs, refs, own_refs, far_refs, step=256):
    half = own_refs[0].shape[1]
    for n in range(0, half, step):
        total = None
        for (upper, lower), ref in zip(lhs, refs):
            term = lax.dot_general(
                upper, ref[n : n + step, :], NT, preferred_element_type=F32
            ) + lax.dot_general(
                lower, ref[half + n : half + n + step, :], NT, preferred_element_type=F32
            )
            total = term if total is None else total + term
        row = 0
        for ref in (*own_refs, *far_refs):
            ref[:, n : n + step] = total[row : row + ref.shape[0]].astype(ref.dtype)
            row += ref.shape[0]


def unit_x(blocks, cap, *refs):
    ins, weights, out_ref, bufs, sems = (
        refs[:blocks],
        refs[blocks : blocks + 4],
        refs[blocks + 4],
        refs[blocks + 5 : -1],
        refs[-1],
    )
    copies = fetch(list(zip(weights, bufs)), sems)
    x_rows = joined([b[...] for b in ins])
    for i in range(2):
        copies[2 * i].wait()
        copies[2 * i + 1].wait()
        out_ref[2 * i], out_ref[2 * i + 1] = factors(x_rows, cap, bufs[2 * i], bufs[2 * i + 1])


def unit_grad(blocks, cap, *refs):
    ins, scale_ref = refs[:blocks], refs[blocks]
    weights, outs = refs[blocks + 1 : blocks + 7], refs[blocks + 7 : -7]
    bufs, sems = refs[-7:-1], refs[-1]
    copies = fetch([(weights[i], bufs[i]) for i in (2, 5, 0, 1, 3, 4)], sems)
    grad_rows = joined([b[...] for b in ins])
    lhs = []
    for i in range(2):
        copies[i].wait()
        lhs += hidden_grads(grad_rows, cap, bufs[3 * i + 2], scale_ref[2 * i], scale_ref[2 * i + 1])
    for c in copies[2:]:
        c.wait()
    groups = len(outs) // 2
    input_grads(lhs, [bufs[i] for i in (0, 1, 3, 4)], outs[:groups], outs[groups:])


def add_far(cap, own_ref, far_ref, *out_refs):
    for k, out_ref in enumerate(out_refs):
        part = slice(2 * cap * k, 2 * cap * (k + 1))
        out_ref[...] = (own_ref[part] + far_ref[part].astype(F32)).astype(BF16)


def body(
    x_first,
    grad_first,
    x_second,
    grad_last,
    ids_first,
    probs_first,
    ids_second,
    probs_second,
    w_gate,
    w_up,
    w_down,
):
    tok, width = x_first.shape[1:]
    topk = ids_first.shape[2]
    devices = lax.axis_size("expert")
    sections = lax.axis_size("pipe")
    window = devices // SPLIT
    cap = 3 * tok * topk // (2 * EXPERTS)
    half = width // 2
    shape = jax.ShapeDtypeStruct

    def send(x, bits):
        return lax.ppermute(x, "expert", [(i, i ^ bits) for i in range(devices)])

    def plane(x, k):
        return send(x, SPLIT * k) if k else x

    def across(x):
        return send(x, 2)

    own_w = (w_gate[0, 0], w_up[0, 0], w_down[0, 0])
    msg = shape((2 * cap, half), BF16)
    pair = shape((2, 2 * cap, half), BF16)
    weights = own_w + tuple(send(w, 1) for w in own_w)
    bufs = [pltpu.VMEM(w.shape, BF16) for w in weights]
    dma = pltpu.SemaphoreType.DMA
    row_buf = pltpu.VMEM((tok, width), BF16)
    order = sequence(window)
    rows = window * 2 * cap
    after = lax.optimization_barrier

    ids_1, probs_1, ids_2, probs_2 = (
        jnp.swapaxes(a[0], 0, 1) for a in (ids_first, probs_first, ids_second, probs_second)
    )
    ring = [(s, (s + 1) % sections) for s in range(sections)]

    def listed(by_k):
        return [by_k[k] for k in order]

    def pack(ids, x, extra=()):
        made = call(
            functools.partial(pack_x, window, cap),
            [msg] * window,
            (ids, x, *extra),
            PACK_MIB if not extra else 16,
            away=range(1, 2 + len(extra)),
            scratch=[row_buf, dma((4,))],
            us=3.0,
        )
        return dict(zip(order, made))

    def forward(near, far):
        return call(
            functools.partial(unit_x, 2 * window, cap),
            shape((4, 2 * rows, w_gate.shape[3]), F32),
            (*listed(near), *listed(far), weights[0], weights[1], weights[3], weights[4]),
            COMPUTE_MIB,
            away=range(2 * window, 2 * window + 4),
            scratch=[bufs[0], bufs[1], bufs[3], bufs[4], dma((4,))],
            us=2.7,
        )

    groups = [order[:-2], order[-2:]] if window > 2 else [order]
    heights = [2 * cap * len(g) for g in groups]

    def backward(near, far, scales):
        made = call(
            functools.partial(unit_grad, 2 * window, cap),
            [shape((h, half), F32) for h in heights] + [shape((h, half), BF16) for h in heights],
            (*listed(near), *listed(far), scales, *weights),
            COMPUTE_MIB,
            away=range(2 * window + 1, 2 * window + 7),
            scratch=[*bufs, dma((6,))],
            us=5.7,
        )
        back = {}
        for group, own, far in zip(groups, made, made[len(groups) :]):
            far = across(far)
            sums = call(functools.partial(add_far, cap), [msg] * len(group), (own, far), 8)
            back.update({k: plane(sums[j], k) for j, k in enumerate(group)})
        return far, listed(back)

    x_1 = pack(ids_1, x_first[0])
    keys, *grad_1 = call(
        functools.partial(pack_grad, window, cap),
        [shape((2 * topk, tok), F32)] + [msg] * window,
        (ids_1, probs_1, ids_2, probs_2, grad_first[0], x_1[0]),
        PACK_MIB,
        away=(4, 5),
        scratch=[row_buf, dma((4,))],
        us=3.0,
    )
    grad_1 = dict(zip(order, grad_1))
    outer = [k for k in order if k > 1]
    near_x = {k: plane(x_1[k], k) for k in outer}
    near_x, grad_1, *peer_w = after((near_x, grad_1, *weights[3:]))
    weights = own_w + tuple(peer_w)
    near_g = {k: plane(grad_1[k], k) for k in outer}
    for k in (1, 0):
        near_x[k] = plane(x_1[k], k)
        near_g[k] = plane(grad_1[k], k)
    far_x = {k: across(near_x[k]) for k in (0, 1, *outer)}
    far_g = {k: across(near_g[k]) for k in (0, 1, *outer)}
    keys = lax.ppermute(after((keys, near_x[1]))[0], "pipe", ring)
    x_2 = pack(ids_2, x_second[0], (near_g[outer[-1]], keys))
    near_x2 = {k: plane(x_2[k], k) for k in order}
    arrived, back = backward(near_g, far_g, forward(near_x, far_x))
    near_x2 = after((near_x2, arrived))[0]
    far_x2 = {k: across(near_x2[k]) for k in order}
    scales = forward(near_x2, far_x2)
    dx_first, *grads = call(
        functools.partial(relay, window, cap),
        [shape((1, tok, width), BF16)] + [msg] * window,
        (ids_1, keys, grad_last, *back),
        16,
        away=(2,),
        scratch=[row_buf, dma((4,))],
        us=1.8,
    )
    near = {}
    for j, k in enumerate(order):
        pairs = [
            (s * devices + i, (s - 1) % sections * devices + (i ^ (SPLIT * k)))
            for s in range(sections)
            for i in range(devices)
        ]
        near[k] = lax.ppermute(grads[j], ("pipe", "expert"), pairs)
    far = {k: across(near[k]) for k in order[::-1]}
    _, back = backward(near, far, scales)
    dx_second = call(
        functools.partial(finish, window, cap),
        shape((1, tok, width), BF16),
        (ids_2, *back),
        16,
    )
    return dx_first, dx_second


def solution(mesh):
    split = P("pipe", "expert", None)
    stacked = P("pipe", "expert", None, None)
    return jax.shard_map(
        body,
        mesh=mesh,
        in_specs=(
            split,
            split,
            split,
            P("expert", None),
            split,
            split,
            split,
            split,
            stacked,
            stacked,
            stacked,
        ),
        out_specs=(split, split),
        check_vma=False,
    )
```

time: 134 us -> 114 us (0.85)
  waiting for transfers between devices: 43.5 us -> 27.5 us
  Pallas kernels: 29.5 us -> 22.2 us
  starting transfers between devices: 50.9 us -> 56.4 us
  local copies, waits for them, and re-layouts: 9.06 us -> 6.82 us
    ppermute x29 -> x38, waiting for transfers between devices: 38 us -> 23.8 us  [send(): return lax.ppermute(x, 'expert', [(i, i ^ bits) for i in range(devices)])]
    pallas_call x9 -> x13, Pallas kernels: 29.5 us -> 22.2 us  [call(): pl.pallas_call(body, out_shape=outs, in_specs=[pl.BlockSpec(memory_space=...]
    ppermute x29 -> x38, starting transfers between devices: 42.1 us -> 48.8 us  [send(): return lax.ppermute(x, 'expert', [(i, i ^ bits) for i in range(devices)])]
    unnamed x24 -> x26, local copies, waits for them, and re-layouts: 9.06 us -> 6.82 us
    ppermute x6 -> x5, waiting for transfers between devices: 5.42 us -> 3.63 us  [the longest x1 2.15 us: body(): keys = lax.ppermute(after((keys, near_x[1]))[0], 'pipe', ring)]
    ppermute x6 -> x5, starting transfers between devices: 8.83 us -> 7.56 us  [the longest x4 6.06 us: body(): near[k] = lax.ppermute(grads[j], ('pipe', 'expert'), pairs)]
  transfers between devices with their start and end apart: 35 -> 43, of which waited for: 15 -> 15; matrix products, arithmetic and copies ran while one was open for 1% -> 0% of each run, Pallas kernels for 6% -> 8%
where the time goes in v2:
time: 114 us
  starting transfers between devices  56.4 us (49%)
  waiting for transfers between devices  27.5 us (24%)
  Pallas kernels  22.2 us (19%)
  local copies, waits for them, and re-layouts  6.82 us (6%)
    ppermute x38, starting transfers between devices, send(): return lax.ppermute(x, 'expert', [(i, i ^ bits) for i in range(devices)])  48.8 us
    ppermute x38, waiting for transfers between devices, send(): return lax.ppermute(x, 'expert', [(i, i ^ bits) for i in range(devices)])  23.8 us
    pallas_call x13, Pallas kernels, call(): pl.pallas_call(body, out_shape=outs, in_specs=[pl.BlockSpec(memory_space=...  22.2 us
    unnamed x26, local copies, waits for them, and re-layouts  6.82 us
    ppermute x4, starting transfers between devices, body(): near[k] = lax.ppermute(grads[j], ('pipe', 'expert'), pairs)  6.06 us
  transfers between devices with their start and end apart: 43, of which 15 were waited for; matrix products, arithmetic and copies ran while one was open for 0% of the time, Pallas kernels for 8%

profile of v2, /device:TPU:0, one launch (start us, length us, event | category | flops | bytes accessed | tf_op | source)
XLA Modules:
  0.0 113.7 jit_solution(9288483598229327460)
XLA Ops:
  1.7 1.2 %copy-done.3 = bf16[1,128,4096]{2,1,0:T(8,128)(2,1)S(1)} copy-done((bf16[1,128,4096]{2,1,0:T(8,128)(2,1)S(1)}, bf16[1,128,4096]{2,1,0:T(8,128)(2,1)}, u32[]{:S(2)}) %copy-start.3) | copy-done | bytes 1048600
  4.2 2.7 %collective-permute-start = (bf16[24,2048]{1,0:T(8,128)(2,1)S(1)}, bf16[24,2048]{1,0:T(8,128)(2,1)S(1)}, u32[]{:S(2)}, u32[]{:S(2)}) collective-permute-start(bf16[24,2048]{1,0:T(8,128)(2,1)S(1)} %get-tuple-element.52), channel_id=1, source_target_pairs={{0,4},{1,5},{2,6},{3,7},{4,0},{5,1},{6,2},{7,3},{8,12},{9,13},{10,... | collective-permute-start | bytes 294920 | tf_op jit(solution)/shard_map/ppermute | solution.py:272
  6.9 2.6 %collective-permute-start.2 = (bf16[24,2048]{1,0:T(8,128)(2,1)S(1)}, bf16[24,2048]{1,0:T(8,128)(2,1)S(1)}, u32[]{:S(2)}, u32[]{:S(2)}) collective-permute-start(bf16[24,2048]{1,0:T(8,128)(2,1)S(1)} %get-tuple-element.54), channel_id=1, source_target_pairs={{0,8},{1,9},{2,10},{3,11},{4,12},{5,13},{6,14},{7,15},{8,0},{9,1},... | collective-permute-start | bytes 294920 | tf_op jit(solution)/shard_map/ppermute | solution.py:272
  9.5 0.8 collective-permute-done.refs_2_
  10.3 4.9 %collective-permute-start.3 = (bf16[24,2048]{1,0:T(8,128)(2,1)S(1)}, bf16[24,2048]{1,0:T(8,128)(2,1)S(1)}, u32[]{:S(2)}, u32[]{:S(2)}) collective-permute-start(bf16[24,2048]{1,0:T(8,128)(2,1)S(1)} %get-tuple-element.55), channel_id=1, source_target_pairs={{0,12},{1,13},{2,14},{3,15},{4,8},{5,9},{6,10},{7,11},{8,4},{9,5},... | collective-permute-start | bytes 294920 | tf_op jit(solution)/shard_map/ppermute | solution.py:272
  15.2 1.5 %collective-permute-start.17 = (bf16[24,2048]{1,0:T(8,128)(2,1)S(1)}, bf16[24,2048]{1,0:T(8,128)(2,1)S(1)}, u32[]{:S(2)}, u32[]{:S(2)}) collective-permute-start(bf16[24,2048]{1,0:T(8,128)(2,1)S(1)} %get-tuple-element.50.refs_0_.refs_3_), channel_id=1, source_target_pairs={{0,2},{1,3},{2,0},{3,1},{4,6},{5,7},{6,4},{7,5},{8,10},{9,11},{10,... | collective-permute-start | bytes 294920 | tf_op jit(solution)/shard_map/ppermute | solution.py:272
  16.7 1.2 %copy-done.4 = bf16[1,128,4096]{2,1,0:T(8,128)(2,1)S(1)} copy-done((bf16[1,128,4096]{2,1,0:T(8,128)(2,1)S(1)}, bf16[1,128,4096]{2,1,0:T(8,128)(2,1)}, u32[]{:S(2)}) %copy-start.4) | copy-done | bytes 1048600
  21.6 2.8 %collective-permute-start.8 = (bf16[24,2048]{1,0:T(8,128)(2,1)S(1)}, bf16[24,2048]{1,0:T(8,128)(2,1)S(1)}, u32[]{:S(2)}, u32[]{:S(2)}) collective-permute-start(bf16[24,2048]{1,0:T(8,128)(2,1)S(1)} %get-tuple-element.61), channel_id=1, source_target_pairs={{0,12},{1,13},{2,14},{3,15},{4,8},{5,9},{6,10},{7,11},{8,4},{9,5},... | collective-permute-start | bytes 294920 | tf_op jit(solution)/shard_map/ppermute | solution.py:272
  24.9 1.5 %collective-permute-start.14 = (bf16[24,2048]{1,0:T(8,128)(2,1)S(1)}, bf16[24,2048]{1,0:T(8,128)(2,1)S(1)}, u32[]{:S(2)}, u32[]{:S(2)}) collective-permute-start(bf16[24,2048]{1,0:T(8,128)(2,1)S(1)} %collective-permute-done.2.refs_0_), channel_id=1, source_target_pairs={{0,2},{1,3},{2,0},{3,1},{4,6},{5,7},{6,4},{7,5},{8,10},{9,11},{10,... | collective-permute-start | bytes 294920 | tf_op jit(solution)/shard_map/ppermute | solution.py:272
  26.9 3.2 %collective-permute-done.7.refs_0_ = bf16[24,2048]{1,0:T(8,128)(2,1)S(1)} collective-permute-done((bf16[24,2048]{1,0:T(8,128)(2,1)S(1)}, bf16[24,2048]{1,0:T(8,128)(2,1)S(1)}, u32[]{:S(2)}, u32[]{:S(2)}) %collective-permute-start.7) | collective-permute-done | bytes 98336 | tf_op jit(solution)/shard_map/ppermute | solution.py:272
  30.1 1.5 %collective-permute-start.13 = (bf16[24,2048]{1,0:T(8,128)(2,1)S(1)}, bf16[24,2048]{1,0:T(8,128)(2,1)S(1)}, u32[]{:S(2)}, u32[]{:S(2)}) collective-permute-start(bf16[24,2048]{1,0:T(8,128)(2,1)S(1)} %get-tuple-element.63.refs_3_), channel_id=1, source_target_pairs={{0,2},{1,3},{2,0},{3,1},{4,6},{5,7},{6,4},{7,5},{8,10},{9,11},{10,... | collective-permute-start | bytes 294920 | tf_op jit(solution)/shard_map/ppermute | solution.py:272
  32.1 1.5 %collective-permute-start.11 = (bf16[24,2048]{1,0:T(8,128)(2,1)S(1)}, bf16[24,2048]{1,0:T(8,128)(2,1)S(1)}, u32[]{:S(2)}, u32[]{:S(2)}) collective-permute-start(bf16[24,2048]{1,0:T(8,128)(2,1)S(1)} %collective-permute-done.8.refs_1_.refs_0_), channel_id=1, source_target_pairs={{0,2},{1,3},{2,0},{3,1},{4,6},{5,7},{6,4},{7,5},{8,10},{9,11},{10,... | collective-permute-start | bytes 294920 | tf_op jit(solution)/shard_map/ppermute | solution.py:272
  34.1 1.6 %copy-done.1 = bf16[1,1,4096,256]{3,2,1,0:T(8,128)(2,1)S(1)} copy-done((bf16[1,1,4096,256]{3,2,1,0:T(8,128)(2,1)S(1)}, bf16[1,1,4096,256]{3,2,1,0:T(8,128)(2,1)}, u32[]{:S(2)}) %copy-start.1) | copy-done | bytes 2097176
  35.7 2.7 %shard_map.124.refs_8_ = f32[4,192,256]{2,1,0:T(8,128)S(1)} custom-call(bf16[24,2048]{1,0:T(8,128)(2,1)S(1)} %collective-permute-done.2.refs_0_, bf16[24,2048]{1,0:T(8,128)(2,1)S(1)} %collective-permute-done.3.refs_1_, bf16[24,2048]{1,0:T(8,128)(2,1)S(1)} %collective-permute-done.refs_2_, bf16[24,2048]{1,0:T(8,128)(2,1)S(1)} %get-tuple-element.50.refs_0_.refs_3_, ...), custom_call_target="tpu_custom_call" | custom-call | bytes 9720000 | tf_op jit(solution)/shard_map/pallas_call | solution.py:19
  38.4 1.5 %collective-permute-done.11.refs_5_ = bf16[24,2048]{1,0:T(8,128)(2,1)S(1)} collective-permute-done((bf16[24,2048]{1,0:T(8,128)(2,1)S(1)}, bf16[24,2048]{1,0:T(8,128)(2,1)S(1)}, u32[]{:S(2)}, u32[]{:S(2)}) %collective-permute-start.11) | collective-permute-done | bytes 98336 | tf_op jit(solution)/shard_map/ppermute | solution.py:272
  40.0 1.1 collective-permute-done.12.refs_6_
  41.0 5.6 %shard_map.125 = (f32[48,2048]{1,0:T(8,128)S(1)}, f32[48,2048]{1,0:T(8,128)S(1)}, bf16[48,2048]{1,0:T(8,128)(2,1)S(1)}, bf16[48,2048]{1,0:T(8,128)(2,1)S(1)}) custom-call(bf16[24,2048]{1,0:T(8,128)(2,1)S(1)} %collective-permute-done.7.refs_0_, bf16[24,2048]{1,0:T(8,128)(2,1)S(1)} %collective-permute-done.8.refs_1_.refs_0_, ...), custom_call_target="tpu_custom_call" | custom-call | bytes 20520000 | tf_op jit(solution)/shard_map/pallas_call | solution.py:19
  46.7 1.2 %collective-permute-start.18 = (bf16[48,2048]{1,0:T(8,128)(2,1)S(1)}, bf16[48,2048]{1,0:T(8,128)(2,1)S(1)}, u32[]{:S(2)}, u32[]{:S(2)}) collective-permute-start(bf16[48,2048]{1,0:T(8,128)(2,1)S(1)} %get-tuple-element.70), channel_id=1, source_target_pairs={{0,2},{1,3},{2,0},{3,1},{4,6},{5,7},{6,4},{7,5},{8,10},{9,11},{10,... | collective-permute-start | bytes 589832 | tf_op jit(solution)/shard_map/ppermute | solution.py:272
  47.9 0.8 collective-permute-start.21
  48.7 1.5 %collective-permute-start.1 = (f32[16,128]{1,0:T(8,128)S(1)}, f32[16,128]{1,0:T(8,128)S(1)}, u32[]{:S(2)}, u32[]{:S(2)}) collective-permute-start(f32[16,128]{1,0:T(8,128)S(1)} %get-tuple-element.53), channel_id=1, source_target_pairs={{0,16},{16,0},{1,17},{17,1},{2,18},{18,2},{3,19},{19,3},{4,20},{20... | collective-permute-start | bytes 24584 | tf_op jit(solution)/shard_map/ppermute | solution.py:363
  50.2 2.2 %collective-permute-done.1.keys_ref.refs_1_ = f32[16,128]{1,0:T(8,128)S(1)} collective-permute-done((f32[16,128]{1,0:T(8,128)S(1)}, f32[16,128]{1,0:T(8,128)S(1)}, u32[]{:S(2)}, u32[]{:S(2)}) %collective-permute-start.1) | collective-permute-done | bytes 8224 | tf_op jit(solution)/shard_map/ppermute | solution.py:363
  53.7 3.8 %collective-permute-start.33 = (bf16[24,2048]{1,0:T(8,128)(2,1)S(1)}, bf16[24,2048]{1,0:T(8,128)(2,1)S(1)}, u32[]{:S(2)}, u32[]{:S(2)}) collective-permute-start(bf16[24,2048]{1,0:T(8,128)(2,1)S(1)} %get-tuple-element.85), channel_id=1, source_target_pairs={{0,12},{1,13},{2,14},{3,15},{4,8},{5,9},{6,10},{7,11},{8,4},{9,5},... | collective-permute-start | bytes 294920 | tf_op jit(solution)/shard_map/ppermute | solution.py:272
  57.6 2.0 %collective-permute-start.20 = (bf16[24,2048]{1,0:T(8,128)(2,1)S(1)}, bf16[24,2048]{1,0:T(8,128)(2,1)S(1)}, u32[]{:S(2)}, u32[]{:S(2)}) collective-permute-start(bf16[24,2048]{1,0:T(8,128)(2,1)S(1)} %get-tuple-element.72), channel_id=1, source_target_pairs={{0,12},{1,13},{2,14},{3,15},{4,8},{5,9},{6,10},{7,11},{8,4},{9,5},... | collective-permute-start | bytes 294920 | tf_op jit(solution)/shard_map/ppermute | solution.py:272
  59.7 1.5 %collective-permute-start.22 = (bf16[24,2048]{1,0:T(8,128)(2,1)S(1)}, bf16[24,2048]{1,0:T(8,128)(2,1)S(1)}, u32[]{:S(2)}, u32[]{:S(2)}) collective-permute-start(bf16[24,2048]{1,0:T(8,128)(2,1)S(1)} %get-tuple-element.75), channel_id=1, source_target_pairs={{0,4},{1,5},{2,6},{3,7},{4,0},{5,1},{6,2},{7,3},{8,12},{9,13},{10,... | collective-permute-start | bytes 294920 | tf_op jit(solution)/shard_map/ppermute | solution.py:272
  61.2 5.6 %collective-permute-done.32.refs_0_ = bf16[24,2048]{1,0:T(8,128)(2,1)S(1)} collective-permute-done((bf16[24,2048]{1,0:T(8,128)(2,1)S(1)}, bf16[24,2048]{1,0:T(8,128)(2,1)S(1)}, u32[]{:S(2)}, u32[]{:S(2)}) %collective-permute-start.32) | collective-permute-done | bytes 98336 | tf_op jit(solution)/shard_map/ppermute | solution.py:272
  66.8 0.9 collective-permute-start.34
  67.7 1.1 collective-permute-start.35
  68.8 1.3 %collective-permute-done.19.refs_0_ = bf16[24,2048]{1,0:T(8,128)(2,1)S(1)} collective-permute-done((bf16[24,2048]{1,0:T(8,128)(2,1)S(1)}, bf16[24,2048]{1,0:T(8,128)(2,1)S(1)}, u32[]{:S(2)}, u32[]{:S(2)}) %collective-permute-start.19) | collective-permute-done | bytes 98336 | tf_op jit(solution)/shard_map/ppermute | solution.py:272
  70.1 1.0 collective-permute-start.36
  71.2 1.8 %shard_map.128 = (bf16[1,128,4096]{2,1,0:T(8,128)(2,1)}, bf16[24,2048]{1,0:T(8,128)(2,1)S(1)}, bf16[24,2048]{1,0:T(8,128)(2,1)S(1)}, bf16[24,2048]{1,0:T(8,128)(2,1)S(1)}, bf16[24,2048]{1,0:T(8,128)(2,1)S(1)}) custom-call(s32[8,128]{1,0:T(8,128)S(1)} %bitcast.36, f32[16,128]{1,0:T(8,128)S(1)} %collective-permute-done.1.keys_ref.refs_1_, ...), custom_call_target="tpu_custom_call" | custom-call | bytes 6480000 | tf_op jit(solution)/shard_map/pallas_call | solution.py:19
  73.0 2.2 %collective-permute-start.23 = (bf16[24,2048]{1,0:T(8,128)(2,1)S(1)}, bf16[24,2048]{1,0:T(8,128)(2,1)S(1)}, u32[]{:S(2)}, u32[]{:S(2)}) collective-permute-start(bf16[24,2048]{1,0:T(8,128)(2,1)S(1)} %get-tuple-element.78), channel_id=1, source_target_pairs={{0,24},{1,25},{2,26},{3,27},{4,28},{5,29},{6,30},{7,31},{8,16},{9,... | collective-permute-start | bytes 294920 | tf_op jit(solution)/shard_map/ppermute | solution.py:386
  75.1 2.4 %collective-permute-start.24 = (bf16[24,2048]{1,0:T(8,128)(2,1)S(1)}, bf16[24,2048]{1,0:T(8,128)(2,1)S(1)}, u32[]{:S(2)}, u32[]{:S(2)}) collective-permute-start(bf16[24,2048]{1,0:T(8,128)(2,1)S(1)} %get-tuple-element.79), channel_id=1, source_target_pairs={{0,28},{1,29},{2,30},{3,31},{4,24},{5,25},{6,26},{7,27},{8,20},{9,... | collective-permute-start | bytes 294920 | tf_op jit(solution)/shard_map/ppermute | solution.py:386
  79.0 1.2 %collective-permute-start.37 = (bf16[24,2048]{1,0:T(8,128)(2,1)S(1)}, bf16[24,2048]{1,0:T(8,128)(2,1)S(1)}, u32[]{:S(2)}, u32[]{:S(2)}) collective-permute-start(bf16[24,2048]{1,0:T(8,128)(2,1)S(1)} %get-tuple-element.89.refs_3_), channel_id=1, source_target_pairs={{0,2},{1,3},{2,0},{3,1},{4,6},{5,7},{6,4},{7,5},{8,10},{9,11},{10,... | collective-permute-start | bytes 294920 | tf_op jit(solution)/shard_map/ppermute | solution.py:272
  80.5 1.0 collective-permute-start.27
  81.5 1.2 %collective-permute-done.24.refs_1_ = bf16[24,2048]{1,0:T(8,128)(2,1)S(1)} collective-permute-done((bf16[24,2048]{1,0:T(8,128)(2,1)S(1)}, bf16[24,2048]{1,0:T(8,128)(2,1)S(1)}, u32[]{:S(2)}, u32[]{:S(2)}) %collective-permute-start.24) | collective-permute-done | bytes 98336 | tf_op jit(solution)/shard_map/ppermute | solution.py:386
  82.7 1.1 collective-permute-start.28
  83.8 1.0 collective-permute-start.29
  84.8 1.0 collective-permute-start.30
  85.8 2.7 %shard_map.130.refs_8_ = f32[4,192,256]{2,1,0:T(8,128)S(1)} custom-call(bf16[24,2048]{1,0:T(8,128)(2,1)S(1)} %collective-permute-done.32.refs_0_, bf16[24,2048]{1,0:T(8,128)(2,1)S(1)} %collective-permute-done.33.refs_1_, bf16[24,2048]{1,0:T(8,128)(2,1)S(1)} %collective-permute-done.31.refs_2_, bf16[24,2048]{1,0:T(8,128)(2,1)S(1)} %get-tuple-element.89.refs_3_, ...), custom_call_target="tpu_custom_call" | custom-call | bytes 9720000 | tf_op jit(solution)/shard_map/pallas_call | solution.py:19
  88.9 1.1 collective-permute-done.30.refs_7_
  90.0 5.8 %shard_map.131 = (f32[48,2048]{1,0:T(8,128)S(1)}, f32[48,2048]{1,0:T(8,128)S(1)}, bf16[48,2048]{1,0:T(8,128)(2,1)S(1)}, bf16[48,2048]{1,0:T(8,128)(2,1)S(1)}) custom-call(bf16[24,2048]{1,0:T(8,128)(2,1)S(1)} %collective-permute-done.23.refs_0_, bf16[24,2048]{1,0:T(8,128)(2,1)S(1)} %collective-permute-done.24.refs_1_, ...), custom_call_target="tpu_custom_call" | custom-call | bytes 20520000 | tf_op jit(solution)/shard_map/pallas_call | solution.py:19
  95.8 1.2 %collective-permute-start.38 = (bf16[48,2048]{1,0:T(8,128)(2,1)S(1)}, bf16[48,2048]{1,0:T(8,128)(2,1)S(1)}, u32[]{:S(2)}, u32[]{:S(2)}) collective-permute-start(bf16[48,2048]{1,0:T(8,128)(2,1)S(1)} %get-tuple-element.91), channel_id=1, source_target_pairs={{0,2},{1,3},{2,0},{3,1},{4,6},{5,7},{6,4},{7,5},{8,10},{9,11},{10,... | collective-permute-start | bytes 589832 | tf_op jit(solution)/shard_map/ppermute | solution.py:272
  97.0 0.9 collective-permute-start.41
  97.9 4.2 %collective-permute-done.38.far_ref = bf16[48,2048]{1,0:T(8,128)(2,1)S(1)} collective-permute-done((bf16[48,2048]{1,0:T(8,128)(2,1)S(1)}, bf16[48,2048]{1,0:T(8,128)(2,1)S(1)}, u32[]{:S(2)}, u32[]{:S(2)}) %collective-permute-start.38) | collective-permute-done | bytes 196640 | tf_op jit(solution)/shard_map/ppermute | solution.py:272
  102.7 4.6 %collective-permute-start.40 = (bf16[24,2048]{1,0:T(8,128)(2,1)S(1)}, bf16[24,2048]{1,0:T(8,128)(2,1)S(1)}, u32[]{:S(2)}, u32[]{:S(2)}) collective-permute-start(bf16[24,2048]{1,0:T(8,128)(2,1)S(1)} %get-tuple-element.93), channel_id=1, source_target_pairs={{0,12},{1,13},{2,14},{3,15},{4,8},{5,9},{6,10},{7,11},{8,4},{9,5},... | collective-permute-start | bytes 294920 | tf_op jit(solution)/shard_map/ppermute | solution.py:272
  107.8 3.3 %collective-permute-done.40.refs_1_ = bf16[24,2048]{1,0:T(8,128)(2,1)S(1)} collective-permute-done((bf16[24,2048]{1,0:T(8,128)(2,1)S(1)}, bf16[24,2048]{1,0:T(8,128)(2,1)S(1)}, u32[]{:S(2)}, u32[]{:S(2)}) %collective-permute-start.40) | collective-permute-done | bytes 98336 | tf_op jit(solution)/shard_map/ppermute | solution.py:272
  111.1 1.0 collective-permute-done.42.refs_2_
  112.1 1.6 %shard_map.134 = bf16[1,128,4096]{2,1,0:T(8,128)(2,1)} custom-call(s32[8,128]{1,0:T(8,128)S(1)} %bitcast.39, bf16[24,2048]{1,0:T(8,128)(2,1)S(1)} %collective-permute-done.39.refs_0_, bf16[24,2048]{1,0:T(8,128)(2,1)S(1)} %collective-permute-done.40.refs_1_, bf16[24,2048]{1,0:T(8,128)(2,1)S(1)} %collective-permute-done.42.refs_2_, ...), custom_call_target="tpu_custom_call" | custom-call | bytes 3600000 | tf_op jit(solution)/shard_map/pallas_call | solution.py:19
  (77 shorter events, 13.0 us)
Async XLA Ops:
  0.6 33.5 %copy-start = (bf16[1,1,4096,256]{3,2,1,0:T(8,128)(2,1)S(1)}, bf16[1,1,4096,256]{3,2,1,0:T(8,128)(2,1)}, u32[]{:S(2)}) copy-start(bf16[1,1,4096,256]{3,2,1,0:T(8,128)(2,1)} %param.19) | copy-start | bytes 6291460
  0.6 20.7 %collective-permute-start.4 = (bf16[4096,256]{1,0:T(8,128)(2,1)}, bf16[4096,256]{1,0:T(8,128)(2,1)S(1)}, u32[]{:S(2)}, u32[]{:S(2)}) collective-permute-start(bf16[4096,256]{1,0:T(8,128)(2,1)} %bitcast.18), channel_id=1, source_target_pairs={{0,1},{1,0},{2,3},{3,2},{4,5},{5,4},{6,7},{7,6},{8,9},{9,8},{10,11... | collective-permute-start | bytes 6291464 | tf_op jit(solution)/shard_map/ppermute | solution.py:272
  1.2 20.2 %collective-permute-start.5 = (bf16[4096,256]{1,0:T(8,128)(2,1)}, bf16[4096,256]{1,0:T(8,128)(2,1)S(1)}, u32[]{:S(2)}, u32[]{:S(2)}) collective-permute-start(bf16[4096,256]{1,0:T(8,128)(2,1)} %bitcast.23), channel_id=1, source_target_pairs={{0,1},{1,0},{2,3},{3,2},{4,5},{5,4},{6,7},{7,6},{8,9},{9,8},{10,11... | collective-permute-start | bytes 6291464 | tf_op jit(solution)/shard_map/ppermute | solution.py:272
  1.2 20.1 %collective-permute-start.6 = (bf16[256,4096]{1,0:T(8,128)(2,1)}, bf16[256,4096]{1,0:T(8,128)(2,1)S(1)}, u32[]{:S(2)}, u32[]{:S(2)}) collective-permute-start(bf16[256,4096]{1,0:T(8,128)(2,1)} %bitcast.28), channel_id=1, source_target_pairs={{0,1},{1,0},{2,3},{3,2},{4,5},{5,4},{6,7},{7,6},{8,9},{9,8},{10,11... | collective-permute-start | bytes 6291464 | tf_op jit(solution)/shard_map/ppermute | solution.py:272
  4.2 6.1 %collective-permute-start = (bf16[24,2048]{1,0:T(8,128)(2,1)S(1)}, bf16[24,2048]{1,0:T(8,128)(2,1)S(1)}, u32[]{:S(2)}, u32[]{:S(2)}) collective-permute-start(bf16[24,2048]{1,0:T(8,128)(2,1)S(1)} %get-tuple-element.52), channel_id=1, source_target_pairs={{0,4},{1,5},{2,6},{3,7},{4,0},{5,1},{6,2},{7,3},{8,12},{9,13},{10,... | collective-permute-start | bytes 294920 | tf_op jit(solution)/shard_map/ppermute | solution.py:272
  6.9 8.3 %collective-permute-start.2 = (bf16[24,2048]{1,0:T(8,128)(2,1)S(1)}, bf16[24,2048]{1,0:T(8,128)(2,1)S(1)}, u32[]{:S(2)}, u32[]{:S(2)}) collective-permute-start(bf16[24,2048]{1,0:T(8,128)(2,1)S(1)} %get-tuple-element.54), channel_id=1, source_target_pairs={{0,8},{1,9},{2,10},{3,11},{4,12},{5,13},{6,14},{7,15},{8,0},{9,1},... | collective-permute-start | bytes 294920 | tf_op jit(solution)/shard_map/ppermute | solution.py:272
  10.3 10.4 %collective-permute-start.3 = (bf16[24,2048]{1,0:T(8,128)(2,1)S(1)}, bf16[24,2048]{1,0:T(8,128)(2,1)S(1)}, u32[]{:S(2)}, u32[]{:S(2)}) collective-permute-start(bf16[24,2048]{1,0:T(8,128)(2,1)S(1)} %get-tuple-element.55), channel_id=1, source_target_pairs={{0,12},{1,13},{2,14},{3,15},{4,8},{5,9},{6,10},{7,11},{8,4},{9,5},... | collective-permute-start | bytes 294920 | tf_op jit(solution)/shard_map/ppermute | solution.py:272
  15.2 9.7 %collective-permute-start.17 = (bf16[24,2048]{1,0:T(8,128)(2,1)S(1)}, bf16[24,2048]{1,0:T(8,128)(2,1)S(1)}, u32[]{:S(2)}, u32[]{:S(2)}) collective-permute-start(bf16[24,2048]{1,0:T(8,128)(2,1)S(1)} %get-tuple-element.50.refs_0_.refs_3_), channel_id=1, source_target_pairs={{0,2},{1,3},{2,0},{3,1},{4,6},{5,7},{6,4},{7,5},{8,10},{9,11},{10,... | collective-permute-start | bytes 294920 | tf_op jit(solution)/shard_map/ppermute | solution.py:272
  20.7 5.7 %collective-permute-start.16 = (bf16[24,2048]{1,0:T(8,128)(2,1)S(1)}, bf16[24,2048]{1,0:T(8,128)(2,1)S(1)}, u32[]{:S(2)}, u32[]{:S(2)}) collective-permute-start(bf16[24,2048]{1,0:T(8,128)(2,1)S(1)} %collective-permute-done.refs_2_), channel_id=1, source_target_pairs={{0,2},{1,3},{2,0},{3,1},{4,6},{5,7},{6,4},{7,5},{8,10},{9,11},{10,... | collective-permute-start | bytes 294920 | tf_op jit(solution)/shard_map/ppermute | solution.py:272
  21.3 8.8 %collective-permute-start.7 = (bf16[24,2048]{1,0:T(8,128)(2,1)S(1)}, bf16[24,2048]{1,0:T(8,128)(2,1)S(1)}, u32[]{:S(2)}, u32[]{:S(2)}) collective-permute-start(bf16[24,2048]{1,0:T(8,128)(2,1)S(1)} %get-tuple-element.60), channel_id=1, source_target_pairs={{0,8},{1,9},{2,10},{3,11},{4,12},{5,13},{6,14},{7,15},{8,0},{9,1},... | collective-permute-start | bytes 294920 | tf_op jit(solution)/shard_map/ppermute | solution.py:272
  21.6 10.0 %collective-permute-start.8 = (bf16[24,2048]{1,0:T(8,128)(2,1)S(1)}, bf16[24,2048]{1,0:T(8,128)(2,1)S(1)}, u32[]{:S(2)}, u32[]{:S(2)}) collective-permute-start(bf16[24,2048]{1,0:T(8,128)(2,1)S(1)} %get-tuple-element.61), channel_id=1, source_target_pairs={{0,12},{1,13},{2,14},{3,15},{4,8},{5,9},{6,10},{7,11},{8,4},{9,5},... | collective-permute-start | bytes 294920 | tf_op jit(solution)/shard_map/ppermute | solution.py:272
  24.4 7.7 %collective-permute-start.9 = (bf16[24,2048]{1,0:T(8,128)(2,1)S(1)}, bf16[24,2048]{1,0:T(8,128)(2,1)S(1)}, u32[]{:S(2)}, u32[]{:S(2)}) collective-permute-start(bf16[24,2048]{1,0:T(8,128)(2,1)S(1)} %get-tuple-element.62), channel_id=1, source_target_pairs={{0,4},{1,5},{2,6},{3,7},{4,0},{5,1},{6,2},{7,3},{8,12},{9,13},{10,... | collective-permute-start | bytes 294920 | tf_op jit(solution)/shard_map/ppermute | solution.py:272
  24.9 8.7 %collective-permute-start.14 = (bf16[24,2048]{1,0:T(8,128)(2,1)S(1)}, bf16[24,2048]{1,0:T(8,128)(2,1)S(1)}, u32[]{:S(2)}, u32[]{:S(2)}) collective-permute-start(bf16[24,2048]{1,0:T(8,128)(2,1)S(1)} %collective-permute-done.2.refs_0_), channel_id=1, source_target_pairs={{0,2},{1,3},{2,0},{3,1},{4,6},{5,7},{6,4},{7,5},{8,10},{9,11},{10,... | collective-permute-start | bytes 294920 | tf_op jit(solution)/shard_map/ppermute | solution.py:272
  26.4 7.8 %collective-permute-start.15 = (bf16[24,2048]{1,0:T(8,128)(2,1)S(1)}, bf16[24,2048]{1,0:T(8,128)(2,1)S(1)}, u32[]{:S(2)}, u32[]{:S(2)}) collective-permute-start(bf16[24,2048]{1,0:T(8,128)(2,1)S(1)} %collective-permute-done.3.refs_1_), channel_id=1, source_target_pairs={{0,2},{1,3},{2,0},{3,1},{4,6},{5,7},{6,4},{7,5},{8,10},{9,11},{10,... | collective-permute-start | bytes 294920 | tf_op jit(solution)/shard_map/ppermute | solution.py:272
  30.1 8.4 %collective-permute-start.13 = (bf16[24,2048]{1,0:T(8,128)(2,1)S(1)}, bf16[24,2048]{1,0:T(8,128)(2,1)S(1)}, u32[]{:S(2)}, u32[]{:S(2)}) collective-permute-start(bf16[24,2048]{1,0:T(8,128)(2,1)S(1)} %get-tuple-element.63.refs_3_), channel_id=1, source_target_pairs={{0,2},{1,3},{2,0},{3,1},{4,6},{5,7},{6,4},{7,5},{8,10},{9,11},{10,... | collective-permute-start | bytes 294920 | tf_op jit(solution)/shard_map/ppermute | solution.py:272
  31.5 6.9 %collective-permute-start.10 = (bf16[24,2048]{1,0:T(8,128)(2,1)S(1)}, bf16[24,2048]{1,0:T(8,128)(2,1)S(1)}, u32[]{:S(2)}, u32[]{:S(2)}) collective-permute-start(bf16[24,2048]{1,0:T(8,128)(2,1)S(1)} %collective-permute-done.7.refs_0_), channel_id=1, source_target_pairs={{0,2},{1,3},{2,0},{3,1},{4,6},{5,7},{6,4},{7,5},{8,10},{9,11},{10,... | collective-permute-start | bytes 294920 | tf_op jit(solution)/shard_map/ppermute | solution.py:272
  32.1 7.9 %collective-permute-start.11 = (bf16[24,2048]{1,0:T(8,128)(2,1)S(1)}, bf16[24,2048]{1,0:T(8,128)(2,1)S(1)}, u32[]{:S(2)}, u32[]{:S(2)}) collective-permute-start(bf16[24,2048]{1,0:T(8,128)(2,1)S(1)} %collective-permute-done.8.refs_1_.refs_0_), channel_id=1, source_target_pairs={{0,2},{1,3},{2,0},{3,1},{4,6},{5,7},{6,4},{7,5},{8,10},{9,11},{10,... | collective-permute-start | bytes 294920 | tf_op jit(solution)/shard_map/ppermute | solution.py:272
  33.6 7.4 %collective-permute-start.12 = (bf16[24,2048]{1,0:T(8,128)(2,1)S(1)}, bf16[24,2048]{1,0:T(8,128)(2,1)S(1)}, u32[]{:S(2)}, u32[]{:S(2)}) collective-permute-start(bf16[24,2048]{1,0:T(8,128)(2,1)S(1)} %collective-permute-done.9.refs_2_), channel_id=1, source_target_pairs={{0,2},{1,3},{2,0},{3,1},{4,6},{5,7},{6,4},{7,5},{8,10},{9,11},{10,... | collective-permute-start | bytes 294920 | tf_op jit(solution)/shard_map/ppermute | solution.py:272
  38.4 14.0 %copy-start.5 = (bf16[1,128,4096]{2,1,0:T(8,128)(2,1)S(1)}, bf16[1,128,4096]{2,1,0:T(8,128)(2,1)}, u32[]{:S(2)}) copy-start(bf16[1,128,4096]{2,1,0:T(8,128)(2,1)} %param.13) | copy-start | bytes 3145732
  38.4 14.0 %copy-start.10 = (s32[1,128,8]{1,2,0:T(8,128)S(1)}, s32[1,128,8]{1,2,0:T(8,128)}, u32[]{:S(2)}) copy-start(s32[1,128,8]{1,2,0:T(8,128)} %param.17) | copy-start | bytes 12292
  46.6 24.5 %copy-start.6 = (bf16[128,4096]{1,0:T(8,128)(2,1)S(1)}, bf16[128,4096]{1,0:T(8,128)(2,1)}, u32[]{:S(2)}) copy-start(bf16[128,4096]{1,0:T(8,128)(2,1)} %grad_last_ref.1) | copy-start | bytes 3145732
  46.6 24.5 %copy-start.8 = (s32[1,128,8]{1,2,0:T(8,128)S(1)}, s32[1,128,8]{1,2,0:T(8,128)}, u32[]{:S(2)}) copy-start(s32[1,128,8]{1,2,0:T(8,128)} %param.15) | copy-start | bytes 12292
  46.7 10.8 %collective-permute-start.18 = (bf16[48,2048]{1,0:T(8,128)(2,1)S(1)}, bf16[48,2048]{1,0:T(8,128)(2,1)S(1)}, u32[]{:S(2)}, u32[]{:S(2)}) collective-permute-start(bf16[48,2048]{1,0:T(8,128)(2,1)S(1)} %get-tuple-element.70), channel_id=1, source_target_pairs={{0,2},{1,3},{2,0},{3,1},{4,6},{5,7},{6,4},{7,5},{8,10},{9,11},{10,... | collective-permute-start | bytes 589832 | tf_op jit(solution)/shard_map/ppermute | solution.py:272
  47.9 9.7 %collective-permute-start.21 = (bf16[48,2048]{1,0:T(8,128)(2,1)S(1)}, bf16[48,2048]{1,0:T(8,128)(2,1)S(1)}, u32[]{:S(2)}, u32[]{:S(2)}) collective-permute-start(bf16[48,2048]{1,0:T(8,128)(2,1)S(1)} %get-tuple-element.74), channel_id=1, source_target_pairs={{0,2},{1,3},{2,0},{3,1},{4,6},{5,7},{6,4},{7,5},{8,10},{9,11},{10,... | collective-permute-start | bytes 589832 | tf_op jit(solution)/shard_map/ppermute | solution.py:272
  48.7 3.7 %collective-permute-start.1 = (f32[16,128]{1,0:T(8,128)S(1)}, f32[16,128]{1,0:T(8,128)S(1)}, u32[]{:S(2)}, u32[]{:S(2)}) collective-permute-start(f32[16,128]{1,0:T(8,128)S(1)} %get-tuple-element.53), channel_id=1, source_target_pairs={{0,16},{16,0},{1,17},{17,1},{2,18},{18,2},{3,19},{19,3},{4,20},{20... | collective-permute-start | bytes 24584 | tf_op jit(solution)/shard_map/ppermute | solution.py:363
  53.0 6.6 %collective-permute-start.31 = (bf16[24,2048]{1,0:T(8,128)(2,1)S(1)}, bf16[24,2048]{1,0:T(8,128)(2,1)S(1)}, u32[]{:S(2)}, u32[]{:S(2)}) collective-permute-start(bf16[24,2048]{1,0:T(8,128)(2,1)S(1)} %get-tuple-element.83), channel_id=1, source_target_pairs={{0,4},{1,5},{2,6},{3,7},{4,0},{5,1},{6,2},{7,3},{8,12},{9,13},{10,... | collective-permute-start | bytes 294920 | tf_op jit(solution)/shard_map/ppermute | solution.py:272
  53.7 13.1 %collective-permute-start.32 = (bf16[24,2048]{1,0:T(8,128)(2,1)S(1)}, bf16[24,2048]{1,0:T(8,128)(2,1)S(1)}, u32[]{:S(2)}, u32[]{:S(2)}) collective-permute-start(bf16[24,2048]{1,0:T(8,128)(2,1)S(1)} %get-tuple-element.84), channel_id=1, source_target_pairs={{0,8},{1,9},{2,10},{3,11},{4,12},{5,13},{6,14},{7,15},{8,0},{9,1},... | collective-permute-start | bytes 294920 | tf_op jit(solution)/shard_map/ppermute | solution.py:272
  53.7 13.1 %collective-permute-start.33 = (bf16[24,2048]{1,0:T(8,128)(2,1)S(1)}, bf16[24,2048]{1,0:T(8,128)(2,1)S(1)}, u32[]{:S(2)}, u32[]{:S(2)}) collective-permute-start(bf16[24,2048]{1,0:T(8,128)(2,1)S(1)} %get-tuple-element.85), channel_id=1, source_target_pairs={{0,12},{1,13},{2,14},{3,15},{4,8},{5,9},{6,10},{7,11},{8,4},{9,5},... | collective-permute-start | bytes 294920 | tf_op jit(solution)/shard_map/ppermute | solution.py:272
  57.5 12.6 %collective-permute-start.19 = (bf16[24,2048]{1,0:T(8,128)(2,1)S(1)}, bf16[24,2048]{1,0:T(8,128)(2,1)S(1)}, u32[]{:S(2)}, u32[]{:S(2)}) collective-permute-start(bf16[24,2048]{1,0:T(8,128)(2,1)S(1)} %get-tuple-element.71), channel_id=1, source_target_pairs={{0,8},{1,9},{2,10},{3,11},{4,12},{5,13},{6,14},{7,15},{8,0},{9,1},... | collective-permute-start | bytes 294920 | tf_op jit(solution)/shard_map/ppermute | solution.py:272
  57.6 13.5 %collective-permute-start.20 = (bf16[24,2048]{1,0:T(8,128)(2,1)S(1)}, bf16[24,2048]{1,0:T(8,128)(2,1)S(1)}, u32[]{:S(2)}, u32[]{:S(2)}) collective-permute-start(bf16[24,2048]{1,0:T(8,128)(2,1)S(1)} %get-tuple-element.72), channel_id=1, source_target_pairs={{0,12},{1,13},{2,14},{3,15},{4,8},{5,9},{6,10},{7,11},{8,4},{9,5},... | collective-permute-start | bytes 294920 | tf_op jit(solution)/shard_map/ppermute | solution.py:272
  59.7 11.5 %collective-permute-start.22 = (bf16[24,2048]{1,0:T(8,128)(2,1)S(1)}, bf16[24,2048]{1,0:T(8,128)(2,1)S(1)}, u32[]{:S(2)}, u32[]{:S(2)}) collective-permute-start(bf16[24,2048]{1,0:T(8,128)(2,1)S(1)} %get-tuple-element.75), channel_id=1, source_target_pairs={{0,4},{1,5},{2,6},{3,7},{4,0},{5,1},{6,2},{7,3},{8,12},{9,13},{10,... | collective-permute-start | bytes 294920 | tf_op jit(solution)/shard_map/ppermute | solution.py:272
  66.8 10.7 %collective-permute-start.34 = (bf16[24,2048]{1,0:T(8,128)(2,1)S(1)}, bf16[24,2048]{1,0:T(8,128)(2,1)S(1)}, u32[]{:S(2)}, u32[]{:S(2)}) collective-permute-start(bf16[24,2048]{1,0:T(8,128)(2,1)S(1)} %collective-permute-done.32.refs_0_), channel_id=1, source_target_pairs={{0,2},{1,3},{2,0},{3,1},{4,6},{5,7},{6,4},{7,5},{8,10},{9,11},{10,... | collective-permute-start | bytes 294920 | tf_op jit(solution)/shard_map/ppermute | solution.py:272
  67.7 10.6 %collective-permute-start.35 = (bf16[24,2048]{1,0:T(8,128)(2,1)S(1)}, bf16[24,2048]{1,0:T(8,128)(2,1)S(1)}, u32[]{:S(2)}, u32[]{:S(2)}) collective-permute-start(bf16[24,2048]{1,0:T(8,128)(2,1)S(1)} %collective-permute-done.33.refs_1_), channel_id=1, source_target_pairs={{0,2},{1,3},{2,0},{3,1},{4,6},{5,7},{6,4},{7,5},{8,10},{9,11},{10,... | collective-permute-start | bytes 294920 | tf_op jit(solution)/shard_map/ppermute | solution.py:272
  70.1 8.9 %collective-permute-start.36 = (bf16[24,2048]{1,0:T(8,128)(2,1)S(1)}, bf16[24,2048]{1,0:T(8,128)(2,1)S(1)}, u32[]{:S(2)}, u32[]{:S(2)}) collective-permute-start(bf16[24,2048]{1,0:T(8,128)(2,1)S(1)} %collective-permute-done.31.refs_2_), channel_id=1, source_target_pairs={{0,2},{1,3},{2,0},{3,1},{4,6},{5,7},{6,4},{7,5},{8,10},{9,11},{10,... | collective-permute-start | bytes 294920 | tf_op jit(solution)/shard_map/ppermute | solution.py:272
  73.0 7.5 %collective-permute-start.23 = (bf16[24,2048]{1,0:T(8,128)(2,1)S(1)}, bf16[24,2048]{1,0:T(8,128)(2,1)S(1)}, u32[]{:S(2)}, u32[]{:S(2)}) collective-permute-start(bf16[24,2048]{1,0:T(8,128)(2,1)S(1)} %get-tuple-element.78), channel_id=1, source_target_pairs={{0,24},{1,25},{2,26},{3,27},{4,28},{5,29},{6,30},{7,31},{8,16},{9,... | collective-permute-start | bytes 294920 | tf_op jit(solution)/shard_map/ppermute | solution.py:386
  75.1 7.6 %collective-permute-start.24 = (bf16[24,2048]{1,0:T(8,128)(2,1)S(1)}, bf16[24,2048]{1,0:T(8,128)(2,1)S(1)}, u32[]{:S(2)}, u32[]{:S(2)}) collective-permute-start(bf16[24,2048]{1,0:T(8,128)(2,1)S(1)} %get-tuple-element.79), channel_id=1, source_target_pairs={{0,28},{1,29},{2,30},{3,31},{4,24},{5,25},{6,26},{7,27},{8,20},{9,... | collective-permute-start | bytes 294920 | tf_op jit(solution)/shard_map/ppermute | solution.py:386
  77.5 6.3 %collective-permute-start.25 = (bf16[24,2048]{1,0:T(8,128)(2,1)S(1)}, bf16[24,2048]{1,0:T(8,128)(2,1)S(1)}, u32[]{:S(2)}, u32[]{:S(2)}) collective-permute-start(bf16[24,2048]{1,0:T(8,128)(2,1)S(1)} %get-tuple-element.80), channel_id=1, source_target_pairs={{0,20},{1,21},{2,22},{3,23},{4,16},{5,17},{6,18},{7,19},{8,28},{9,... | collective-permute-start | bytes 294920 | tf_op jit(solution)/shard_map/ppermute | solution.py:386
  78.3 6.5 %collective-permute-start.26 = (bf16[24,2048]{1,0:T(8,128)(2,1)S(1)}, bf16[24,2048]{1,0:T(8,128)(2,1)S(1)}, u32[]{:S(2)}, u32[]{:S(2)}) collective-permute-start(bf16[24,2048]{1,0:T(8,128)(2,1)S(1)} %get-tuple-element.81), channel_id=1, source_target_pairs={{0,16},{1,17},{2,18},{3,19},{4,20},{5,21},{6,22},{7,23},{8,24},{9,... | collective-permute-start | bytes 294920 | tf_op jit(solution)/shard_map/ppermute | solution.py:386
  79.0 6.8 %collective-permute-start.37 = (bf16[24,2048]{1,0:T(8,128)(2,1)S(1)}, bf16[24,2048]{1,0:T(8,128)(2,1)S(1)}, u32[]{:S(2)}, u32[]{:S(2)}) collective-permute-start(bf16[24,2048]{1,0:T(8,128)(2,1)S(1)} %get-tuple-element.89.refs_3_), channel_id=1, source_target_pairs={{0,2},{1,3},{2,0},{3,1},{4,6},{5,7},{6,4},{7,5},{8,10},{9,11},{10,... | collective-permute-start | bytes 294920 | tf_op jit(solution)/shard_map/ppermute | solution.py:272
  80.5 8.0 %collective-permute-start.27 = (bf16[24,2048]{1,0:T(8,128)(2,1)S(1)}, bf16[24,2048]{1,0:T(8,128)(2,1)S(1)}, u32[]{:S(2)}, u32[]{:S(2)}) collective-permute-start(bf16[24,2048]{1,0:T(8,128)(2,1)S(1)} %collective-permute-done.23.refs_0_), channel_id=1, source_target_pairs={{0,2},{1,3},{2,0},{3,1},{4,6},{5,7},{6,4},{7,5},{8,10},{9,11},{10,... | collective-permute-start | bytes 294920 | tf_op jit(solution)/shard_map/ppermute | solution.py:272
  82.7 5.8 %collective-permute-start.28 = (bf16[24,2048]{1,0:T(8,128)(2,1)S(1)}, bf16[24,2048]{1,0:T(8,128)(2,1)S(1)}, u32[]{:S(2)}, u32[]{:S(2)}) collective-permute-start(bf16[24,2048]{1,0:T(8,128)(2,1)S(1)} %collective-permute-done.24.refs_1_), channel_id=1, source_target_pairs={{0,2},{1,3},{2,0},{3,1},{4,6},{5,7},{6,4},{7,5},{8,10},{9,11},{10,... | collective-permute-start | bytes 294920 | tf_op jit(solution)/shard_map/ppermute | solution.py:272
  83.8 5.1 %collective-permute-start.29 = (bf16[24,2048]{1,0:T(8,128)(2,1)S(1)}, bf16[24,2048]{1,0:T(8,128)(2,1)S(1)}, u32[]{:S(2)}, u32[]{:S(2)}) collective-permute-start(bf16[24,2048]{1,0:T(8,128)(2,1)S(1)} %collective-permute-done.25.refs_2_), channel_id=1, source_target_pairs={{0,2},{1,3},{2,0},{3,1},{4,6},{5,7},{6,4},{7,5},{8,10},{9,11},{10,... | collective-permute-start | bytes 294920 | tf_op jit(solution)/shard_map/ppermute | solution.py:272
  84.8 5.2 %collective-permute-start.30 = (bf16[24,2048]{1,0:T(8,128)(2,1)S(1)}, bf16[24,2048]{1,0:T(8,128)(2,1)S(1)}, u32[]{:S(2)}, u32[]{:S(2)}) collective-permute-start(bf16[24,2048]{1,0:T(8,128)(2,1)S(1)} %collective-permute-done.26.refs_3_), channel_id=1, source_target_pairs={{0,2},{1,3},{2,0},{3,1},{4,6},{5,7},{6,4},{7,5},{8,10},{9,11},{10,... | collective-permute-start | bytes 294920 | tf_op jit(solution)/shard_map/ppermute | solution.py:272
  95.8 6.3 %collective-permute-start.38 = (bf16[48,2048]{1,0:T(8,128)(2,1)S(1)}, bf16[48,2048]{1,0:T(8,128)(2,1)S(1)}, u32[]{:S(2)}, u32[]{:S(2)}) collective-permute-start(bf16[48,2048]{1,0:T(8,128)(2,1)S(1)} %get-tuple-element.91), channel_id=1, source_target_pairs={{0,2},{1,3},{2,0},{3,1},{4,6},{5,7},{6,4},{7,5},{8,10},{9,11},{10,... | collective-permute-start | bytes 589832 | tf_op jit(solution)/shard_map/ppermute | solution.py:272
  97.0 10.3 %collective-permute-start.41 = (bf16[48,2048]{1,0:T(8,128)(2,1)S(1)}, bf16[48,2048]{1,0:T(8,128)(2,1)S(1)}, u32[]{:S(2)}, u32[]{:S(2)}) collective-permute-start(bf16[48,2048]{1,0:T(8,128)(2,1)S(1)} %get-tuple-element.95), channel_id=1, source_target_pairs={{0,2},{1,3},{2,0},{3,1},{4,6},{5,7},{6,4},{7,5},{8,10},{9,11},{10,... | collective-permute-start | bytes 589832 | tf_op jit(solution)/shard_map/ppermute | solution.py:272
  102.1 5.7 %collective-permute-start.39 = (bf16[24,2048]{1,0:T(8,128)(2,1)S(1)}, bf16[24,2048]{1,0:T(8,128)(2,1)S(1)}, u32[]{:S(2)}, u32[]{:S(2)}) collective-permute-start(bf16[24,2048]{1,0:T(8,128)(2,1)S(1)} %get-tuple-element.92), channel_id=1, source_target_pairs={{0,8},{1,9},{2,10},{3,11},{4,12},{5,13},{6,14},{7,15},{8,0},{9,1},... | collective-permute-start | bytes 294920 | tf_op jit(solution)/shard_map/ppermute | solution.py:272
  102.7 8.3 %collective-permute-start.40 = (bf16[24,2048]{1,0:T(8,128)(2,1)S(1)}, bf16[24,2048]{1,0:T(8,128)(2,1)S(1)}, u32[]{:S(2)}, u32[]{:S(2)}) collective-permute-start(bf16[24,2048]{1,0:T(8,128)(2,1)S(1)} %get-tuple-element.93), channel_id=1, source_target_pairs={{0,12},{1,13},{2,14},{3,15},{4,8},{5,9},{6,10},{7,11},{8,4},{9,5},... | collective-permute-start | bytes 294920 | tf_op jit(solution)/shard_map/ppermute | solution.py:272
  107.4 4.8 %collective-permute-start.42 = (bf16[24,2048]{1,0:T(8,128)(2,1)S(1)}, bf16[24,2048]{1,0:T(8,128)(2,1)S(1)}, u32[]{:S(2)}, u32[]{:S(2)}) collective-permute-start(bf16[24,2048]{1,0:T(8,128)(2,1)S(1)} %get-tuple-element.96), channel_id=1, source_target_pairs={{0,4},{1,5},{2,6},{3,7},{4,0},{5,1},{6,2},{7,3},{8,12},{9,13},{10,... | collective-permute-start | bytes 294920 | tf_op jit(solution)/shard_map/ppermute | solution.py:272
  (8 other events, 12.1 us)

commit v3 on v2

--- a/solution.py
+++ b/solution.py
@@ -99,19 +99,25 @@
         out_refs[k][...] = picked[2 * cap * k : 2 * cap * (k + 1)].astype(BF16)
 
 
-def pack_grad(window, cap, ids_ref, probs_ref, ids_on_ref, probs_on_ref, grad_ref, *refs):
-    keys_ref, *out_refs = refs[-3 - window : -2]
-    grad_buf, sems = refs[-2:]
+def pack_rest(window, cap, ids_ref, probs_ref, ids_on_ref, probs_on_ref, grad_ref, x_ref, *refs):
+    out_refs, (grad_buf, x_buf, sems) = refs[-4 - 2 * window : -3], refs[-3:]
+    keys_ref, out_refs = out_refs[0], out_refs[1:]
+    copies = fetch(row_parts(grad_ref, grad_buf) + row_parts(x_ref, x_buf), sems)
     topk = ids_on_ref.shape[0]
     keys_ref[:topk] = ids_on_ref[...].astype(F32)
     keys_ref[topk:] = probs_on_ref[...]
-    copies = fetch(row_parts(grad_ref, grad_buf), sems)
     top, bot, coef = tables(ids_ref[...], window, cap, probs_ref[...])
-    for c in copies:
+    top_on, bot_on, _ = tables(ids_on_ref[...], window, cap)
+    for c in copies[:4]:
         c.wait()
     picked = gathered(top, bot, grad_buf[...]) * coef
     for k in range(window):
         out_refs[k][...] = picked[2 * cap * k : 2 * cap * (k + 1)].astype(BF16)
+    for c in copies[4:]:
+        c.wait()
+    picked = gathered(top_on, bot_on, x_buf[...])
+    for k in range(window):
+        out_refs[window + k][...] = picked[2 * cap * k : 2 * cap * (k + 1)].astype(BF16)
 
 
 def scattered(ids_ref, window, cap, blocks):
@@ -212,8 +218,8 @@
     ins, weights, out_ref, bufs, sems = (
         refs[:blocks],
         refs[blocks : blocks + 4],
-        refs[blocks + 4],
-        refs[blocks + 5 : -1],
+        refs[-6],
+        refs[-5:-1],
         refs[-1],
     )
     copies = fetch(list(zip(weights, bufs)), sems)
@@ -280,8 +286,7 @@
     own_w = (w_gate[0, 0], w_up[0, 0], w_down[0, 0])
     msg = shape((2 * cap, half), BF16)
     pair = shape((2, 2 * cap, half), BF16)
-    weights = own_w + tuple(send(w, 1) for w in own_w)
-    bufs = [pltpu.VMEM(w.shape, BF16) for w in weights]
+    bufs = [pltpu.VMEM(w.shape, BF16) for w in own_w * 2]
     dma = pltpu.SemaphoreType.DMA
     row_buf = pltpu.VMEM((tok, width), BF16)
     order = sequence(window)
@@ -296,25 +301,13 @@
     def listed(by_k):
         return [by_k[k] for k in order]
 
-    def pack(ids, x, extra=()):
-        made = call(
-            functools.partial(pack_x, window, cap),
-            [msg] * window,
-            (ids, x, *extra),
-            PACK_MIB if not extra else 16,
-            away=range(1, 2 + len(extra)),
-            scratch=[row_buf, dma((4,))],
-            us=3.0,
-        )
-        return dict(zip(order, made))
-
-    def forward(near, far):
+    def forward(near, far, *extra):
         return call(
             functools.partial(unit_x, 2 * window, cap),
             shape((4, 2 * rows, w_gate.shape[3]), F32),
-            (*listed(near), *listed(far), weights[0], weights[1], weights[3], weights[4]),
+            (*listed(near), *listed(far), weights[0], weights[1], weights[3], weights[4], *extra),
             COMPUTE_MIB,
-            away=range(2 * window, 2 * window + 4),
+            away=range(2 * window, 2 * window + 4 + len(extra)),
             scratch=[bufs[0], bufs[1], bufs[3], bufs[4], dma((4,))],
             us=2.7,
         )
@@ -339,29 +332,42 @@
             back.update({k: plane(sums[j], k) for j, k in enumerate(group)})
         return far, listed(back)
 
-    x_1 = pack(ids_1, x_first[0])
-    keys, *grad_1 = call(
-        functools.partial(pack_grad, window, cap),
-        [shape((2 * topk, tok), F32)] + [msg] * window,
-        (ids_1, probs_1, ids_2, probs_2, grad_first[0], x_1[0]),
-        PACK_MIB,
-        away=(4, 5),
+    x_1 = call(
+        functools.partial(pack_x, window, cap),
+        [msg] * window,
+        (ids_1, x_first[0]),
+        44,
+        away=(1,),
         scratch=[row_buf, dma((4,))],
         us=3.0,
     )
-    grad_1 = dict(zip(order, grad_1))
+    keys, *packed = call(
+        functools.partial(pack_rest, window, cap),
+        [shape((2 * topk, tok), F32)] + [msg] * (2 * window),
+        (ids_1, probs_1, ids_2, probs_2, grad_first[0], x_second[0], x_1[0]),
+        56,
+        away=(4, 5, 6),
+        scratch=[row_buf, row_buf, dma((8,))],
+        us=5.0,
+    )
+    x_1 = dict(zip(order, x_1))
+    grad_1 = dict(zip(order, packed))
+    x_2 = dict(zip(order, packed[window:]))
     outer = [k for k in order if k > 1]
     near_x = {k: plane(x_1[k], k) for k in outer}
-    near_x, grad_1, *peer_w = after((near_x, grad_1, *weights[3:]))
-    weights = own_w + tuple(peer_w)
+    peer_w = [send(w, 1) for w in own_w]
+    grad_1, peer_w = after((grad_1, peer_w))
+    weights = (*own_w, *peer_w)
     near_g = {k: plane(grad_1[k], k) for k in outer}
-    for k in (1, 0):
-        near_x[k] = plane(x_1[k], k)
-        near_g[k] = plane(grad_1[k], k)
+    inner = [(x_1[k], grad_1[k]) for k in (1, 0)]
+    near_x, inner, keys = after((near_x, inner, keys))
+    for k, (x, grad) in zip((1, 0), inner):
+        near_x[k] = plane(x, k)
+        near_g[k] = plane(grad, k)
     far_x = {k: across(near_x[k]) for k in (0, 1, *outer)}
+    keys = lax.ppermute(keys, "pipe", ring)
+    x_2 = after((near_g, x_2))[1]
     far_g = {k: across(near_g[k]) for k in (0, 1, *outer)}
-    keys = lax.ppermute(after((keys, near_x[1]))[0], "pipe", ring)
-    x_2 = pack(ids_2, x_second[0], (near_g[outer[-1]], keys))
     near_x2 = {k: plane(x_2[k], k) for k in order}
     arrived, back = backward(near_g, far_g, forward(near_x, far_x))
     near_x2 = after((near_x2, arrived))[0]

time: 114 us -> 108 us (0.947)
  starting transfers between devices: 56.4 us -> 51.4 us
  local copies, waits for them, and re-layouts: 6.82 us -> 3.56 us
  Pallas kernels: 22.2 us -> 24.3 us
    ppermute x38, starting transfers between devices: 48.8 us -> 44.1 us  [send(): return lax.ppermute(x, 'expert', [(i, i ^ bits) for i in range(devices)])]
    unnamed x26 -> x30, local copies, waits for them, and re-layouts: 6.82 us -> 3.56 us
    pallas_call x13 -> x12, Pallas kernels: 22.2 us -> 24.3 us  [call(): pl.pallas_call(body, out_shape=outs, in_specs=[pl.BlockSpec(memory_space=...]
    ppermute x1, waiting for transfers between devices: 2.15 us -> 0.01 us  [body(): keys = lax.ppermute(keys, 'pipe', ring)]
    ppermute x38, waiting for transfers between devices: 23.8 us -> 25.3 us  [send(): return lax.ppermute(x, 'expert', [(i, i ^ bits) for i in range(devices)])]
  transfers between devices with their start and end apart: 43 -> 43, of which waited for: 15 -> 16; matrix products, arithmetic and copies ran while one was open for 0% -> 0% of each run, Pallas kernels for 8% -> 11%
where the time goes in v3:
time: 108 us
  starting transfers between devices  51.4 us (48%)
  waiting for transfers between devices  27.7 us (26%)
  Pallas kernels  24.3 us (22%)
  local copies, waits for them, and re-layouts  3.56 us (3%)
    ppermute x38, starting transfers between devices, send(): return lax.ppermute(x, 'expert', [(i, i ^ bits) for i in range(devices)])  44.1 us
    ppermute x38, waiting for transfers between devices, send(): return lax.ppermute(x, 'expert', [(i, i ^ bits) for i in range(devices)])  25.3 us
    pallas_call x12, Pallas kernels, call(): pl.pallas_call(body, out_shape=outs, in_specs=[pl.BlockSpec(memory_space=...  24.3 us
    ppermute x4, starting transfers between devices, body(): near[k] = lax.ppermute(grads[j], ('pipe', 'expert'), pairs)  5.92 us
    unnamed x30, local copies, waits for them, and re-layouts  3.56 us
    ppermute x4, waiting for transfers between devices, body(): near[k] = lax.ppermute(grads[j], ('pipe', 'expert'), pairs)  2.41 us
  transfers between devices with their start and end apart: 43, of which 16 were waited for; matrix products, arithmetic and copies ran while one was open for 0% of the time, Pallas kernels for 11%

profile of v3, /device:TPU:0, one launch (start us, length us, event | category | flops | bytes accessed | tf_op | source)
XLA Modules:
  0.0 107.9 jit_solution(14491411908932977671)
XLA Ops:
  1.7 1.2 %copy-done.3 = bf16[1,128,4096]{2,1,0:T(8,128)(2,1)S(1)} copy-done((bf16[1,128,4096]{2,1,0:T(8,128)(2,1)S(1)}, bf16[1,128,4096]{2,1,0:T(8,128)(2,1)}, u32[]{:S(2)}) %copy-start.3) | copy-done | bytes 1048600
  4.2 4.7 %collective-permute-start.1 = (bf16[24,2048]{1,0:T(8,128)(2,1)S(1)}, bf16[24,2048]{1,0:T(8,128)(2,1)S(1)}, u32[]{:S(2)}, u32[]{:S(2)}) collective-permute-start(bf16[24,2048]{1,0:T(8,128)(2,1)S(1)} %get-tuple-element.59), channel_id=1, source_target_pairs={{0,12},{1,13},{2,14},{3,15},{4,8},{5,9},{6,10},{7,11},{8,4},{9,5},... | collective-permute-start | bytes 294920 | tf_op jit(solution)/shard_map/ppermute | solution.py:278
  9.0 3.5 %shard_map.123 = (f32[16,128]{1,0:T(8,128)}, bf16[24,2048]{1,0:T(8,128)(2,1)}, bf16[24,2048]{1,0:T(8,128)(2,1)}, bf16[24,2048]{1,0:T(8,128)(2,1)}, bf16[24,2048]...) custom-call(s32[8,128]{1,0:T(8,128)} %bitcast.32, ...), custom_call_target="tpu_custom_call" | custom-call | bytes 18000000 | tf_op jit(solution)/shard_map/pallas_call | solution.py:19
  12.7 5.1 %collective-permute-done.refs_0_ = bf16[24,2048]{1,0:T(8,128)(2,1)S(1)} collective-permute-done((bf16[24,2048]{1,0:T(8,128)(2,1)S(1)}, bf16[24,2048]{1,0:T(8,128)(2,1)S(1)}, u32[]{:S(2)}, u32[]{:S(2)}) %collective-permute-start) | collective-permute-done | bytes 98336 | tf_op jit(solution)/shard_map/ppermute | solution.py:278
  17.8 2.0 %collective-permute-start.13 = (bf16[24,2048]{1,0:T(8,128)(2,1)S(1)}, bf16[24,2048]{1,0:T(8,128)(2,1)S(1)}, u32[]{:S(2)}, u32[]{:S(2)}) collective-permute-start(bf16[24,2048]{1,0:T(8,128)(2,1)S(1)} %get-tuple-element.76), channel_id=1, source_target_pairs={{0,4},{1,5},{2,6},{3,7},{4,0},{5,1},{6,2},{7,3},{8,12},{9,13},{10,... | collective-permute-start | bytes 294920 | tf_op jit(solution)/shard_map/ppermute | solution.py:278
  19.9 1.5 %collective-permute-start.14 = (bf16[24,2048]{1,0:T(8,128)(2,1)S(1)}, bf16[24,2048]{1,0:T(8,128)(2,1)S(1)}, u32[]{:S(2)}, u32[]{:S(2)}) collective-permute-start(bf16[24,2048]{1,0:T(8,128)(2,1)S(1)} %collective-permute-done.refs_0_), channel_id=1, source_target_pairs={{0,2},{1,3},{2,0},{3,1},{4,6},{5,7},{6,4},{7,5},{8,10},{9,11},{10,... | collective-permute-start | bytes 294920 | tf_op jit(solution)/shard_map/ppermute | solution.py:278
  21.9 1.5 %collective-permute-start.17 = (bf16[24,2048]{1,0:T(8,128)(2,1)S(1)}, bf16[24,2048]{1,0:T(8,128)(2,1)S(1)}, u32[]{:S(2)}, u32[]{:S(2)}) collective-permute-start(bf16[24,2048]{1,0:T(8,128)(2,1)S(1)} %get-tuple-element.77.refs_3_), channel_id=1, source_target_pairs={{0,2},{1,3},{2,0},{3,1},{4,6},{5,7},{6,4},{7,5},{8,10},{9,11},{10,... | collective-permute-start | bytes 294920 | tf_op jit(solution)/shard_map/ppermute | solution.py:278
  23.5 1.1 collective-permute-start.6
  24.5 2.4 %collective-permute-start.7 = (bf16[24,2048]{1,0:T(8,128)(2,1)}, bf16[24,2048]{1,0:T(8,128)(2,1)S(1)}, u32[]{:S(2)}, u32[]{:S(2)}) collective-permute-start(bf16[24,2048]{1,0:T(8,128)(2,1)} %get-tuple-element.71), channel_id=1, source_target_pairs={{0,12},{1,13},{2,14},{3,15},{4,8},{5,9},{6,10},{7,11},{8,4},{9,5},... | collective-permute-start | bytes 294920 | tf_op jit(solution)/shard_map/ppermute | solution.py:278
  27.0 1.5 %collective-permute-start.16 = (bf16[24,2048]{1,0:T(8,128)(2,1)S(1)}, bf16[24,2048]{1,0:T(8,128)(2,1)S(1)}, u32[]{:S(2)}, u32[]{:S(2)}) collective-permute-start(bf16[24,2048]{1,0:T(8,128)(2,1)S(1)} %collective-permute-done.13.refs_2_), channel_id=1, source_target_pairs={{0,2},{1,3},{2,0},{3,1},{4,6},{5,7},{6,4},{7,5},{8,10},{9,11},{10,... | collective-permute-start | bytes 294920 | tf_op jit(solution)/shard_map/ppermute | solution.py:278
  29.0 1.5 %collective-permute-start.11 = (bf16[24,2048]{1,0:T(8,128)(2,1)S(1)}, bf16[24,2048]{1,0:T(8,128)(2,1)S(1)}, u32[]{:S(2)}, u32[]{:S(2)}) collective-permute-start(bf16[24,2048]{1,0:T(8,128)(2,1)S(1)} %collective-permute-done.8.refs_2_), channel_id=1, source_target_pairs={{0,2},{1,3},{2,0},{3,1},{4,6},{5,7},{6,4},{7,5},{8,10},{9,11},{10,... | collective-permute-start | bytes 294920 | tf_op jit(solution)/shard_map/ppermute | solution.py:278
  30.6 2.0 %collective-permute-done.6.refs_0_ = bf16[24,2048]{1,0:T(8,128)(2,1)S(1)} collective-permute-done((bf16[24,2048]{1,0:T(8,128)(2,1)}, bf16[24,2048]{1,0:T(8,128)(2,1)S(1)}, u32[]{:S(2)}, u32[]{:S(2)}) %collective-permute-start.6) | collective-permute-done | bytes 98336 | tf_op jit(solution)/shard_map/ppermute | solution.py:278
  32.6 1.2 %collective-permute-start.9 = (bf16[24,2048]{1,0:T(8,128)(2,1)S(1)}, bf16[24,2048]{1,0:T(8,128)(2,1)S(1)}, u32[]{:S(2)}, u32[]{:S(2)}) collective-permute-start(bf16[24,2048]{1,0:T(8,128)(2,1)S(1)} %collective-permute-done.6.refs_0_), channel_id=1, source_target_pairs={{0,2},{1,3},{2,0},{3,1},{4,6},{5,7},{6,4},{7,5},{8,10},{9,11},{10,... | collective-permute-start | bytes 294920 | tf_op jit(solution)/shard_map/ppermute | solution.py:278
  33.8 0.8 collective-permute-start.10
  34.6 1.6 %copy-done.1 = bf16[1,1,4096,256]{3,2,1,0:T(8,128)(2,1)S(1)} copy-done((bf16[1,1,4096,256]{3,2,1,0:T(8,128)(2,1)S(1)}, bf16[1,1,4096,256]{3,2,1,0:T(8,128)(2,1)}, u32[]{:S(2)}) %copy-start.1) | copy-done | bytes 2097176
  36.2 2.7 %shard_map.124.refs_8_ = f32[4,192,256]{2,1,0:T(8,128)S(1)} custom-call(bf16[24,2048]{1,0:T(8,128)(2,1)S(1)} %collective-permute-done.refs_0_, bf16[24,2048]{1,0:T(8,128)(2,1)S(1)} %collective-permute-done.1.refs_1_, bf16[24,2048]{1,0:T(8,128)(2,1)S(1)} %collective-permute-done.13.refs_2_, bf16[24,2048]{1,0:T(8,128)(2,1)S(1)} %get-tuple-element.77.refs_3_, ...), custom_call_target="tpu_custom_call" | custom-call | bytes 9720000 | tf_op jit(solution)/shard_map/pallas_call | solution.py:19
  39.0 5.8 %shard_map.125 = (f32[48,2048]{1,0:T(8,128)S(1)}, f32[48,2048]{1,0:T(8,128)S(1)}, bf16[48,2048]{1,0:T(8,128)(2,1)S(1)}, bf16[48,2048]{1,0:T(8,128)(2,1)S(1)}) custom-call(bf16[24,2048]{1,0:T(8,128)(2,1)S(1)} %collective-permute-done.6.refs_0_, bf16[24,2048]{1,0:T(8,128)(2,1)S(1)} %collective-permute-done.7.refs_1_, ...), custom_call_target="tpu_custom_call" | custom-call | bytes 20520000 | tf_op jit(solution)/shard_map/pallas_call | solution.py:19
  44.8 1.2 %collective-permute-start.18 = (bf16[48,2048]{1,0:T(8,128)(2,1)S(1)}, bf16[48,2048]{1,0:T(8,128)(2,1)S(1)}, u32[]{:S(2)}, u32[]{:S(2)}) collective-permute-start(bf16[48,2048]{1,0:T(8,128)(2,1)S(1)} %get-tuple-element.82), channel_id=1, source_target_pairs={{0,2},{1,3},{2,0},{3,1},{4,6},{5,7},{6,4},{7,5},{8,10},{9,11},{10,... | collective-permute-start | bytes 589832 | tf_op jit(solution)/shard_map/ppermute | solution.py:278
  47.7 2.2 %collective-permute-start.32 = (bf16[24,2048]{1,0:T(8,128)(2,1)S(1)}, bf16[24,2048]{1,0:T(8,128)(2,1)S(1)}, u32[]{:S(2)}, u32[]{:S(2)}) collective-permute-start(bf16[24,2048]{1,0:T(8,128)(2,1)S(1)} %copy-done.12), channel_id=1, source_target_pairs={{0,8},{1,9},{2,10},{3,11},{4,12},{5,13},{6,14},{7,15},{8,0},{9,1},... | collective-permute-start | bytes 294920 | tf_op jit(solution)/shard_map/ppermute | solution.py:278
  49.9 1.4 %collective-permute-start.33 = (bf16[24,2048]{1,0:T(8,128)(2,1)S(1)}, bf16[24,2048]{1,0:T(8,128)(2,1)S(1)}, u32[]{:S(2)}, u32[]{:S(2)}) collective-permute-start(bf16[24,2048]{1,0:T(8,128)(2,1)S(1)} %copy-done.11), channel_id=1, source_target_pairs={{0,12},{1,13},{2,14},{3,15},{4,8},{5,9},{6,10},{7,11},{8,4},{9,5},... | collective-permute-start | bytes 294920 | tf_op jit(solution)/shard_map/ppermute | solution.py:278
  51.6 1.5 %collective-permute-start.5 = (f32[16,128]{1,0:T(8,128)S(1)}, f32[16,128]{1,0:T(8,128)S(1)}, u32[]{:S(2)}, u32[]{:S(2)}) collective-permute-start(f32[16,128]{1,0:T(8,128)S(1)} %copy-done.14), channel_id=1, source_target_pairs={{0,16},{16,0},{1,17},{17,1},{2,18},{18,2},{3,19},{19,3},{4,20},{20... | collective-permute-start | bytes 24584 | tf_op jit(solution)/shard_map/ppermute | solution.py:368
  53.7 1.9 %collective-permute-start.19 = (bf16[24,2048]{1,0:T(8,128)(2,1)S(1)}, bf16[24,2048]{1,0:T(8,128)(2,1)S(1)}, u32[]{:S(2)}, u32[]{:S(2)}) collective-permute-start(bf16[24,2048]{1,0:T(8,128)(2,1)S(1)} %get-tuple-element.83), channel_id=1, source_target_pairs={{0,8},{1,9},{2,10},{3,11},{4,12},{5,13},{6,14},{7,15},{8,0},{9,1},... | collective-permute-start | bytes 294920 | tf_op jit(solution)/shard_map/ppermute | solution.py:278
  55.7 1.4 %collective-permute-start.20 = (bf16[24,2048]{1,0:T(8,128)(2,1)S(1)}, bf16[24,2048]{1,0:T(8,128)(2,1)S(1)}, u32[]{:S(2)}, u32[]{:S(2)}) collective-permute-start(bf16[24,2048]{1,0:T(8,128)(2,1)S(1)} %get-tuple-element.84), channel_id=1, source_target_pairs={{0,12},{1,13},{2,14},{3,15},{4,8},{5,9},{6,10},{7,11},{8,4},{9,5},... | collective-permute-start | bytes 294920 | tf_op jit(solution)/shard_map/ppermute | solution.py:278
  57.0 1.0 collective-permute-done.32.refs_0_
  58.6 1.5 %collective-permute-start.35 = (bf16[24,2048]{1,0:T(8,128)(2,1)S(1)}, bf16[24,2048]{1,0:T(8,128)(2,1)S(1)}, u32[]{:S(2)}, u32[]{:S(2)}) collective-permute-start(bf16[24,2048]{1,0:T(8,128)(2,1)S(1)} %collective-permute-done.33.refs_1_), channel_id=1, source_target_pairs={{0,2},{1,3},{2,0},{3,1},{4,6},{5,7},{6,4},{7,5},{8,10},{9,11},{10,... | collective-permute-start | bytes 294920 | tf_op jit(solution)/shard_map/ppermute | solution.py:278
  60.1 4.0 %collective-permute-done.19.refs_0_ = bf16[24,2048]{1,0:T(8,128)(2,1)S(1)} collective-permute-done((bf16[24,2048]{1,0:T(8,128)(2,1)S(1)}, bf16[24,2048]{1,0:T(8,128)(2,1)S(1)}, u32[]{:S(2)}, u32[]{:S(2)}) %collective-permute-start.19) | collective-permute-done | bytes 98336 | tf_op jit(solution)/shard_map/ppermute | solution.py:278
  64.1 1.2 %collective-permute-start.36 = (bf16[24,2048]{1,0:T(8,128)(2,1)S(1)}, bf16[24,2048]{1,0:T(8,128)(2,1)S(1)}, u32[]{:S(2)}, u32[]{:S(2)}) collective-permute-start(bf16[24,2048]{1,0:T(8,128)(2,1)S(1)} %collective-permute-done.31.refs_2_), channel_id=1, source_target_pairs={{0,2},{1,3},{2,0},{3,1},{4,6},{5,7},{6,4},{7,5},{8,10},{9,11},{10,... | collective-permute-start | bytes 294920 | tf_op jit(solution)/shard_map/ppermute | solution.py:278
  65.3 1.8 %shard_map.128 = (bf16[1,128,4096]{2,1,0:T(8,128)(2,1)}, bf16[24,2048]{1,0:T(8,128)(2,1)S(1)}, bf16[24,2048]{1,0:T(8,128)(2,1)S(1)}, bf16[24,2048]{1,0:T(8,128)(2,1)S(1)}, bf16[24,2048]{1,0:T(8,128)(2,1)S(1)}) custom-call(s32[8,128]{1,0:T(8,128)S(1)} %bitcast.34, f32[16,128]{1,0:T(8,128)S(1)} %collective-permute-done.5.keys_ref, ...), custom_call_target="tpu_custom_call" | custom-call | bytes 6480000 | tf_op jit(solution)/shard_map/pallas_call | solution.py:19
  67.1 2.4 %collective-permute-start.23 = (bf16[24,2048]{1,0:T(8,128)(2,1)S(1)}, bf16[24,2048]{1,0:T(8,128)(2,1)S(1)}, u32[]{:S(2)}, u32[]{:S(2)}) collective-permute-start(bf16[24,2048]{1,0:T(8,128)(2,1)S(1)} %get-tuple-element.90), channel_id=1, source_target_pairs={{0,24},{1,25},{2,26},{3,27},{4,28},{5,29},{6,30},{7,31},{8,16},{9,... | collective-permute-start | bytes 294920 | tf_op jit(solution)/shard_map/ppermute | solution.py:392
  69.6 1.6 %collective-permute-start.24 = (bf16[24,2048]{1,0:T(8,128)(2,1)S(1)}, bf16[24,2048]{1,0:T(8,128)(2,1)S(1)}, u32[]{:S(2)}, u32[]{:S(2)}) collective-permute-start(bf16[24,2048]{1,0:T(8,128)(2,1)S(1)} %get-tuple-element.91), channel_id=1, source_target_pairs={{0,28},{1,29},{2,30},{3,31},{4,24},{5,25},{6,26},{7,27},{8,20},{9,... | collective-permute-start | bytes 294920 | tf_op jit(solution)/shard_map/ppermute | solution.py:392
  71.2 1.4 %collective-permute-start.25 = (bf16[24,2048]{1,0:T(8,128)(2,1)S(1)}, bf16[24,2048]{1,0:T(8,128)(2,1)S(1)}, u32[]{:S(2)}, u32[]{:S(2)}) collective-permute-start(bf16[24,2048]{1,0:T(8,128)(2,1)S(1)} %get-tuple-element.92), channel_id=1, source_target_pairs={{0,20},{1,21},{2,22},{3,23},{4,16},{5,17},{6,18},{7,19},{8,28},{9,... | collective-permute-start | bytes 294920 | tf_op jit(solution)/shard_map/ppermute | solution.py:392
  73.9 1.9 %collective-permute-done.23.refs_0_ = bf16[24,2048]{1,0:T(8,128)(2,1)S(1)} collective-permute-done((bf16[24,2048]{1,0:T(8,128)(2,1)S(1)}, bf16[24,2048]{1,0:T(8,128)(2,1)S(1)}, u32[]{:S(2)}, u32[]{:S(2)}) %collective-permute-start.23) | collective-permute-done | bytes 98336 | tf_op jit(solution)/shard_map/ppermute | solution.py:392
  75.7 0.8 collective-permute-start.27
  77.1 1.3 %collective-permute-start.28 = (bf16[24,2048]{1,0:T(8,128)(2,1)S(1)}, bf16[24,2048]{1,0:T(8,128)(2,1)S(1)}, u32[]{:S(2)}, u32[]{:S(2)}) collective-permute-start(bf16[24,2048]{1,0:T(8,128)(2,1)S(1)} %collective-permute-done.24.refs_1_), channel_id=1, source_target_pairs={{0,2},{1,3},{2,0},{3,1},{4,6},{5,7},{6,4},{7,5},{8,10},{9,11},{10,... | collective-permute-start | bytes 294920 | tf_op jit(solution)/shard_map/ppermute | solution.py:278
  79.1 1.3 %collective-permute-start.30 = (bf16[24,2048]{1,0:T(8,128)(2,1)S(1)}, bf16[24,2048]{1,0:T(8,128)(2,1)S(1)}, u32[]{:S(2)}, u32[]{:S(2)}) collective-permute-start(bf16[24,2048]{1,0:T(8,128)(2,1)S(1)} %collective-permute-done.26.refs_3_), channel_id=1, source_target_pairs={{0,2},{1,3},{2,0},{3,1},{4,6},{5,7},{6,4},{7,5},{8,10},{9,11},{10,... | collective-permute-start | bytes 294920 | tf_op jit(solution)/shard_map/ppermute | solution.py:278
  80.4 2.7 %shard_map.129.refs_8_ = f32[4,192,256]{2,1,0:T(8,128)S(1)} custom-call(bf16[24,2048]{1,0:T(8,128)(2,1)S(1)} %collective-permute-done.32.refs_0_, bf16[24,2048]{1,0:T(8,128)(2,1)S(1)} %collective-permute-done.33.refs_1_, bf16[24,2048]{1,0:T(8,128)(2,1)S(1)} %collective-permute-done.31.refs_2_, bf16[24,2048]{1,0:T(8,128)(2,1)S(1)} %copy-done.5, ...), custom_call_target="tpu_custom_call" | custom-call | bytes 9720000 | tf_op jit(solution)/shard_map/pallas_call | solution.py:19
  83.1 0.9 collective-permute-done.29.refs_6_
  84.0 1.1 collective-permute-done.30.refs_7_
  85.1 5.6 %shard_map.130 = (f32[48,2048]{1,0:T(8,128)S(1)}, f32[48,2048]{1,0:T(8,128)S(1)}, bf16[48,2048]{1,0:T(8,128)(2,1)S(1)}, bf16[48,2048]{1,0:T(8,128)(2,1)S(1)}) custom-call(bf16[24,2048]{1,0:T(8,128)(2,1)S(1)} %collective-permute-done.23.refs_0_, bf16[24,2048]{1,0:T(8,128)(2,1)S(1)} %collective-permute-done.24.refs_1_, ...), custom_call_target="tpu_custom_call" | custom-call | bytes 20520000 | tf_op jit(solution)/shard_map/pallas_call | solution.py:19
  90.7 1.2 %collective-permute-start.38 = (bf16[48,2048]{1,0:T(8,128)(2,1)S(1)}, bf16[48,2048]{1,0:T(8,128)(2,1)S(1)}, u32[]{:S(2)}, u32[]{:S(2)}) collective-permute-start(bf16[48,2048]{1,0:T(8,128)(2,1)S(1)} %get-tuple-element.107), channel_id=1, source_target_pairs={{0,2},{1,3},{2,0},{3,1},{4,6},{5,7},{6,4},{7,5},{8,10},{9,11},{10,... | collective-permute-start | bytes 589832 | tf_op jit(solution)/shard_map/ppermute | solution.py:278
  91.9 0.9 collective-permute-start.41
  92.8 4.3 %collective-permute-done.38.far_ref = bf16[48,2048]{1,0:T(8,128)(2,1)S(1)} collective-permute-done((bf16[48,2048]{1,0:T(8,128)(2,1)S(1)}, bf16[48,2048]{1,0:T(8,128)(2,1)S(1)}, u32[]{:S(2)}, u32[]{:S(2)}) %collective-permute-start.38) | collective-permute-done | bytes 196640 | tf_op jit(solution)/shard_map/ppermute | solution.py:278
  97.2 1.6 %collective-permute-start.39 = (bf16[24,2048]{1,0:T(8,128)(2,1)S(1)}, bf16[24,2048]{1,0:T(8,128)(2,1)S(1)}, u32[]{:S(2)}, u32[]{:S(2)}) collective-permute-start(bf16[24,2048]{1,0:T(8,128)(2,1)S(1)} %get-tuple-element.108), channel_id=1, source_target_pairs={{0,8},{1,9},{2,10},{3,11},{4,12},{5,13},{6,14},{7,15},{8,0},{9,1},... | collective-permute-start | bytes 294920 | tf_op jit(solution)/shard_map/ppermute | solution.py:278
  98.8 1.8 %collective-permute-start.40 = (bf16[24,2048]{1,0:T(8,128)(2,1)S(1)}, bf16[24,2048]{1,0:T(8,128)(2,1)S(1)}, u32[]{:S(2)}, u32[]{:S(2)}) collective-permute-start(bf16[24,2048]{1,0:T(8,128)(2,1)S(1)} %get-tuple-element.109), channel_id=1, source_target_pairs={{0,12},{1,13},{2,14},{3,15},{4,8},{5,9},{6,10},{7,11},{8,4},{9,5},... | collective-permute-start | bytes 294920 | tf_op jit(solution)/shard_map/ppermute | solution.py:278
  100.8 3.0 %collective-permute-done.39.refs_0_ = bf16[24,2048]{1,0:T(8,128)(2,1)S(1)} collective-permute-done((bf16[24,2048]{1,0:T(8,128)(2,1)S(1)}, bf16[24,2048]{1,0:T(8,128)(2,1)S(1)}, u32[]{:S(2)}, u32[]{:S(2)}) %collective-permute-start.39) | collective-permute-done | bytes 98336 | tf_op jit(solution)/shard_map/ppermute | solution.py:278
  103.8 1.6 %collective-permute-done.40.refs_1_ = bf16[24,2048]{1,0:T(8,128)(2,1)S(1)} collective-permute-done((bf16[24,2048]{1,0:T(8,128)(2,1)S(1)}, bf16[24,2048]{1,0:T(8,128)(2,1)S(1)}, u32[]{:S(2)}, u32[]{:S(2)}) %collective-permute-start.40) | collective-permute-done | bytes 98336 | tf_op jit(solution)/shard_map/ppermute | solution.py:278
  105.4 0.9 collective-permute-done.42.refs_2_
  106.3 1.6 %shard_map.133 = bf16[1,128,4096]{2,1,0:T(8,128)(2,1)} custom-call(s32[8,128]{1,0:T(8,128)S(1)} %bitcast.36, bf16[24,2048]{1,0:T(8,128)(2,1)S(1)} %collective-permute-done.39.refs_0_, bf16[24,2048]{1,0:T(8,128)(2,1)S(1)} %collective-permute-done.40.refs_1_, bf16[24,2048]{1,0:T(8,128)(2,1)S(1)} %collective-permute-done.42.refs_2_, ...), custom_call_target="tpu_custom_call" | custom-call | bytes 3600000 | tf_op jit(solution)/shard_map/pallas_call | solution.py:19
  (80 shorter events, 9.8 us)
Async XLA Ops:
  0.6 34.0 %copy-start = (bf16[1,1,4096,256]{3,2,1,0:T(8,128)(2,1)S(1)}, bf16[1,1,4096,256]{3,2,1,0:T(8,128)(2,1)}, u32[]{:S(2)}) copy-start(bf16[1,1,4096,256]{3,2,1,0:T(8,128)(2,1)} %param.19) | copy-start | bytes 6291460
  0.6 11.8 %collective-permute-start.2 = (bf16[4096,256]{1,0:T(8,128)(2,1)}, bf16[4096,256]{1,0:T(8,128)(2,1)S(1)}, u32[]{:S(2)}, u32[]{:S(2)}) collective-permute-start(bf16[4096,256]{1,0:T(8,128)(2,1)} %bitcast.18), channel_id=1, source_target_pairs={{0,1},{1,0},{2,3},{3,2},{4,5},{5,4},{6,7},{7,6},{8,9},{9,8},{10,11... | collective-permute-start | bytes 6291464 | tf_op jit(solution)/shard_map/ppermute | solution.py:278
  1.2 11.3 %collective-permute-start.3 = (bf16[4096,256]{1,0:T(8,128)(2,1)}, bf16[4096,256]{1,0:T(8,128)(2,1)S(1)}, u32[]{:S(2)}, u32[]{:S(2)}) collective-permute-start(bf16[4096,256]{1,0:T(8,128)(2,1)} %bitcast.23), channel_id=1, source_target_pairs={{0,1},{1,0},{2,3},{3,2},{4,5},{5,4},{6,7},{7,6},{8,9},{9,8},{10,11... | collective-permute-start | bytes 6291464 | tf_op jit(solution)/shard_map/ppermute | solution.py:278
  1.2 11.2 %collective-permute-start.4 = (bf16[256,4096]{1,0:T(8,128)(2,1)}, bf16[256,4096]{1,0:T(8,128)(2,1)}, u32[]{:S(2)}, u32[]{:S(2)}) collective-permute-start(bf16[256,4096]{1,0:T(8,128)(2,1)} %bitcast.28), channel_id=1, source_target_pairs={{0,1},{1,0},{2,3},{3,2},{4,5},{5,4},{6,7},{7,6},{8,9},{9,8},{10,11... | collective-permute-start | bytes 6291464 | tf_op jit(solution)/shard_map/ppermute | solution.py:278
  4.2 8.5 %collective-permute-start.1 = (bf16[24,2048]{1,0:T(8,128)(2,1)S(1)}, bf16[24,2048]{1,0:T(8,128)(2,1)S(1)}, u32[]{:S(2)}, u32[]{:S(2)}) collective-permute-start(bf16[24,2048]{1,0:T(8,128)(2,1)S(1)} %get-tuple-element.59), channel_id=1, source_target_pairs={{0,12},{1,13},{2,14},{3,15},{4,8},{5,9},{6,10},{7,11},{8,4},{9,5},... | collective-permute-start | bytes 294920 | tf_op jit(solution)/shard_map/ppermute | solution.py:278
  9.0 8.9 %collective-permute-start = (bf16[24,2048]{1,0:T(8,128)(2,1)S(1)}, bf16[24,2048]{1,0:T(8,128)(2,1)S(1)}, u32[]{:S(2)}, u32[]{:S(2)}) collective-permute-start(bf16[24,2048]{1,0:T(8,128)(2,1)S(1)} %get-tuple-element.58.refs_0_), channel_id=1, source_target_pairs={{0,8},{1,9},{2,10},{3,11},{4,12},{5,13},{6,14},{7,15},{8,0},{9,1},... | collective-permute-start | bytes 294920 | tf_op jit(solution)/shard_map/ppermute | solution.py:278
  17.8 5.6 %collective-permute-start.8 = (bf16[24,2048]{1,0:T(8,128)(2,1)}, bf16[24,2048]{1,0:T(8,128)(2,1)S(1)}, u32[]{:S(2)}, u32[]{:S(2)}) collective-permute-start(bf16[24,2048]{1,0:T(8,128)(2,1)} %get-tuple-element.72), channel_id=1, source_target_pairs={{0,4},{1,5},{2,6},{3,7},{4,0},{5,1},{6,2},{7,3},{8,12},{9,13},{10,... | collective-permute-start | bytes 294920 | tf_op jit(solution)/shard_map/ppermute | solution.py:278
  17.8 6.7 %collective-permute-start.13 = (bf16[24,2048]{1,0:T(8,128)(2,1)S(1)}, bf16[24,2048]{1,0:T(8,128)(2,1)S(1)}, u32[]{:S(2)}, u32[]{:S(2)}) collective-permute-start(bf16[24,2048]{1,0:T(8,128)(2,1)S(1)} %get-tuple-element.76), channel_id=1, source_target_pairs={{0,4},{1,5},{2,6},{3,7},{4,0},{5,1},{6,2},{7,3},{8,12},{9,13},{10,... | collective-permute-start | bytes 294920 | tf_op jit(solution)/shard_map/ppermute | solution.py:278
  19.9 7.1 %collective-permute-start.14 = (bf16[24,2048]{1,0:T(8,128)(2,1)S(1)}, bf16[24,2048]{1,0:T(8,128)(2,1)S(1)}, u32[]{:S(2)}, u32[]{:S(2)}) collective-permute-start(bf16[24,2048]{1,0:T(8,128)(2,1)S(1)} %collective-permute-done.refs_0_), channel_id=1, source_target_pairs={{0,2},{1,3},{2,0},{3,1},{4,6},{5,7},{6,4},{7,5},{8,10},{9,11},{10,... | collective-permute-start | bytes 294920 | tf_op jit(solution)/shard_map/ppermute | solution.py:278
  21.4 7.1 %collective-permute-start.15 = (bf16[24,2048]{1,0:T(8,128)(2,1)S(1)}, bf16[24,2048]{1,0:T(8,128)(2,1)S(1)}, u32[]{:S(2)}, u32[]{:S(2)}) collective-permute-start(bf16[24,2048]{1,0:T(8,128)(2,1)S(1)} %collective-permute-done.1.refs_1_), channel_id=1, source_target_pairs={{0,2},{1,3},{2,0},{3,1},{4,6},{5,7},{6,4},{7,5},{8,10},{9,11},{10,... | collective-permute-start | bytes 294920 | tf_op jit(solution)/shard_map/ppermute | solution.py:278
  21.9 7.1 %collective-permute-start.17 = (bf16[24,2048]{1,0:T(8,128)(2,1)S(1)}, bf16[24,2048]{1,0:T(8,128)(2,1)S(1)}, u32[]{:S(2)}, u32[]{:S(2)}) collective-permute-start(bf16[24,2048]{1,0:T(8,128)(2,1)S(1)} %get-tuple-element.77.refs_3_), channel_id=1, source_target_pairs={{0,2},{1,3},{2,0},{3,1},{4,6},{5,7},{6,4},{7,5},{8,10},{9,11},{10,... | collective-permute-start | bytes 294920 | tf_op jit(solution)/shard_map/ppermute | solution.py:278
  23.5 9.1 %collective-permute-start.6 = (bf16[24,2048]{1,0:T(8,128)(2,1)}, bf16[24,2048]{1,0:T(8,128)(2,1)S(1)}, u32[]{:S(2)}, u32[]{:S(2)}) collective-permute-start(bf16[24,2048]{1,0:T(8,128)(2,1)} %get-tuple-element.70), channel_id=1, source_target_pairs={{0,8},{1,9},{2,10},{3,11},{4,12},{5,13},{6,14},{7,15},{8,0},{9,1},... | collective-permute-start | bytes 294920 | tf_op jit(solution)/shard_map/ppermute | solution.py:278
  24.5 9.2 %collective-permute-start.7 = (bf16[24,2048]{1,0:T(8,128)(2,1)}, bf16[24,2048]{1,0:T(8,128)(2,1)S(1)}, u32[]{:S(2)}, u32[]{:S(2)}) collective-permute-start(bf16[24,2048]{1,0:T(8,128)(2,1)} %get-tuple-element.71), channel_id=1, source_target_pairs={{0,12},{1,13},{2,14},{3,15},{4,8},{5,9},{6,10},{7,11},{8,4},{9,5},... | collective-permute-start | bytes 294920 | tf_op jit(solution)/shard_map/ppermute | solution.py:278
  27.0 7.7 %collective-permute-start.16 = (bf16[24,2048]{1,0:T(8,128)(2,1)S(1)}, bf16[24,2048]{1,0:T(8,128)(2,1)S(1)}, u32[]{:S(2)}, u32[]{:S(2)}) collective-permute-start(bf16[24,2048]{1,0:T(8,128)(2,1)S(1)} %collective-permute-done.13.refs_2_), channel_id=1, source_target_pairs={{0,2},{1,3},{2,0},{3,1},{4,6},{5,7},{6,4},{7,5},{8,10},{9,11},{10,... | collective-permute-start | bytes 294920 | tf_op jit(solution)/shard_map/ppermute | solution.py:278
  28.5 10.4 %collective-permute-start.12 = (bf16[24,2048]{1,0:T(8,128)(2,1)}, bf16[24,2048]{1,0:T(8,128)(2,1)S(1)}, u32[]{:S(2)}, u32[]{:S(2)}) collective-permute-start(bf16[24,2048]{1,0:T(8,128)(2,1)} %get-tuple-element.73.refs_3_), channel_id=1, source_target_pairs={{0,2},{1,3},{2,0},{3,1},{4,6},{5,7},{6,4},{7,5},{8,10},{9,11},{10,... | collective-permute-start | bytes 294920 | tf_op jit(solution)/shard_map/ppermute | solution.py:278
  29.0 10.0 %collective-permute-start.11 = (bf16[24,2048]{1,0:T(8,128)(2,1)S(1)}, bf16[24,2048]{1,0:T(8,128)(2,1)S(1)}, u32[]{:S(2)}, u32[]{:S(2)}) collective-permute-start(bf16[24,2048]{1,0:T(8,128)(2,1)S(1)} %collective-permute-done.8.refs_2_), channel_id=1, source_target_pairs={{0,2},{1,3},{2,0},{3,1},{4,6},{5,7},{6,4},{7,5},{8,10},{9,11},{10,... | collective-permute-start | bytes 294920 | tf_op jit(solution)/shard_map/ppermute | solution.py:278
  32.6 6.4 %collective-permute-start.9 = (bf16[24,2048]{1,0:T(8,128)(2,1)S(1)}, bf16[24,2048]{1,0:T(8,128)(2,1)S(1)}, u32[]{:S(2)}, u32[]{:S(2)}) collective-permute-start(bf16[24,2048]{1,0:T(8,128)(2,1)S(1)} %collective-permute-done.6.refs_0_), channel_id=1, source_target_pairs={{0,2},{1,3},{2,0},{3,1},{4,6},{5,7},{6,4},{7,5},{8,10},{9,11},{10,... | collective-permute-start | bytes 294920 | tf_op jit(solution)/shard_map/ppermute | solution.py:278
  33.8 5.2 %collective-permute-start.10 = (bf16[24,2048]{1,0:T(8,128)(2,1)S(1)}, bf16[24,2048]{1,0:T(8,128)(2,1)S(1)}, u32[]{:S(2)}, u32[]{:S(2)}) collective-permute-start(bf16[24,2048]{1,0:T(8,128)(2,1)S(1)} %collective-permute-done.7.refs_1_), channel_id=1, source_target_pairs={{0,2},{1,3},{2,0},{3,1},{4,6},{5,7},{6,4},{7,5},{8,10},{9,11},{10,... | collective-permute-start | bytes 294920 | tf_op jit(solution)/shard_map/ppermute | solution.py:278
  38.9 26.4 %copy-start.4 = (bf16[128,4096]{1,0:T(8,128)(2,1)S(1)}, bf16[128,4096]{1,0:T(8,128)(2,1)}, u32[]{:S(2)}) copy-start(bf16[128,4096]{1,0:T(8,128)(2,1)} %grad_last_ref.1) | copy-start | bytes 3145732
  38.9 26.4 %copy-start.9 = (s32[1,128,8]{1,2,0:T(8,128)S(1)}, s32[1,128,8]{1,2,0:T(8,128)}, u32[]{:S(2)}) copy-start(s32[1,128,8]{1,2,0:T(8,128)} %param.15) | copy-start | bytes 12292
  44.8 28.3 %copy-start.5 = (bf16[24,2048]{1,0:T(8,128)(2,1)S(1)}, bf16[24,2048]{1,0:T(8,128)(2,1)}, u32[]{:S(2)}) copy-start(bf16[24,2048]{1,0:T(8,128)(2,1)} %get-tuple-element.105.refs_3_) | copy-start | bytes 294916
  44.8 6.8 %collective-permute-start.18 = (bf16[48,2048]{1,0:T(8,128)(2,1)S(1)}, bf16[48,2048]{1,0:T(8,128)(2,1)S(1)}, u32[]{:S(2)}, u32[]{:S(2)}) collective-permute-start(bf16[48,2048]{1,0:T(8,128)(2,1)S(1)} %get-tuple-element.82), channel_id=1, source_target_pairs={{0,2},{1,3},{2,0},{3,1},{4,6},{5,7},{6,4},{7,5},{8,10},{9,11},{10,... | collective-permute-start | bytes 589832 | tf_op jit(solution)/shard_map/ppermute | solution.py:278
  46.0 7.7 %collective-permute-start.21 = (bf16[48,2048]{1,0:T(8,128)(2,1)S(1)}, bf16[48,2048]{1,0:T(8,128)(2,1)S(1)}, u32[]{:S(2)}, u32[]{:S(2)}) collective-permute-start(bf16[48,2048]{1,0:T(8,128)(2,1)S(1)} %get-tuple-element.86), channel_id=1, source_target_pairs={{0,2},{1,3},{2,0},{3,1},{4,6},{5,7},{6,4},{7,5},{8,10},{9,11},{10,... | collective-permute-start | bytes 589832 | tf_op jit(solution)/shard_map/ppermute | solution.py:278
  46.9 8.8 %collective-permute-start.31 = (bf16[24,2048]{1,0:T(8,128)(2,1)S(1)}, bf16[24,2048]{1,0:T(8,128)(2,1)S(1)}, u32[]{:S(2)}, u32[]{:S(2)}) collective-permute-start(bf16[24,2048]{1,0:T(8,128)(2,1)S(1)} %copy-done.13), channel_id=1, source_target_pairs={{0,4},{1,5},{2,6},{3,7},{4,0},{5,1},{6,2},{7,3},{8,12},{9,13},{10,... | collective-permute-start | bytes 294920 | tf_op jit(solution)/shard_map/ppermute | solution.py:278
  47.7 10.4 %collective-permute-start.32 = (bf16[24,2048]{1,0:T(8,128)(2,1)S(1)}, bf16[24,2048]{1,0:T(8,128)(2,1)S(1)}, u32[]{:S(2)}, u32[]{:S(2)}) collective-permute-start(bf16[24,2048]{1,0:T(8,128)(2,1)S(1)} %copy-done.12), channel_id=1, source_target_pairs={{0,8},{1,9},{2,10},{3,11},{4,12},{5,13},{6,14},{7,15},{8,0},{9,1},... | collective-permute-start | bytes 294920 | tf_op jit(solution)/shard_map/ppermute | solution.py:278
  49.9 8.2 %collective-permute-start.33 = (bf16[24,2048]{1,0:T(8,128)(2,1)S(1)}, bf16[24,2048]{1,0:T(8,128)(2,1)S(1)}, u32[]{:S(2)}, u32[]{:S(2)}) collective-permute-start(bf16[24,2048]{1,0:T(8,128)(2,1)S(1)} %copy-done.11), channel_id=1, source_target_pairs={{0,12},{1,13},{2,14},{3,15},{4,8},{5,9},{6,10},{7,11},{8,4},{9,5},... | collective-permute-start | bytes 294920 | tf_op jit(solution)/shard_map/ppermute | solution.py:278
  51.6 6.9 %collective-permute-start.5 = (f32[16,128]{1,0:T(8,128)S(1)}, f32[16,128]{1,0:T(8,128)S(1)}, u32[]{:S(2)}, u32[]{:S(2)}) collective-permute-start(f32[16,128]{1,0:T(8,128)S(1)} %copy-done.14), channel_id=1, source_target_pairs={{0,16},{16,0},{1,17},{17,1},{2,18},{18,2},{3,19},{19,3},{4,20},{20... | collective-permute-start | bytes 24584 | tf_op jit(solution)/shard_map/ppermute | solution.py:368
  53.7 10.4 %collective-permute-start.19 = (bf16[24,2048]{1,0:T(8,128)(2,1)S(1)}, bf16[24,2048]{1,0:T(8,128)(2,1)S(1)}, u32[]{:S(2)}, u32[]{:S(2)}) collective-permute-start(bf16[24,2048]{1,0:T(8,128)(2,1)S(1)} %get-tuple-element.83), channel_id=1, source_target_pairs={{0,8},{1,9},{2,10},{3,11},{4,12},{5,13},{6,14},{7,15},{8,0},{9,1},... | collective-permute-start | bytes 294920 | tf_op jit(solution)/shard_map/ppermute | solution.py:278
  55.7 9.7 %collective-permute-start.20 = (bf16[24,2048]{1,0:T(8,128)(2,1)S(1)}, bf16[24,2048]{1,0:T(8,128)(2,1)S(1)}, u32[]{:S(2)}, u32[]{:S(2)}) collective-permute-start(bf16[24,2048]{1,0:T(8,128)(2,1)S(1)} %get-tuple-element.84), channel_id=1, source_target_pairs={{0,12},{1,13},{2,14},{3,15},{4,8},{5,9},{6,10},{7,11},{8,4},{9,5},... | collective-permute-start | bytes 294920 | tf_op jit(solution)/shard_map/ppermute | solution.py:278
  58.1 7.3 %collective-permute-start.22 = (bf16[24,2048]{1,0:T(8,128)(2,1)S(1)}, bf16[24,2048]{1,0:T(8,128)(2,1)S(1)}, u32[]{:S(2)}, u32[]{:S(2)}) collective-permute-start(bf16[24,2048]{1,0:T(8,128)(2,1)S(1)} %get-tuple-element.87), channel_id=1, source_target_pairs={{0,4},{1,5},{2,6},{3,7},{4,0},{5,1},{6,2},{7,3},{8,12},{9,13},{10,... | collective-permute-start | bytes 294920 | tf_op jit(solution)/shard_map/ppermute | solution.py:278
  58.1 13.1 %collective-permute-start.34 = (bf16[24,2048]{1,0:T(8,128)(2,1)S(1)}, bf16[24,2048]{1,0:T(8,128)(2,1)S(1)}, u32[]{:S(2)}, u32[]{:S(2)}) collective-permute-start(bf16[24,2048]{1,0:T(8,128)(2,1)S(1)} %collective-permute-done.32.refs_0_), channel_id=1, source_target_pairs={{0,2},{1,3},{2,0},{3,1},{4,6},{5,7},{6,4},{7,5},{8,10},{9,11},{10,... | collective-permute-start | bytes 294920 | tf_op jit(solution)/shard_map/ppermute | solution.py:278
  58.6 14.0 %collective-permute-start.35 = (bf16[24,2048]{1,0:T(8,128)(2,1)S(1)}, bf16[24,2048]{1,0:T(8,128)(2,1)S(1)}, u32[]{:S(2)}, u32[]{:S(2)}) collective-permute-start(bf16[24,2048]{1,0:T(8,128)(2,1)S(1)} %collective-permute-done.33.refs_1_), channel_id=1, source_target_pairs={{0,2},{1,3},{2,0},{3,1},{4,6},{5,7},{6,4},{7,5},{8,10},{9,11},{10,... | collective-permute-start | bytes 294920 | tf_op jit(solution)/shard_map/ppermute | solution.py:278
  64.1 9.0 %collective-permute-start.36 = (bf16[24,2048]{1,0:T(8,128)(2,1)S(1)}, bf16[24,2048]{1,0:T(8,128)(2,1)S(1)}, u32[]{:S(2)}, u32[]{:S(2)}) collective-permute-start(bf16[24,2048]{1,0:T(8,128)(2,1)S(1)} %collective-permute-done.31.refs_2_), channel_id=1, source_target_pairs={{0,2},{1,3},{2,0},{3,1},{4,6},{5,7},{6,4},{7,5},{8,10},{9,11},{10,... | collective-permute-start | bytes 294920 | tf_op jit(solution)/shard_map/ppermute | solution.py:278
  67.1 8.6 %collective-permute-start.23 = (bf16[24,2048]{1,0:T(8,128)(2,1)S(1)}, bf16[24,2048]{1,0:T(8,128)(2,1)S(1)}, u32[]{:S(2)}, u32[]{:S(2)}) collective-permute-start(bf16[24,2048]{1,0:T(8,128)(2,1)S(1)} %get-tuple-element.90), channel_id=1, source_target_pairs={{0,24},{1,25},{2,26},{3,27},{4,28},{5,29},{6,30},{7,31},{8,16},{9,... | collective-permute-start | bytes 294920 | tf_op jit(solution)/shard_map/ppermute | solution.py:392
  69.6 7.5 %collective-permute-start.24 = (bf16[24,2048]{1,0:T(8,128)(2,1)S(1)}, bf16[24,2048]{1,0:T(8,128)(2,1)S(1)}, u32[]{:S(2)}, u32[]{:S(2)}) collective-permute-start(bf16[24,2048]{1,0:T(8,128)(2,1)S(1)} %get-tuple-element.91), channel_id=1, source_target_pairs={{0,28},{1,29},{2,30},{3,31},{4,24},{5,25},{6,26},{7,27},{8,20},{9,... | collective-permute-start | bytes 294920 | tf_op jit(solution)/shard_map/ppermute | solution.py:392
  71.2 7.2 %collective-permute-start.25 = (bf16[24,2048]{1,0:T(8,128)(2,1)S(1)}, bf16[24,2048]{1,0:T(8,128)(2,1)S(1)}, u32[]{:S(2)}, u32[]{:S(2)}) collective-permute-start(bf16[24,2048]{1,0:T(8,128)(2,1)S(1)} %get-tuple-element.92), channel_id=1, source_target_pairs={{0,20},{1,21},{2,22},{3,23},{4,16},{5,17},{6,18},{7,19},{8,28},{9,... | collective-permute-start | bytes 294920 | tf_op jit(solution)/shard_map/ppermute | solution.py:392
  72.6 6.6 %collective-permute-start.26 = (bf16[24,2048]{1,0:T(8,128)(2,1)S(1)}, bf16[24,2048]{1,0:T(8,128)(2,1)S(1)}, u32[]{:S(2)}, u32[]{:S(2)}) collective-permute-start(bf16[24,2048]{1,0:T(8,128)(2,1)S(1)} %get-tuple-element.93), channel_id=1, source_target_pairs={{0,16},{1,17},{2,18},{3,19},{4,20},{5,21},{6,22},{7,23},{8,24},{9,... | collective-permute-start | bytes 294920 | tf_op jit(solution)/shard_map/ppermute | solution.py:392
  73.1 7.4 %collective-permute-start.37 = (bf16[24,2048]{1,0:T(8,128)(2,1)S(1)}, bf16[24,2048]{1,0:T(8,128)(2,1)S(1)}, u32[]{:S(2)}, u32[]{:S(2)}) collective-permute-start(bf16[24,2048]{1,0:T(8,128)(2,1)S(1)} %copy-done.5), channel_id=1, source_target_pairs={{0,2},{1,3},{2,0},{3,1},{4,6},{5,7},{6,4},{7,5},{8,10},{9,11},{10,... | collective-permute-start | bytes 294920 | tf_op jit(solution)/shard_map/ppermute | solution.py:278
  75.7 7.4 %collective-permute-start.27 = (bf16[24,2048]{1,0:T(8,128)(2,1)S(1)}, bf16[24,2048]{1,0:T(8,128)(2,1)S(1)}, u32[]{:S(2)}, u32[]{:S(2)}) collective-permute-start(bf16[24,2048]{1,0:T(8,128)(2,1)S(1)} %collective-permute-done.23.refs_0_), channel_id=1, source_target_pairs={{0,2},{1,3},{2,0},{3,1},{4,6},{5,7},{6,4},{7,5},{8,10},{9,11},{10,... | collective-permute-start | bytes 294920 | tf_op jit(solution)/shard_map/ppermute | solution.py:278
  77.1 6.0 %collective-permute-start.28 = (bf16[24,2048]{1,0:T(8,128)(2,1)S(1)}, bf16[24,2048]{1,0:T(8,128)(2,1)S(1)}, u32[]{:S(2)}, u32[]{:S(2)}) collective-permute-start(bf16[24,2048]{1,0:T(8,128)(2,1)S(1)} %collective-permute-done.24.refs_1_), channel_id=1, source_target_pairs={{0,2},{1,3},{2,0},{3,1},{4,6},{5,7},{6,4},{7,5},{8,10},{9,11},{10,... | collective-permute-start | bytes 294920 | tf_op jit(solution)/shard_map/ppermute | solution.py:278
  78.4 5.6 %collective-permute-start.29 = (bf16[24,2048]{1,0:T(8,128)(2,1)S(1)}, bf16[24,2048]{1,0:T(8,128)(2,1)S(1)}, u32[]{:S(2)}, u32[]{:S(2)}) collective-permute-start(bf16[24,2048]{1,0:T(8,128)(2,1)S(1)} %collective-permute-done.25.refs_2_), channel_id=1, source_target_pairs={{0,2},{1,3},{2,0},{3,1},{4,6},{5,7},{6,4},{7,5},{8,10},{9,11},{10,... | collective-permute-start | bytes 294920 | tf_op jit(solution)/shard_map/ppermute | solution.py:278
  79.1 5.9 %collective-permute-start.30 = (bf16[24,2048]{1,0:T(8,128)(2,1)S(1)}, bf16[24,2048]{1,0:T(8,128)(2,1)S(1)}, u32[]{:S(2)}, u32[]{:S(2)}) collective-permute-start(bf16[24,2048]{1,0:T(8,128)(2,1)S(1)} %collective-permute-done.26.refs_3_), channel_id=1, source_target_pairs={{0,2},{1,3},{2,0},{3,1},{4,6},{5,7},{6,4},{7,5},{8,10},{9,11},{10,... | collective-permute-start | bytes 294920 | tf_op jit(solution)/shard_map/ppermute | solution.py:278
  83.1 23.3 %copy-start.10 = (s32[1,128,8]{1,2,0:T(8,128)S(1)}, s32[1,128,8]{1,2,0:T(8,128)}, u32[]{:S(2)}) copy-start(s32[1,128,8]{1,2,0:T(8,128)} %param.17) | copy-start | bytes 12292
  90.7 6.4 %collective-permute-start.38 = (bf16[48,2048]{1,0:T(8,128)(2,1)S(1)}, bf16[48,2048]{1,0:T(8,128)(2,1)S(1)}, u32[]{:S(2)}, u32[]{:S(2)}) collective-permute-start(bf16[48,2048]{1,0:T(8,128)(2,1)S(1)} %get-tuple-element.107), channel_id=1, source_target_pairs={{0,2},{1,3},{2,0},{3,1},{4,6},{5,7},{6,4},{7,5},{8,10},{9,11},{10,... | collective-permute-start | bytes 589832 | tf_op jit(solution)/shard_map/ppermute | solution.py:278
  91.9 8.7 %collective-permute-start.41 = (bf16[48,2048]{1,0:T(8,128)(2,1)S(1)}, bf16[48,2048]{1,0:T(8,128)(2,1)S(1)}, u32[]{:S(2)}, u32[]{:S(2)}) collective-permute-start(bf16[48,2048]{1,0:T(8,128)(2,1)S(1)} %get-tuple-element.111), channel_id=1, source_target_pairs={{0,2},{1,3},{2,0},{3,1},{4,6},{5,7},{6,4},{7,5},{8,10},{9,11},{10,... | collective-permute-start | bytes 589832 | tf_op jit(solution)/shard_map/ppermute | solution.py:278
  97.2 6.6 %collective-permute-start.39 = (bf16[24,2048]{1,0:T(8,128)(2,1)S(1)}, bf16[24,2048]{1,0:T(8,128)(2,1)S(1)}, u32[]{:S(2)}, u32[]{:S(2)}) collective-permute-start(bf16[24,2048]{1,0:T(8,128)(2,1)S(1)} %get-tuple-element.108), channel_id=1, source_target_pairs={{0,8},{1,9},{2,10},{3,11},{4,12},{5,13},{6,14},{7,15},{8,0},{9,1},... | collective-permute-start | bytes 294920 | tf_op jit(solution)/shard_map/ppermute | solution.py:278
  98.8 6.6 %collective-permute-start.40 = (bf16[24,2048]{1,0:T(8,128)(2,1)S(1)}, bf16[24,2048]{1,0:T(8,128)(2,1)S(1)}, u32[]{:S(2)}, u32[]{:S(2)}) collective-permute-start(bf16[24,2048]{1,0:T(8,128)(2,1)S(1)} %get-tuple-element.109), channel_id=1, source_target_pairs={{0,12},{1,13},{2,14},{3,15},{4,8},{5,9},{6,10},{7,11},{8,4},{9,5},... | collective-permute-start | bytes 294920 | tf_op jit(solution)/shard_map/ppermute | solution.py:278
  100.6 5.7 %collective-permute-start.42 = (bf16[24,2048]{1,0:T(8,128)(2,1)S(1)}, bf16[24,2048]{1,0:T(8,128)(2,1)S(1)}, u32[]{:S(2)}, u32[]{:S(2)}) collective-permute-start(bf16[24,2048]{1,0:T(8,128)(2,1)S(1)} %get-tuple-element.112), channel_id=1, source_target_pairs={{0,4},{1,5},{2,6},{3,7},{4,0},{5,1},{6,2},{7,3},{8,12},{9,13},{10,... | collective-permute-start | bytes 294920 | tf_op jit(solution)/shard_map/ppermute | solution.py:278
  (10 other events, 54.2 us)

commit v4 on v3

--- a/solution.py
+++ b/solution.py
@@ -131,13 +131,11 @@
 
 def relay(window, cap, ids_ref, keys_ref, grad_last_ref, *refs):
     topk = ids_ref.shape[0]
-    blocks, dx_ref, out_refs = refs[:window], refs[window], refs[window + 1 : -2]
+    blocks, out_refs = refs[:window], refs[window:-2]
     grad_buf, sems = refs[-2:]
     copies = fetch(row_parts(grad_last_ref, grad_buf), sems)
     left, right = scattered(ids_ref, window, cap, blocks)
     half = left.shape[1]
-    dx_ref[0, :, :half] = left
-    dx_ref[0, :, half:] = right
     top, bot, coef = tables(
         keys_ref[:topk].astype(jnp.int32), window, cap, keys_ref[topk:]
     )
@@ -155,7 +153,7 @@
 
 
 def finish(window, cap, ids_ref, *refs):
-    blocks, dx_ref = refs[:window], refs[window]
+    blocks, dx_ref = refs[:window], refs[-1]
     left, right = scattered(ids_ref, window, cap, blocks)
     half = left.shape[1]
     dx_ref[0, :, :half] = left
@@ -298,14 +296,17 @@
     )
     ring = [(s, (s + 1) % sections) for s in range(sections)]
 
-    def listed(by_k):
-        return [by_k[k] for k in order]
+    def listed(by_k, ks=order):
+        return [by_k[k] for k in ks]
+
+    far_order = order[-2:] + order[:-2]
+    x_far_order = order[-2:] + order[:-2]
 
     def forward(near, far, *extra):
         return call(
             functools.partial(unit_x, 2 * window, cap),
             shape((4, 2 * rows, w_gate.shape[3]), F32),
-            (*listed(near), *listed(far), weights[0], weights[1], weights[3], weights[4], *extra),
+            (*listed(near), *listed(far, far_order), weights[0], weights[1], weights[3], weights[4], *extra),
             COMPUTE_MIB,
             away=range(2 * window, 2 * window + 4 + len(extra)),
             scratch=[bufs[0], bufs[1], bufs[3], bufs[4], dma((4,))],
@@ -315,22 +316,39 @@
     groups = [order[:-2], order[-2:]] if window > 2 else [order]
     heights = [2 * cap * len(g) for g in groups]
 
-    def backward(near, far, scales):
+    def backward(near, far, scales, *held):
         made = call(
             functools.partial(unit_grad, 2 * window, cap),
-            [shape((h, half), F32) for h in heights] + [shape((h, half), BF16) for h in heights],
-            (*listed(near), *listed(far), scales, *weights),
+            [shape((h, half), F32) for h in heights]
+            + [shape((h, half), BF16) for h in heights[::-1]],
+            (*listed(near), *listed(far, far_order), scales, *weights),
             COMPUTE_MIB,
             away=range(2 * window + 1, 2 * window + 7),
             scratch=[*bufs, dma((6,))],
             us=5.7,
         )
+        own, far = made[: len(groups)], list(made[len(groups) :][::-1])
+        if held:
+            far, held = after((far, *held))
         back = {}
-        for group, own, far in zip(groups, made, made[len(groups) :]):
-            far = across(far)
-            sums = call(functools.partial(add_far, cap), [msg] * len(group), (own, far), 8)
+        for group, near_rows, far_rows in zip(groups, own, far):
+            far_rows = across(far_rows)
+            sums = call(
+                functools.partial(add_far, cap), [msg] * len(group), (near_rows, far_rows), 8
+            )
             back.update({k: plane(sums[j], k) for j, k in enumerate(group)})
-        return far, listed(back)
+        return far_rows, listed(back), held
+
+
+    def ended(ids, back, *extra):
+        return call(
+            functools.partial(finish, window, cap),
+            shape((1, tok, width), BF16),
+            (ids, *back, *extra),
+            16,
+            away=range(1 + window, 1 + window + len(extra)),
+            us=1.6,
+        )
 
     x_1 = call(
         functools.partial(pack_x, window, cap),
@@ -359,29 +377,31 @@
     grad_1, peer_w = after((grad_1, peer_w))
     weights = (*own_w, *peer_w)
     near_g = {k: plane(grad_1[k], k) for k in outer}
-    inner = [(x_1[k], grad_1[k]) for k in (1, 0)]
-    near_x, inner, keys = after((near_x, inner, keys))
-    for k, (x, grad) in zip((1, 0), inner):
-        near_x[k] = plane(x, k)
-        near_g[k] = plane(grad, k)
-    far_x = {k: across(near_x[k]) for k in (0, 1, *outer)}
+    near_x[0], near_g[0] = after((x_1[0], grad_1[0]))
+    far_x = {0: across(near_x[0])}
+    near_x, x_in, grad_in, keys = after((near_x, x_1[1], grad_1[1], keys))
+    near_x[1], near_g[1] = plane(x_in, 1), plane(grad_in, 1)
+    far_x.update({k: across(near_x[k]) for k in (1, *outer)})
     keys = lax.ppermute(keys, "pipe", ring)
-    x_2 = after((near_g, x_2))[1]
+    scales = forward(near_x, far_x)
+    x_2 = after((near_g, x_2, scales))[1]
     far_g = {k: across(near_g[k]) for k in (0, 1, *outer)}
-    near_x2 = {k: plane(x_2[k], k) for k in order}
-    arrived, back = backward(near_g, far_g, forward(near_x, far_x))
-    near_x2 = after((near_x2, arrived))[0]
+    near_x2 = {k: plane(x_2[k], k) for k in order if k > 1}
+    arrived, back, near_x2 = backward(near_g, far_g, scales, near_x2)
+    near_x2, x_in = after((near_x2, [x_2[1], x_2[0]], arrived))[:2]
+    near_x2[1], near_x2[0] = plane(x_in[0], 1), x_in[1]
     far_x2 = {k: across(near_x2[k]) for k in order}
     scales = forward(near_x2, far_x2)
-    dx_first, *grads = call(
+    grads = call(
         functools.partial(relay, window, cap),
-        [shape((1, tok, width), BF16)] + [msg] * window,
+        [msg] * window,
         (ids_1, keys, grad_last, *back),
         16,
         away=(2,),
         scratch=[row_buf, dma((4,))],
         us=1.8,
     )
+    dx_first = ended(ids_1, back, grads[0])
     near = {}
     for j, k in enumerate(order):
         pairs = [
@@ -390,14 +410,9 @@
             for i in range(devices)
         ]
         near[k] = lax.ppermute(grads[j], ("pipe", "expert"), pairs)
-    far = {k: across(near[k]) for k in order[::-1]}
-    _, back = backward(near, far, scales)
-    dx_second = call(
-        functools.partial(finish, window, cap),
-        shape((1, tok, width), BF16),
-        (ids_2, *back),
-        16,
-    )
+    far = {k: across(near[k]) for k in far_order}
+    _, back, _ = backward(near, far, scales)
+    dx_second = ended(ids_2, back)
     return dx_first, dx_second
 
 

time: 108 us -> 104 us (0.963)
  waiting for transfers between devices: 27.7 us -> 23.3 us
    ppermute x38, waiting for transfers between devices: 25.3 us -> 22.3 us  [send(): return lax.ppermute(x, 'expert', [(i, i ^ bits) for i in range(devices)])]
    ppermute x4, waiting for transfers between devices: 2.41 us -> 1.03 us  [body(): near[k] = lax.ppermute(grads[j], ('pipe', 'expert'), pairs)]
    pallas_call x12 -> x13, Pallas kernels: 24.3 us -> 25.1 us  [call(): pl.pallas_call(body, out_shape=outs, in_specs=[pl.BlockSpec(memory_space=...]
  transfers between devices with their start and end apart: 43 -> 43, of which waited for: 16 -> 13; matrix products, arithmetic and copies ran while one was open for 0% -> 0% of each run, Pallas kernels for 11% -> 17%
where the time goes in v4:
time: 104 us
  starting transfers between devices  51.1 us (49%)
  Pallas kernels  25.1 us (24%)
  waiting for transfers between devices  23.3 us (22%)
  local copies, waits for them, and re-layouts  3.56 us (3%)
    ppermute x38, starting transfers between devices, send(): return lax.ppermute(x, 'expert', [(i, i ^ bits) for i in range(devices)])  43.5 us
    pallas_call x13, Pallas kernels, call(): pl.pallas_call(body, out_shape=outs, in_specs=[pl.BlockSpec(memory_space=...  25.1 us
    ppermute x38, waiting for transfers between devices, send(): return lax.ppermute(x, 'expert', [(i, i ^ bits) for i in range(devices)])  22.3 us
    ppermute x4, starting transfers between devices, body(): near[k] = lax.ppermute(grads[j], ('pipe', 'expert'), pairs)  6.18 us
    unnamed x30, local copies, waits for them, and re-layouts  3.56 us
  transfers between devices with their start and end apart: 43, of which 13 were waited for; matrix products, arithmetic and copies ran while one was open for 0% of the time, Pallas kernels for 17%

profile of v4, /device:TPU:0, one launch (start us, length us, event | category | flops | bytes accessed | tf_op | source)
XLA Modules:
  0.0 104.1 jit_solution(13900447759659094692)
XLA Ops:
  1.7 1.2 %copy-done.3 = bf16[1,128,4096]{2,1,0:T(8,128)(2,1)S(1)} copy-done((bf16[1,128,4096]{2,1,0:T(8,128)(2,1)S(1)}, bf16[1,128,4096]{2,1,0:T(8,128)(2,1)}, u32[]{:S(2)}) %copy-start.3) | copy-done | bytes 1048600
  4.2 4.7 %collective-permute-start.6 = (bf16[24,2048]{1,0:T(8,128)(2,1)S(1)}, bf16[24,2048]{1,0:T(8,128)(2,1)S(1)}, u32[]{:S(2)}, u32[]{:S(2)}) collective-permute-start(bf16[24,2048]{1,0:T(8,128)(2,1)S(1)} %get-tuple-element.72), channel_id=1, source_target_pairs={{0,12},{1,13},{2,14},{3,15},{4,8},{5,9},{6,10},{7,11},{8,4},{9,5},... | collective-permute-start | bytes 294920 | tf_op jit(solution)/shard_map/ppermute | solution.py:276
  9.0 3.5 %shard_map.123 = (f32[16,128]{1,0:T(8,128)}, bf16[24,2048]{1,0:T(8,128)(2,1)}, bf16[24,2048]{1,0:T(8,128)(2,1)}, bf16[24,2048]{1,0:T(8,128)(2,1)}, bf16[24,2048]...) custom-call(s32[8,128]{1,0:T(8,128)} %bitcast.32, ...), custom_call_target="tpu_custom_call" | custom-call | bytes 18000000 | tf_op jit(solution)/shard_map/pallas_call | solution.py:19
  12.7 5.1 %collective-permute-done.5.refs_0_ = bf16[24,2048]{1,0:T(8,128)(2,1)S(1)} collective-permute-done((bf16[24,2048]{1,0:T(8,128)(2,1)S(1)}, bf16[24,2048]{1,0:T(8,128)(2,1)S(1)}, u32[]{:S(2)}, u32[]{:S(2)}) %collective-permute-start.5) | collective-permute-done | bytes 98336 | tf_op jit(solution)/shard_map/ppermute | solution.py:276
  17.8 2.0 %collective-permute-start.12 = (bf16[24,2048]{1,0:T(8,128)(2,1)S(1)}, bf16[24,2048]{1,0:T(8,128)(2,1)S(1)}, u32[]{:S(2)}, u32[]{:S(2)}) collective-permute-start(bf16[24,2048]{1,0:T(8,128)(2,1)S(1)} %get-tuple-element.80), channel_id=1, source_target_pairs={{0,4},{1,5},{2,6},{3,7},{4,0},{5,1},{6,2},{7,3},{8,12},{9,13},{10,... | collective-permute-start | bytes 294920 | tf_op jit(solution)/shard_map/ppermute | solution.py:276
  19.9 1.5 %collective-permute-start.15 = (bf16[24,2048]{1,0:T(8,128)(2,1)S(1)}, bf16[24,2048]{1,0:T(8,128)(2,1)S(1)}, u32[]{:S(2)}, u32[]{:S(2)}) collective-permute-start(bf16[24,2048]{1,0:T(8,128)(2,1)S(1)} %collective-permute-done.5.refs_0_), channel_id=1, source_target_pairs={{0,2},{1,3},{2,0},{3,1},{4,6},{5,7},{6,4},{7,5},{8,10},{9,11},{10,... | collective-permute-start | bytes 294920 | tf_op jit(solution)/shard_map/ppermute | solution.py:276
  21.9 1.5 %collective-permute-start.14 = (bf16[24,2048]{1,0:T(8,128)(2,1)S(1)}, bf16[24,2048]{1,0:T(8,128)(2,1)S(1)}, u32[]{:S(2)}, u32[]{:S(2)}) collective-permute-start(bf16[24,2048]{1,0:T(8,128)(2,1)S(1)} %get-tuple-element.81.refs_3_), channel_id=1, source_target_pairs={{0,2},{1,3},{2,0},{3,1},{4,6},{5,7},{6,4},{7,5},{8,10},{9,11},{10,... | collective-permute-start | bytes 294920 | tf_op jit(solution)/shard_map/ppermute | solution.py:276
  23.5 1.1 %collective-permute-start.3 = (bf16[24,2048]{1,0:T(8,128)(2,1)}, bf16[24,2048]{1,0:T(8,128)(2,1)S(1)}, u32[]{:S(2)}, u32[]{:S(2)}) collective-permute-start(bf16[24,2048]{1,0:T(8,128)(2,1)} %get-tuple-element.67), channel_id=1, source_target_pairs={{0,8},{1,9},{2,10},{3,11},{4,12},{5,13},{6,14},{7,15},{8,0},{9,1},... | collective-permute-start | bytes 294920 | tf_op jit(solution)/shard_map/ppermute | solution.py:276
  24.5 2.4 %collective-permute-start.4 = (bf16[24,2048]{1,0:T(8,128)(2,1)}, bf16[24,2048]{1,0:T(8,128)(2,1)S(1)}, u32[]{:S(2)}, u32[]{:S(2)}) collective-permute-start(bf16[24,2048]{1,0:T(8,128)(2,1)} %get-tuple-element.68), channel_id=1, source_target_pairs={{0,12},{1,13},{2,14},{3,15},{4,8},{5,9},{6,10},{7,11},{8,4},{9,5},... | collective-permute-start | bytes 294920 | tf_op jit(solution)/shard_map/ppermute | solution.py:276
  27.0 1.5 %collective-permute-start.13 = (bf16[24,2048]{1,0:T(8,128)(2,1)S(1)}, bf16[24,2048]{1,0:T(8,128)(2,1)S(1)}, u32[]{:S(2)}, u32[]{:S(2)}) collective-permute-start(bf16[24,2048]{1,0:T(8,128)(2,1)S(1)} %collective-permute-done.12.refs_2_), channel_id=1, source_target_pairs={{0,2},{1,3},{2,0},{3,1},{4,6},{5,7},{6,4},{7,5},{8,10},{9,11},{10,... | collective-permute-start | bytes 294920 | tf_op jit(solution)/shard_map/ppermute | solution.py:276
  29.0 1.5 %collective-permute-start.8 = (bf16[24,2048]{1,0:T(8,128)(2,1)S(1)}, bf16[24,2048]{1,0:T(8,128)(2,1)S(1)}, u32[]{:S(2)}, u32[]{:S(2)}) collective-permute-start(bf16[24,2048]{1,0:T(8,128)(2,1)S(1)} %collective-permute-done.7.refs_2_), channel_id=1, source_target_pairs={{0,2},{1,3},{2,0},{3,1},{4,6},{5,7},{6,4},{7,5},{8,10},{9,11},{10,... | collective-permute-start | bytes 294920 | tf_op jit(solution)/shard_map/ppermute | solution.py:276
  30.6 2.0 %collective-permute-done.3.refs_0_ = bf16[24,2048]{1,0:T(8,128)(2,1)S(1)} collective-permute-done((bf16[24,2048]{1,0:T(8,128)(2,1)}, bf16[24,2048]{1,0:T(8,128)(2,1)S(1)}, u32[]{:S(2)}, u32[]{:S(2)}) %collective-permute-start.3) | collective-permute-done | bytes 98336 | tf_op jit(solution)/shard_map/ppermute | solution.py:276
  32.6 1.2 %collective-permute-start.10 = (bf16[24,2048]{1,0:T(8,128)(2,1)S(1)}, bf16[24,2048]{1,0:T(8,128)(2,1)S(1)}, u32[]{:S(2)}, u32[]{:S(2)}) collective-permute-start(bf16[24,2048]{1,0:T(8,128)(2,1)S(1)} %collective-permute-done.3.refs_0_), channel_id=1, source_target_pairs={{0,2},{1,3},{2,0},{3,1},{4,6},{5,7},{6,4},{7,5},{8,10},{9,11},{10,... | collective-permute-start | bytes 294920 | tf_op jit(solution)/shard_map/ppermute | solution.py:276
  34.6 1.6 %copy-done.1 = bf16[1,1,4096,256]{3,2,1,0:T(8,128)(2,1)S(1)} copy-done((bf16[1,1,4096,256]{3,2,1,0:T(8,128)(2,1)S(1)}, bf16[1,1,4096,256]{3,2,1,0:T(8,128)(2,1)}, u32[]{:S(2)}) %copy-start.1) | copy-done | bytes 2097176
  36.2 2.7 %shard_map.124.refs_8_ = f32[4,192,256]{2,1,0:T(8,128)S(1)} custom-call(bf16[24,2048]{1,0:T(8,128)(2,1)S(1)} %collective-permute-done.5.refs_0_, bf16[24,2048]{1,0:T(8,128)(2,1)S(1)} %collective-permute-done.6.refs_1_, bf16[24,2048]{1,0:T(8,128)(2,1)S(1)} %collective-permute-done.12.refs_2_, bf16[24,2048]{1,0:T(8,128)(2,1)S(1)} %get-tuple-element.81.refs_3_, ...), custom_call_target="tpu_custom_call" | custom-call | bytes 9720000 | tf_op jit(solution)/shard_map/pallas_call | solution.py:19
  39.0 1.8 %collective-permute-start.17 = (bf16[24,2048]{1,0:T(8,128)(2,1)S(1)}, bf16[24,2048]{1,0:T(8,128)(2,1)S(1)}, u32[]{:S(2)}, u32[]{:S(2)}) collective-permute-start(bf16[24,2048]{1,0:T(8,128)(2,1)S(1)} %copy-done.13), channel_id=1, source_target_pairs={{0,8},{1,9},{2,10},{3,11},{4,12},{5,13},{6,14},{7,15},{8,0},{9,1},... | collective-permute-start | bytes 294920 | tf_op jit(solution)/shard_map/ppermute | solution.py:276
  40.8 1.3 %collective-permute-start.18 = (bf16[24,2048]{1,0:T(8,128)(2,1)S(1)}, bf16[24,2048]{1,0:T(8,128)(2,1)S(1)}, u32[]{:S(2)}, u32[]{:S(2)}) collective-permute-start(bf16[24,2048]{1,0:T(8,128)(2,1)S(1)} %copy-done.12), channel_id=1, source_target_pairs={{0,12},{1,13},{2,14},{3,15},{4,8},{5,9},{6,10},{7,11},{8,4},{9,5},... | collective-permute-start | bytes 294920 | tf_op jit(solution)/shard_map/ppermute | solution.py:276
  42.2 5.6 %shard_map.125 = (f32[48,2048]{1,0:T(8,128)S(1)}, f32[48,2048]{1,0:T(8,128)S(1)}, bf16[48,2048]{1,0:T(8,128)(2,1)S(1)}, bf16[48,2048]{1,0:T(8,128)(2,1)S(1)}) custom-call(bf16[24,2048]{1,0:T(8,128)(2,1)S(1)} %collective-permute-done.3.refs_0_, bf16[24,2048]{1,0:T(8,128)(2,1)S(1)} %collective-permute-done.4.refs_1_, ...), custom_call_target="tpu_custom_call" | custom-call | bytes 20520000 | tf_op jit(solution)/shard_map/pallas_call | solution.py:19
  47.8 0.9 collective-permute-start.19
  48.7 1.2 %collective-permute-start.22 = (bf16[48,2048]{1,0:T(8,128)(2,1)S(1)}, bf16[48,2048]{1,0:T(8,128)(2,1)S(1)}, u32[]{:S(2)}, u32[]{:S(2)}) collective-permute-start(bf16[48,2048]{1,0:T(8,128)(2,1)S(1)} %get-tuple-element.98), channel_id=1, source_target_pairs={{0,2},{1,3},{2,0},{3,1},{4,6},{5,7},{6,4},{7,5},{8,10},{9,11},{10,... | collective-permute-start | bytes 589832 | tf_op jit(solution)/shard_map/ppermute | solution.py:276
  49.9 4.2 %collective-permute-done.19.far_ref = bf16[48,2048]{1,0:T(8,128)(2,1)S(1)} collective-permute-done((bf16[48,2048]{1,0:T(8,128)(2,1)S(1)}, bf16[48,2048]{1,0:T(8,128)(2,1)S(1)}, u32[]{:S(2)}, u32[]{:S(2)}) %collective-permute-start.19) | collective-permute-done | bytes 196640 | tf_op jit(solution)/shard_map/ppermute | solution.py:276
  55.0 1.5 %collective-permute-start.24 = (f32[16,128]{1,0:T(8,128)S(1)}, f32[16,128]{1,0:T(8,128)S(1)}, u32[]{:S(2)}, u32[]{:S(2)}) collective-permute-start(f32[16,128]{1,0:T(8,128)S(1)} %copy-done.14), channel_id=1, source_target_pairs={{0,16},{16,0},{1,17},{17,1},{2,18},{18,2},{3,19},{19,3},{4,20},{20... | collective-permute-start | bytes 24584 | tf_op jit(solution)/shard_map/ppermute | solution.py:385
  56.5 1.9 %collective-permute-start.21 = (bf16[24,2048]{1,0:T(8,128)(2,1)S(1)}, bf16[24,2048]{1,0:T(8,128)(2,1)S(1)}, u32[]{:S(2)}, u32[]{:S(2)}) collective-permute-start(bf16[24,2048]{1,0:T(8,128)(2,1)S(1)} %get-tuple-element.96), channel_id=1, source_target_pairs={{0,12},{1,13},{2,14},{3,15},{4,8},{5,9},{6,10},{7,11},{8,4},{9,5},... | collective-permute-start | bytes 294920 | tf_op jit(solution)/shard_map/ppermute | solution.py:276
  58.4 0.9 collective-permute-start.23
  59.3 1.2 %collective-permute-start.33 = (bf16[24,2048]{1,0:T(8,128)(2,1)S(1)}, bf16[24,2048]{1,0:T(8,128)(2,1)S(1)}, u32[]{:S(2)}, u32[]{:S(2)}) collective-permute-start(bf16[24,2048]{1,0:T(8,128)(2,1)S(1)} %copy-done.11), channel_id=1, source_target_pairs={{0,4},{1,5},{2,6},{3,7},{4,0},{5,1},{6,2},{7,3},{8,12},{9,13},{10,... | collective-permute-start | bytes 294920 | tf_op jit(solution)/shard_map/ppermute | solution.py:276
  60.5 1.0 collective-permute-start.36
  61.5 1.0 collective-permute-start.37
  63.1 1.2 %collective-permute-start.35 = (bf16[24,2048]{1,0:T(8,128)(2,1)S(1)}, bf16[24,2048]{1,0:T(8,128)(2,1)S(1)}, u32[]{:S(2)}, u32[]{:S(2)}) collective-permute-start(bf16[24,2048]{1,0:T(8,128)(2,1)S(1)} %copy-done.5), channel_id=1, source_target_pairs={{0,2},{1,3},{2,0},{3,1},{4,6},{5,7},{6,4},{7,5},{8,10},{9,11},{10,... | collective-permute-start | bytes 294920 | tf_op jit(solution)/shard_map/ppermute | solution.py:276
  64.3 1.2 %shard_map.128 = (bf16[24,2048]{1,0:T(8,128)(2,1)S(1)}, bf16[24,2048]{1,0:T(8,128)(2,1)S(1)}, bf16[24,2048]{1,0:T(8,128)(2,1)S(1)}, bf16[24,2048]{1,0:T(8,128)(2,1)S(1)}) custom-call(s32[8,128]{1,0:T(8,128)S(1)} %bitcast.34, f32[16,128]{1,0:T(8,128)S(1)} %collective-permute-done.24.keys_ref, bf16[128,4096]{1,0:T(8,128)(2,1)S(1)} %copy-done.4, ...), custom_call_target="tpu_custom_call" | custom-call | bytes 6480000 | tf_op jit(solution)/shard_map/pallas_call | solution.py:19
  65.5 1.7 %collective-permute-start.26 = (bf16[24,2048]{1,0:T(8,128)(2,1)S(1)}, bf16[24,2048]{1,0:T(8,128)(2,1)S(1)}, u32[]{:S(2)}, u32[]{:S(2)}) collective-permute-start(bf16[24,2048]{1,0:T(8,128)(2,1)S(1)} %get-tuple-element.103), channel_id=1, source_target_pairs={{0,28},{1,29},{2,30},{3,31},{4,24},{5,25},{6,26},{7,27},{8,20},{9,... | collective-permute-start | bytes 294920 | tf_op jit(solution)/shard_map/ppermute | solution.py:412
  67.9 1.4 %collective-permute-start.27 = (bf16[24,2048]{1,0:T(8,128)(2,1)S(1)}, bf16[24,2048]{1,0:T(8,128)(2,1)S(1)}, u32[]{:S(2)}, u32[]{:S(2)}) collective-permute-start(bf16[24,2048]{1,0:T(8,128)(2,1)S(1)} %get-tuple-element.104), channel_id=1, source_target_pairs={{0,20},{1,21},{2,22},{3,23},{4,16},{5,17},{6,18},{7,19},{8,28},{9,... | collective-permute-start | bytes 294920 | tf_op jit(solution)/shard_map/ppermute | solution.py:412
  69.9 2.4 %collective-permute-start.25 = (bf16[24,2048]{1,0:T(8,128)(2,1)S(1)}, bf16[24,2048]{1,0:T(8,128)(2,1)S(1)}, u32[]{:S(2)}, u32[]{:S(2)}) collective-permute-start(bf16[24,2048]{1,0:T(8,128)(2,1)S(1)} %get-tuple-element.102.refs_4_), channel_id=1, source_target_pairs={{0,24},{1,25},{2,26},{3,27},{4,28},{5,29},{6,30},{7,31},{8,16},{9,... | collective-permute-start | bytes 294920 | tf_op jit(solution)/shard_map/ppermute | solution.py:412
  72.3 0.9 collective-permute-start.34
  73.2 1.2 %collective-permute-start.32 = (bf16[24,2048]{1,0:T(8,128)(2,1)S(1)}, bf16[24,2048]{1,0:T(8,128)(2,1)S(1)}, u32[]{:S(2)}, u32[]{:S(2)}) collective-permute-start(bf16[24,2048]{1,0:T(8,128)(2,1)S(1)} %collective-permute-done.26.refs_1_), channel_id=1, source_target_pairs={{0,2},{1,3},{2,0},{3,1},{4,6},{5,7},{6,4},{7,5},{8,10},{9,11},{10,... | collective-permute-start | bytes 294920 | tf_op jit(solution)/shard_map/ppermute | solution.py:276
  74.3 0.9 collective-permute-start.29
  75.2 1.2 %collective-permute-start.30 = (bf16[24,2048]{1,0:T(8,128)(2,1)S(1)}, bf16[24,2048]{1,0:T(8,128)(2,1)S(1)}, u32[]{:S(2)}, u32[]{:S(2)}) collective-permute-start(bf16[24,2048]{1,0:T(8,128)(2,1)S(1)} %collective-permute-done.28.refs_3_), channel_id=1, source_target_pairs={{0,2},{1,3},{2,0},{3,1},{4,6},{5,7},{6,4},{7,5},{8,10},{9,11},{10,... | collective-permute-start | bytes 294920 | tf_op jit(solution)/shard_map/ppermute | solution.py:276
  76.4 1.0 collective-permute-done.25.refs_0_
  77.4 2.7 %shard_map.130.refs_8_ = f32[4,192,256]{2,1,0:T(8,128)S(1)} custom-call(bf16[24,2048]{1,0:T(8,128)(2,1)S(1)} %collective-permute-done.17.refs_0_, bf16[24,2048]{1,0:T(8,128)(2,1)S(1)} %collective-permute-done.18.refs_1_, bf16[24,2048]{1,0:T(8,128)(2,1)S(1)} %collective-permute-done.33.refs_2_, bf16[24,2048]{1,0:T(8,128)(2,1)S(1)} %copy-done.5, ...), custom_call_target="tpu_custom_call" | custom-call | bytes 9720000 | tf_op jit(solution)/shard_map/pallas_call | solution.py:19
  80.1 1.9 %collective-permute-done.31.refs_6_ = bf16[24,2048]{1,0:T(8,128)(2,1)S(1)} collective-permute-done((bf16[24,2048]{1,0:T(8,128)(2,1)S(1)}, bf16[24,2048]{1,0:T(8,128)(2,1)S(1)}, u32[]{:S(2)}, u32[]{:S(2)}) %collective-permute-start.31) | collective-permute-done | bytes 98336 | tf_op jit(solution)/shard_map/ppermute | solution.py:276
  82.0 5.6 %shard_map.131 = (f32[48,2048]{1,0:T(8,128)S(1)}, f32[48,2048]{1,0:T(8,128)S(1)}, bf16[48,2048]{1,0:T(8,128)(2,1)S(1)}, bf16[48,2048]{1,0:T(8,128)(2,1)S(1)}) custom-call(bf16[24,2048]{1,0:T(8,128)(2,1)S(1)} %collective-permute-done.25.refs_0_, bf16[24,2048]{1,0:T(8,128)(2,1)S(1)} %collective-permute-done.26.refs_1_, ...), custom_call_target="tpu_custom_call" | custom-call | bytes 20520000 | tf_op jit(solution)/shard_map/pallas_call | solution.py:19
  87.9 1.9 %collective-permute-start.41 = (bf16[48,2048]{1,0:T(8,128)(2,1)S(1)}, bf16[48,2048]{1,0:T(8,128)(2,1)S(1)}, u32[]{:S(2)}, u32[]{:S(2)}) collective-permute-start(bf16[48,2048]{1,0:T(8,128)(2,1)S(1)} %get-tuple-element.119), channel_id=1, source_target_pairs={{0,2},{1,3},{2,0},{3,1},{4,6},{5,7},{6,4},{7,5},{8,10},{9,11},{10,... | collective-permute-start | bytes 589832 | tf_op jit(solution)/shard_map/ppermute | solution.py:276
  89.8 3.6 %collective-permute-done.38.far_ref = bf16[48,2048]{1,0:T(8,128)(2,1)S(1)} collective-permute-done((bf16[48,2048]{1,0:T(8,128)(2,1)S(1)}, bf16[48,2048]{1,0:T(8,128)(2,1)S(1)}, u32[]{:S(2)}, u32[]{:S(2)}) %collective-permute-start.38) | collective-permute-done | bytes 196640 | tf_op jit(solution)/shard_map/ppermute | solution.py:276
  93.5 1.8 %collective-permute-start.39 = (bf16[24,2048]{1,0:T(8,128)(2,1)S(1)}, bf16[24,2048]{1,0:T(8,128)(2,1)S(1)}, u32[]{:S(2)}, u32[]{:S(2)}) collective-permute-start(bf16[24,2048]{1,0:T(8,128)(2,1)S(1)} %get-tuple-element.116), channel_id=1, source_target_pairs={{0,8},{1,9},{2,10},{3,11},{4,12},{5,13},{6,14},{7,15},{8,0},{9,1},... | collective-permute-start | bytes 294920 | tf_op jit(solution)/shard_map/ppermute | solution.py:276
  95.2 1.5 %collective-permute-start.40 = (bf16[24,2048]{1,0:T(8,128)(2,1)S(1)}, bf16[24,2048]{1,0:T(8,128)(2,1)S(1)}, u32[]{:S(2)}, u32[]{:S(2)}) collective-permute-start(bf16[24,2048]{1,0:T(8,128)(2,1)S(1)} %get-tuple-element.117), channel_id=1, source_target_pairs={{0,12},{1,13},{2,14},{3,15},{4,8},{5,9},{6,10},{7,11},{8,4},{9,5},... | collective-permute-start | bytes 294920 | tf_op jit(solution)/shard_map/ppermute | solution.py:276
  97.1 1.6 %shard_map.129 = bf16[1,128,4096]{2,1,0:T(8,128)(2,1)} custom-call(s32[8,128]{1,0:T(8,128)S(1)} %bitcast.35, bf16[24,2048]{1,0:T(8,128)(2,1)S(1)} %collective-permute-done.20.refs_0_, bf16[24,2048]{1,0:T(8,128)(2,1)S(1)} %collective-permute-done.21.refs_1_, bf16[24,2048]{1,0:T(8,128)(2,1)S(1)} %collective-permute-done.23.refs_2_, ...), custom_call_target="tpu_custom_call" | custom-call | bytes 5760000 | tf_op jit(solution)/shard_map/pallas_call | solution.py:19
  98.7 1.4 %collective-permute-done.39.refs_0_ = bf16[24,2048]{1,0:T(8,128)(2,1)S(1)} collective-permute-done((bf16[24,2048]{1,0:T(8,128)(2,1)S(1)}, bf16[24,2048]{1,0:T(8,128)(2,1)S(1)}, u32[]{:S(2)}, u32[]{:S(2)}) %collective-permute-start.39) | collective-permute-done | bytes 98336 | tf_op jit(solution)/shard_map/ppermute | solution.py:276
  100.1 1.7 %collective-permute-done.40.refs_1_ = bf16[24,2048]{1,0:T(8,128)(2,1)S(1)} collective-permute-done((bf16[24,2048]{1,0:T(8,128)(2,1)S(1)}, bf16[24,2048]{1,0:T(8,128)(2,1)S(1)}, u32[]{:S(2)}, u32[]{:S(2)}) %collective-permute-start.40) | collective-permute-done | bytes 98336 | tf_op jit(solution)/shard_map/ppermute | solution.py:276
  102.5 1.6 %shard_map.134 = bf16[1,128,4096]{2,1,0:T(8,128)(2,1)} custom-call(s32[8,128]{1,0:T(8,128)S(1)} %bitcast.37, bf16[24,2048]{1,0:T(8,128)(2,1)S(1)} %collective-permute-done.39.refs_0_, bf16[24,2048]{1,0:T(8,128)(2,1)S(1)} %collective-permute-done.40.refs_1_, bf16[24,2048]{1,0:T(8,128)(2,1)S(1)} %collective-permute-done.42.refs_2_, ...), custom_call_target="tpu_custom_call" | custom-call | bytes 5760000 | tf_op jit(solution)/shard_map/pallas_call | solution.py:19
  (81 shorter events, 8.7 us)
Async XLA Ops:
  0.6 34.0 %copy-start = (bf16[1,1,4096,256]{3,2,1,0:T(8,128)(2,1)S(1)}, bf16[1,1,4096,256]{3,2,1,0:T(8,128)(2,1)}, u32[]{:S(2)}) copy-start(bf16[1,1,4096,256]{3,2,1,0:T(8,128)(2,1)} %param.19) | copy-start | bytes 6291460
  0.6 11.8 %collective-permute-start = (bf16[4096,256]{1,0:T(8,128)(2,1)}, bf16[4096,256]{1,0:T(8,128)(2,1)S(1)}, u32[]{:S(2)}, u32[]{:S(2)}) collective-permute-start(bf16[4096,256]{1,0:T(8,128)(2,1)} %bitcast.18), channel_id=1, source_target_pairs={{0,1},{1,0},{2,3},{3,2},{4,5},{5,4},{6,7},{7,6},{8,9},{9,8},{10,11... | collective-permute-start | bytes 6291464 | tf_op jit(solution)/shard_map/ppermute | solution.py:276
  1.2 11.3 %collective-permute-start.1 = (bf16[4096,256]{1,0:T(8,128)(2,1)}, bf16[4096,256]{1,0:T(8,128)(2,1)S(1)}, u32[]{:S(2)}, u32[]{:S(2)}) collective-permute-start(bf16[4096,256]{1,0:T(8,128)(2,1)} %bitcast.23), channel_id=1, source_target_pairs={{0,1},{1,0},{2,3},{3,2},{4,5},{5,4},{6,7},{7,6},{8,9},{9,8},{10,11... | collective-permute-start | bytes 6291464 | tf_op jit(solution)/shard_map/ppermute | solution.py:276
  1.2 11.2 %collective-permute-start.2 = (bf16[256,4096]{1,0:T(8,128)(2,1)}, bf16[256,4096]{1,0:T(8,128)(2,1)}, u32[]{:S(2)}, u32[]{:S(2)}) collective-permute-start(bf16[256,4096]{1,0:T(8,128)(2,1)} %bitcast.28), channel_id=1, source_target_pairs={{0,1},{1,0},{2,3},{3,2},{4,5},{5,4},{6,7},{7,6},{8,9},{9,8},{10,11... | collective-permute-start | bytes 6291464 | tf_op jit(solution)/shard_map/ppermute | solution.py:276
  4.2 8.5 %collective-permute-start.6 = (bf16[24,2048]{1,0:T(8,128)(2,1)S(1)}, bf16[24,2048]{1,0:T(8,128)(2,1)S(1)}, u32[]{:S(2)}, u32[]{:S(2)}) collective-permute-start(bf16[24,2048]{1,0:T(8,128)(2,1)S(1)} %get-tuple-element.72), channel_id=1, source_target_pairs={{0,12},{1,13},{2,14},{3,15},{4,8},{5,9},{6,10},{7,11},{8,4},{9,5},... | collective-permute-start | bytes 294920 | tf_op jit(solution)/shard_map/ppermute | solution.py:276
  9.0 8.9 %collective-permute-start.5 = (bf16[24,2048]{1,0:T(8,128)(2,1)S(1)}, bf16[24,2048]{1,0:T(8,128)(2,1)S(1)}, u32[]{:S(2)}, u32[]{:S(2)}) collective-permute-start(bf16[24,2048]{1,0:T(8,128)(2,1)S(1)} %get-tuple-element.62.refs_0_), channel_id=1, source_target_pairs={{0,8},{1,9},{2,10},{3,11},{4,12},{5,13},{6,14},{7,15},{8,0},{9,1},... | collective-permute-start | bytes 294920 | tf_op jit(solution)/shard_map/ppermute | solution.py:276
  17.8 5.6 %collective-permute-start.7 = (bf16[24,2048]{1,0:T(8,128)(2,1)}, bf16[24,2048]{1,0:T(8,128)(2,1)S(1)}, u32[]{:S(2)}, u32[]{:S(2)}) collective-permute-start(bf16[24,2048]{1,0:T(8,128)(2,1)} %get-tuple-element.76), channel_id=1, source_target_pairs={{0,4},{1,5},{2,6},{3,7},{4,0},{5,1},{6,2},{7,3},{8,12},{9,13},{10,... | collective-permute-start | bytes 294920 | tf_op jit(solution)/shard_map/ppermute | solution.py:276
  17.8 6.7 %collective-permute-start.12 = (bf16[24,2048]{1,0:T(8,128)(2,1)S(1)}, bf16[24,2048]{1,0:T(8,128)(2,1)S(1)}, u32[]{:S(2)}, u32[]{:S(2)}) collective-permute-start(bf16[24,2048]{1,0:T(8,128)(2,1)S(1)} %get-tuple-element.80), channel_id=1, source_target_pairs={{0,4},{1,5},{2,6},{3,7},{4,0},{5,1},{6,2},{7,3},{8,12},{9,13},{10,... | collective-permute-start | bytes 294920 | tf_op jit(solution)/shard_map/ppermute | solution.py:276
  19.9 7.1 %collective-permute-start.15 = (bf16[24,2048]{1,0:T(8,128)(2,1)S(1)}, bf16[24,2048]{1,0:T(8,128)(2,1)S(1)}, u32[]{:S(2)}, u32[]{:S(2)}) collective-permute-start(bf16[24,2048]{1,0:T(8,128)(2,1)S(1)} %collective-permute-done.5.refs_0_), channel_id=1, source_target_pairs={{0,2},{1,3},{2,0},{3,1},{4,6},{5,7},{6,4},{7,5},{8,10},{9,11},{10,... | collective-permute-start | bytes 294920 | tf_op jit(solution)/shard_map/ppermute | solution.py:276
  21.4 7.1 %collective-permute-start.16 = (bf16[24,2048]{1,0:T(8,128)(2,1)S(1)}, bf16[24,2048]{1,0:T(8,128)(2,1)S(1)}, u32[]{:S(2)}, u32[]{:S(2)}) collective-permute-start(bf16[24,2048]{1,0:T(8,128)(2,1)S(1)} %collective-permute-done.6.refs_1_), channel_id=1, source_target_pairs={{0,2},{1,3},{2,0},{3,1},{4,6},{5,7},{6,4},{7,5},{8,10},{9,11},{10,... | collective-permute-start | bytes 294920 | tf_op jit(solution)/shard_map/ppermute | solution.py:276
  21.9 7.1 %collective-permute-start.14 = (bf16[24,2048]{1,0:T(8,128)(2,1)S(1)}, bf16[24,2048]{1,0:T(8,128)(2,1)S(1)}, u32[]{:S(2)}, u32[]{:S(2)}) collective-permute-start(bf16[24,2048]{1,0:T(8,128)(2,1)S(1)} %get-tuple-element.81.refs_3_), channel_id=1, source_target_pairs={{0,2},{1,3},{2,0},{3,1},{4,6},{5,7},{6,4},{7,5},{8,10},{9,11},{10,... | collective-permute-start | bytes 294920 | tf_op jit(solution)/shard_map/ppermute | solution.py:276
  23.5 9.1 %collective-permute-start.3 = (bf16[24,2048]{1,0:T(8,128)(2,1)}, bf16[24,2048]{1,0:T(8,128)(2,1)S(1)}, u32[]{:S(2)}, u32[]{:S(2)}) collective-permute-start(bf16[24,2048]{1,0:T(8,128)(2,1)} %get-tuple-element.67), channel_id=1, source_target_pairs={{0,8},{1,9},{2,10},{3,11},{4,12},{5,13},{6,14},{7,15},{8,0},{9,1},... | collective-permute-start | bytes 294920 | tf_op jit(solution)/shard_map/ppermute | solution.py:276
  24.5 9.2 %collective-permute-start.4 = (bf16[24,2048]{1,0:T(8,128)(2,1)}, bf16[24,2048]{1,0:T(8,128)(2,1)S(1)}, u32[]{:S(2)}, u32[]{:S(2)}) collective-permute-start(bf16[24,2048]{1,0:T(8,128)(2,1)} %get-tuple-element.68), channel_id=1, source_target_pairs={{0,12},{1,13},{2,14},{3,15},{4,8},{5,9},{6,10},{7,11},{8,4},{9,5},... | collective-permute-start | bytes 294920 | tf_op jit(solution)/shard_map/ppermute | solution.py:276
  27.0 7.7 %collective-permute-start.13 = (bf16[24,2048]{1,0:T(8,128)(2,1)S(1)}, bf16[24,2048]{1,0:T(8,128)(2,1)S(1)}, u32[]{:S(2)}, u32[]{:S(2)}) collective-permute-start(bf16[24,2048]{1,0:T(8,128)(2,1)S(1)} %collective-permute-done.12.refs_2_), channel_id=1, source_target_pairs={{0,2},{1,3},{2,0},{3,1},{4,6},{5,7},{6,4},{7,5},{8,10},{9,11},{10,... | collective-permute-start | bytes 294920 | tf_op jit(solution)/shard_map/ppermute | solution.py:276
  28.5 12.3 %collective-permute-start.9 = (bf16[24,2048]{1,0:T(8,128)(2,1)}, bf16[24,2048]{1,0:T(8,128)(2,1)S(1)}, u32[]{:S(2)}, u32[]{:S(2)}) collective-permute-start(bf16[24,2048]{1,0:T(8,128)(2,1)} %get-tuple-element.77.refs_3_), channel_id=1, source_target_pairs={{0,2},{1,3},{2,0},{3,1},{4,6},{5,7},{6,4},{7,5},{8,10},{9,11},{10,... | collective-permute-start | bytes 294920 | tf_op jit(solution)/shard_map/ppermute | solution.py:276
  29.0 13.2 %collective-permute-start.8 = (bf16[24,2048]{1,0:T(8,128)(2,1)S(1)}, bf16[24,2048]{1,0:T(8,128)(2,1)S(1)}, u32[]{:S(2)}, u32[]{:S(2)}) collective-permute-start(bf16[24,2048]{1,0:T(8,128)(2,1)S(1)} %collective-permute-done.7.refs_2_), channel_id=1, source_target_pairs={{0,2},{1,3},{2,0},{3,1},{4,6},{5,7},{6,4},{7,5},{8,10},{9,11},{10,... | collective-permute-start | bytes 294920 | tf_op jit(solution)/shard_map/ppermute | solution.py:276
  32.6 9.6 %collective-permute-start.10 = (bf16[24,2048]{1,0:T(8,128)(2,1)S(1)}, bf16[24,2048]{1,0:T(8,128)(2,1)S(1)}, u32[]{:S(2)}, u32[]{:S(2)}) collective-permute-start(bf16[24,2048]{1,0:T(8,128)(2,1)S(1)} %collective-permute-done.3.refs_0_), channel_id=1, source_target_pairs={{0,2},{1,3},{2,0},{3,1},{4,6},{5,7},{6,4},{7,5},{8,10},{9,11},{10,... | collective-permute-start | bytes 294920 | tf_op jit(solution)/shard_map/ppermute | solution.py:276
  33.8 8.4 %collective-permute-start.11 = (bf16[24,2048]{1,0:T(8,128)(2,1)S(1)}, bf16[24,2048]{1,0:T(8,128)(2,1)S(1)}, u32[]{:S(2)}, u32[]{:S(2)}) collective-permute-start(bf16[24,2048]{1,0:T(8,128)(2,1)S(1)} %collective-permute-done.4.refs_1_), channel_id=1, source_target_pairs={{0,2},{1,3},{2,0},{3,1},{4,6},{5,7},{6,4},{7,5},{8,10},{9,11},{10,... | collective-permute-start | bytes 294920 | tf_op jit(solution)/shard_map/ppermute | solution.py:276
  38.9 20.4 %copy-start.11 = (bf16[24,2048]{1,0:T(8,128)(2,1)S(1)}, bf16[24,2048]{1,0:T(8,128)(2,1)}, u32[]{:S(2)}) copy-start(bf16[24,2048]{1,0:T(8,128)(2,1)} %get-tuple-element.112) | copy-start | bytes 294916
  38.9 24.2 %copy-start.5 = (bf16[24,2048]{1,0:T(8,128)(2,1)S(1)}, bf16[24,2048]{1,0:T(8,128)(2,1)}, u32[]{:S(2)}) copy-start(bf16[24,2048]{1,0:T(8,128)(2,1)} %get-tuple-element.113.refs_3_) | copy-start | bytes 294916
  38.9 25.3 %copy-start.4 = (bf16[128,4096]{1,0:T(8,128)(2,1)S(1)}, bf16[128,4096]{1,0:T(8,128)(2,1)}, u32[]{:S(2)}) copy-start(bf16[128,4096]{1,0:T(8,128)(2,1)} %grad_last_ref.1) | copy-start | bytes 3145732
  39.0 25.3 %copy-start.9 = (s32[1,128,8]{1,2,0:T(8,128)S(1)}, s32[1,128,8]{1,2,0:T(8,128)}, u32[]{:S(2)}) copy-start(s32[1,128,8]{1,2,0:T(8,128)} %param.15) | copy-start | bytes 12292
  39.0 8.8 %collective-permute-start.17 = (bf16[24,2048]{1,0:T(8,128)(2,1)S(1)}, bf16[24,2048]{1,0:T(8,128)(2,1)S(1)}, u32[]{:S(2)}, u32[]{:S(2)}) collective-permute-start(bf16[24,2048]{1,0:T(8,128)(2,1)S(1)} %copy-done.13), channel_id=1, source_target_pairs={{0,8},{1,9},{2,10},{3,11},{4,12},{5,13},{6,14},{7,15},{8,0},{9,1},... | collective-permute-start | bytes 294920 | tf_op jit(solution)/shard_map/ppermute | solution.py:276
  40.8 7.0 %collective-permute-start.18 = (bf16[24,2048]{1,0:T(8,128)(2,1)S(1)}, bf16[24,2048]{1,0:T(8,128)(2,1)S(1)}, u32[]{:S(2)}, u32[]{:S(2)}) collective-permute-start(bf16[24,2048]{1,0:T(8,128)(2,1)S(1)} %copy-done.12), channel_id=1, source_target_pairs={{0,12},{1,13},{2,14},{3,15},{4,8},{5,9},{6,10},{7,11},{8,4},{9,5},... | collective-permute-start | bytes 294920 | tf_op jit(solution)/shard_map/ppermute | solution.py:276
  47.8 6.3 %collective-permute-start.19 = (bf16[48,2048]{1,0:T(8,128)(2,1)S(1)}, bf16[48,2048]{1,0:T(8,128)(2,1)S(1)}, u32[]{:S(2)}, u32[]{:S(2)}) collective-permute-start(bf16[48,2048]{1,0:T(8,128)(2,1)S(1)} %get-tuple-element.94), channel_id=1, source_target_pairs={{0,2},{1,3},{2,0},{3,1},{4,6},{5,7},{6,4},{7,5},{8,10},{9,11},{10,... | collective-permute-start | bytes 589832 | tf_op jit(solution)/shard_map/ppermute | solution.py:276
  48.7 9.6 %collective-permute-start.22 = (bf16[48,2048]{1,0:T(8,128)(2,1)S(1)}, bf16[48,2048]{1,0:T(8,128)(2,1)S(1)}, u32[]{:S(2)}, u32[]{:S(2)}) collective-permute-start(bf16[48,2048]{1,0:T(8,128)(2,1)S(1)} %get-tuple-element.98), channel_id=1, source_target_pairs={{0,2},{1,3},{2,0},{3,1},{4,6},{5,7},{6,4},{7,5},{8,10},{9,11},{10,... | collective-permute-start | bytes 589832 | tf_op jit(solution)/shard_map/ppermute | solution.py:276
  54.2 7.3 %collective-permute-start.20 = (bf16[24,2048]{1,0:T(8,128)(2,1)S(1)}, bf16[24,2048]{1,0:T(8,128)(2,1)S(1)}, u32[]{:S(2)}, u32[]{:S(2)}) collective-permute-start(bf16[24,2048]{1,0:T(8,128)(2,1)S(1)} %get-tuple-element.95), channel_id=1, source_target_pairs={{0,8},{1,9},{2,10},{3,11},{4,12},{5,13},{6,14},{7,15},{8,0},{9,1},... | collective-permute-start | bytes 294920 | tf_op jit(solution)/shard_map/ppermute | solution.py:276
  55.0 5.5 %collective-permute-start.24 = (f32[16,128]{1,0:T(8,128)S(1)}, f32[16,128]{1,0:T(8,128)S(1)}, u32[]{:S(2)}, u32[]{:S(2)}) collective-permute-start(f32[16,128]{1,0:T(8,128)S(1)} %copy-done.14), channel_id=1, source_target_pairs={{0,16},{16,0},{1,17},{17,1},{2,18},{18,2},{3,19},{19,3},{4,20},{20... | collective-permute-start | bytes 24584 | tf_op jit(solution)/shard_map/ppermute | solution.py:385
  56.5 6.6 %collective-permute-start.21 = (bf16[24,2048]{1,0:T(8,128)(2,1)S(1)}, bf16[24,2048]{1,0:T(8,128)(2,1)S(1)}, u32[]{:S(2)}, u32[]{:S(2)}) collective-permute-start(bf16[24,2048]{1,0:T(8,128)(2,1)S(1)} %get-tuple-element.96), channel_id=1, source_target_pairs={{0,12},{1,13},{2,14},{3,15},{4,8},{5,9},{6,10},{7,11},{8,4},{9,5},... | collective-permute-start | bytes 294920 | tf_op jit(solution)/shard_map/ppermute | solution.py:276
  58.4 5.9 %collective-permute-start.23 = (bf16[24,2048]{1,0:T(8,128)(2,1)S(1)}, bf16[24,2048]{1,0:T(8,128)(2,1)S(1)}, u32[]{:S(2)}, u32[]{:S(2)}) collective-permute-start(bf16[24,2048]{1,0:T(8,128)(2,1)S(1)} %get-tuple-element.99), channel_id=1, source_target_pairs={{0,4},{1,5},{2,6},{3,7},{4,0},{5,1},{6,2},{7,3},{8,12},{9,13},{10,... | collective-permute-start | bytes 294920 | tf_op jit(solution)/shard_map/ppermute | solution.py:276
  59.3 8.5 %collective-permute-start.33 = (bf16[24,2048]{1,0:T(8,128)(2,1)S(1)}, bf16[24,2048]{1,0:T(8,128)(2,1)S(1)}, u32[]{:S(2)}, u32[]{:S(2)}) collective-permute-start(bf16[24,2048]{1,0:T(8,128)(2,1)S(1)} %copy-done.11), channel_id=1, source_target_pairs={{0,4},{1,5},{2,6},{3,7},{4,0},{5,1},{6,2},{7,3},{8,12},{9,13},{10,... | collective-permute-start | bytes 294920 | tf_op jit(solution)/shard_map/ppermute | solution.py:276
  60.5 8.8 %collective-permute-start.36 = (bf16[24,2048]{1,0:T(8,128)(2,1)S(1)}, bf16[24,2048]{1,0:T(8,128)(2,1)S(1)}, u32[]{:S(2)}, u32[]{:S(2)}) collective-permute-start(bf16[24,2048]{1,0:T(8,128)(2,1)S(1)} %collective-permute-done.17.refs_0_), channel_id=1, source_target_pairs={{0,2},{1,3},{2,0},{3,1},{4,6},{5,7},{6,4},{7,5},{8,10},{9,11},{10,... | collective-permute-start | bytes 294920 | tf_op jit(solution)/shard_map/ppermute | solution.py:276
  61.5 8.4 %collective-permute-start.37 = (bf16[24,2048]{1,0:T(8,128)(2,1)S(1)}, bf16[24,2048]{1,0:T(8,128)(2,1)S(1)}, u32[]{:S(2)}, u32[]{:S(2)}) collective-permute-start(bf16[24,2048]{1,0:T(8,128)(2,1)S(1)} %collective-permute-done.18.refs_1_), channel_id=1, source_target_pairs={{0,2},{1,3},{2,0},{3,1},{4,6},{5,7},{6,4},{7,5},{8,10},{9,11},{10,... | collective-permute-start | bytes 294920 | tf_op jit(solution)/shard_map/ppermute | solution.py:276
  63.1 9.2 %collective-permute-start.35 = (bf16[24,2048]{1,0:T(8,128)(2,1)S(1)}, bf16[24,2048]{1,0:T(8,128)(2,1)S(1)}, u32[]{:S(2)}, u32[]{:S(2)}) collective-permute-start(bf16[24,2048]{1,0:T(8,128)(2,1)S(1)} %copy-done.5), channel_id=1, source_target_pairs={{0,2},{1,3},{2,0},{3,1},{4,6},{5,7},{6,4},{7,5},{8,10},{9,11},{10,... | collective-permute-start | bytes 294920 | tf_op jit(solution)/shard_map/ppermute | solution.py:276
  65.5 7.7 %collective-permute-start.26 = (bf16[24,2048]{1,0:T(8,128)(2,1)S(1)}, bf16[24,2048]{1,0:T(8,128)(2,1)S(1)}, u32[]{:S(2)}, u32[]{:S(2)}) collective-permute-start(bf16[24,2048]{1,0:T(8,128)(2,1)S(1)} %get-tuple-element.103), channel_id=1, source_target_pairs={{0,28},{1,29},{2,30},{3,31},{4,24},{5,25},{6,26},{7,27},{8,20},{9,... | collective-permute-start | bytes 294920 | tf_op jit(solution)/shard_map/ppermute | solution.py:412
  67.9 6.5 %collective-permute-start.27 = (bf16[24,2048]{1,0:T(8,128)(2,1)S(1)}, bf16[24,2048]{1,0:T(8,128)(2,1)S(1)}, u32[]{:S(2)}, u32[]{:S(2)}) collective-permute-start(bf16[24,2048]{1,0:T(8,128)(2,1)S(1)} %get-tuple-element.104), channel_id=1, source_target_pairs={{0,20},{1,21},{2,22},{3,23},{4,16},{5,17},{6,18},{7,19},{8,28},{9,... | collective-permute-start | bytes 294920 | tf_op jit(solution)/shard_map/ppermute | solution.py:412
  69.3 5.9 %collective-permute-start.28 = (bf16[24,2048]{1,0:T(8,128)(2,1)S(1)}, bf16[24,2048]{1,0:T(8,128)(2,1)S(1)}, u32[]{:S(2)}, u32[]{:S(2)}) collective-permute-start(bf16[24,2048]{1,0:T(8,128)(2,1)S(1)} %get-tuple-element.105), channel_id=1, source_target_pairs={{0,16},{1,17},{2,18},{3,19},{4,20},{5,21},{6,22},{7,23},{8,24},{9,... | collective-permute-start | bytes 294920 | tf_op jit(solution)/shard_map/ppermute | solution.py:412
  69.9 7.5 %collective-permute-start.25 = (bf16[24,2048]{1,0:T(8,128)(2,1)S(1)}, bf16[24,2048]{1,0:T(8,128)(2,1)S(1)}, u32[]{:S(2)}, u32[]{:S(2)}) collective-permute-start(bf16[24,2048]{1,0:T(8,128)(2,1)S(1)} %get-tuple-element.102.refs_4_), channel_id=1, source_target_pairs={{0,24},{1,25},{2,26},{3,27},{4,28},{5,29},{6,30},{7,31},{8,16},{9,... | collective-permute-start | bytes 294920 | tf_op jit(solution)/shard_map/ppermute | solution.py:412
  72.3 5.1 %collective-permute-start.34 = (bf16[24,2048]{1,0:T(8,128)(2,1)S(1)}, bf16[24,2048]{1,0:T(8,128)(2,1)S(1)}, u32[]{:S(2)}, u32[]{:S(2)}) collective-permute-start(bf16[24,2048]{1,0:T(8,128)(2,1)S(1)} %collective-permute-done.33.refs_2_), channel_id=1, source_target_pairs={{0,2},{1,3},{2,0},{3,1},{4,6},{5,7},{6,4},{7,5},{8,10},{9,11},{10,... | collective-permute-start | bytes 294920 | tf_op jit(solution)/shard_map/ppermute | solution.py:276
  73.2 6.9 %collective-permute-start.32 = (bf16[24,2048]{1,0:T(8,128)(2,1)S(1)}, bf16[24,2048]{1,0:T(8,128)(2,1)S(1)}, u32[]{:S(2)}, u32[]{:S(2)}) collective-permute-start(bf16[24,2048]{1,0:T(8,128)(2,1)S(1)} %collective-permute-done.26.refs_1_), channel_id=1, source_target_pairs={{0,2},{1,3},{2,0},{3,1},{4,6},{5,7},{6,4},{7,5},{8,10},{9,11},{10,... | collective-permute-start | bytes 294920 | tf_op jit(solution)/shard_map/ppermute | solution.py:276
  74.3 5.7 %collective-permute-start.29 = (bf16[24,2048]{1,0:T(8,128)(2,1)S(1)}, bf16[24,2048]{1,0:T(8,128)(2,1)S(1)}, u32[]{:S(2)}, u32[]{:S(2)}) collective-permute-start(bf16[24,2048]{1,0:T(8,128)(2,1)S(1)} %collective-permute-done.27.refs_2_), channel_id=1, source_target_pairs={{0,2},{1,3},{2,0},{3,1},{4,6},{5,7},{6,4},{7,5},{8,10},{9,11},{10,... | collective-permute-start | bytes 294920 | tf_op jit(solution)/shard_map/ppermute | solution.py:276
  75.2 4.9 %collective-permute-start.30 = (bf16[24,2048]{1,0:T(8,128)(2,1)S(1)}, bf16[24,2048]{1,0:T(8,128)(2,1)S(1)}, u32[]{:S(2)}, u32[]{:S(2)}) collective-permute-start(bf16[24,2048]{1,0:T(8,128)(2,1)S(1)} %collective-permute-done.28.refs_3_), channel_id=1, source_target_pairs={{0,2},{1,3},{2,0},{3,1},{4,6},{5,7},{6,4},{7,5},{8,10},{9,11},{10,... | collective-permute-start | bytes 294920 | tf_op jit(solution)/shard_map/ppermute | solution.py:276
  77.4 4.6 %collective-permute-start.31 = (bf16[24,2048]{1,0:T(8,128)(2,1)S(1)}, bf16[24,2048]{1,0:T(8,128)(2,1)S(1)}, u32[]{:S(2)}, u32[]{:S(2)}) collective-permute-start(bf16[24,2048]{1,0:T(8,128)(2,1)S(1)} %collective-permute-done.25.refs_0_), channel_id=1, source_target_pairs={{0,2},{1,3},{2,0},{3,1},{4,6},{5,7},{6,4},{7,5},{8,10},{9,11},{10,... | collective-permute-start | bytes 294920 | tf_op jit(solution)/shard_map/ppermute | solution.py:276
  87.7 5.7 %collective-permute-start.38 = (bf16[48,2048]{1,0:T(8,128)(2,1)S(1)}, bf16[48,2048]{1,0:T(8,128)(2,1)S(1)}, u32[]{:S(2)}, u32[]{:S(2)}) collective-permute-start(bf16[48,2048]{1,0:T(8,128)(2,1)S(1)} %get-tuple-element.115), channel_id=1, source_target_pairs={{0,2},{1,3},{2,0},{3,1},{4,6},{5,7},{6,4},{7,5},{8,10},{9,11},{10,... | collective-permute-start | bytes 589832 | tf_op jit(solution)/shard_map/ppermute | solution.py:276
  87.9 8.8 %collective-permute-start.41 = (bf16[48,2048]{1,0:T(8,128)(2,1)S(1)}, bf16[48,2048]{1,0:T(8,128)(2,1)S(1)}, u32[]{:S(2)}, u32[]{:S(2)}) collective-permute-start(bf16[48,2048]{1,0:T(8,128)(2,1)S(1)} %get-tuple-element.119), channel_id=1, source_target_pairs={{0,2},{1,3},{2,0},{3,1},{4,6},{5,7},{6,4},{7,5},{8,10},{9,11},{10,... | collective-permute-start | bytes 589832 | tf_op jit(solution)/shard_map/ppermute | solution.py:276
  93.5 6.6 %collective-permute-start.39 = (bf16[24,2048]{1,0:T(8,128)(2,1)S(1)}, bf16[24,2048]{1,0:T(8,128)(2,1)S(1)}, u32[]{:S(2)}, u32[]{:S(2)}) collective-permute-start(bf16[24,2048]{1,0:T(8,128)(2,1)S(1)} %get-tuple-element.116), channel_id=1, source_target_pairs={{0,8},{1,9},{2,10},{3,11},{4,12},{5,13},{6,14},{7,15},{8,0},{9,1},... | collective-permute-start | bytes 294920 | tf_op jit(solution)/shard_map/ppermute | solution.py:276
  95.2 6.6 %collective-permute-start.40 = (bf16[24,2048]{1,0:T(8,128)(2,1)S(1)}, bf16[24,2048]{1,0:T(8,128)(2,1)S(1)}, u32[]{:S(2)}, u32[]{:S(2)}) collective-permute-start(bf16[24,2048]{1,0:T(8,128)(2,1)S(1)} %get-tuple-element.117), channel_id=1, source_target_pairs={{0,12},{1,13},{2,14},{3,15},{4,8},{5,9},{6,10},{7,11},{8,4},{9,5},... | collective-permute-start | bytes 294920 | tf_op jit(solution)/shard_map/ppermute | solution.py:276
  96.7 5.7 %collective-permute-start.42 = (bf16[24,2048]{1,0:T(8,128)(2,1)S(1)}, bf16[24,2048]{1,0:T(8,128)(2,1)S(1)}, u32[]{:S(2)}, u32[]{:S(2)}) collective-permute-start(bf16[24,2048]{1,0:T(8,128)(2,1)S(1)} %get-tuple-element.120), channel_id=1, source_target_pairs={{0,4},{1,5},{2,6},{3,7},{4,0},{5,1},{6,2},{7,3},{8,12},{9,13},{10,... | collective-permute-start | bytes 294920 | tf_op jit(solution)/shard_map/ppermute | solution.py:276
  (10 other events, 58.3 us)
